TPU v7x, 128 devices: a whole 4x4x4 slice. The times are simulated.
128 devices in a mesh: gx: 4 (over z), yz: 32 (over y, x, core).
Axes of the slice: x: 4, y: 4, z: 4, core: 2. Of those that a mesh axis runs over, the one named last changes fastest.
Arguments:
- coarse_density: float32 [128, 1024, 128], P('gx', 'yz'), may hold values from 0.5 to 2
- coarse_velocity: float32 [3, 128, 1024, 128], P(None, 'gx', 'yz'), may hold values from -3 to 3
- coarse_pressure: float32 [128, 1024, 128], P('gx', 'yz'), may hold values from 0.5 to 2
- coarse_bins: int32 [128, 1024], P('gx', 'yz'), may hold values from 0 to 1998
- fine_density: float32 [4096, 8, 8, 256], P(('gx', 'yz')), may hold values from 0.5 to 2
- fine_velocity: float32 [3, 4096, 8, 8, 256], P(None, ('gx', 'yz')), may hold values from -3 to 3
- fine_pressure: float32 [4096, 8, 8, 256], P(('gx', 'yz')), may hold values from 0.5 to 2
- fine_bins: int32 [4096, 8, 8], P(('gx', 'yz')), may hold values from 0 to 1998
- patch_host: int32 [4096], replicated, may hold values from 0 to 31, as said below
- patch_spot: int32 [4096], replicated, may hold values from 0 to 35, as said below
- heat_rate: float32 [2000], replicated, may hold values from 1 to 16
- cool_rate: float32 [2000], replicated, may hold values from 1 to 16
Outputs:
- coarse_state: float32 [5, 128, 1024, 128], P(None, 'gx', 'yz')
- fine_state: float32 [5, 4096, 8, 8, 256], P(None, ('gx', 'yz'))
Inputs may be any that keep to these rules, and one draw needn't show every extreme that they name: Patch p is held by device p // 32 of the mesh (gx slowest) and lies in the block of the device of the same gx row whose yz index is patch_host[p]. Of one device's 32 patches at most 2 have the same host, and one block hosts at most 36 patches; both bounds are reached. `patch_spot`: patches of one gx row with the same host have different places.
All inputs are finite; a program needn't handle non-finite values.
Results may differ from a plain program's by a relative error of at most 0.00002.
Values sent between devices are 32-bit elements; how exact they have to be, the bound alone decides.
No kernel may reach another device: no remote copies, remote signals or barrier semaphores. Data moves between devices by JAX's collectives and lax.ppermute only.
A program may use at most 640 MiB of HBM per device.

v0:
```python
import jax
import jax.numpy as jnp
from jax import lax
from jax.sharding import PartitionSpec as P

GAMMA = 5.0 / 3.0
STEP = 0.02
FINE_STEP = 0.04


def with_halo(cells, sides, width):
    for axis, dim in sides:
        count = lax.axis_size(axis)
        head = lax.slice_in_dim(cells, 0, width, axis=dim)
        tail = lax.slice_in_dim(cells, cells.shape[dim] - width, cells.shape[dim], axis=dim)
        cells = jnp.concatenate(
            [
                lax.ppermute(tail, axis, [(i, (i + 1) % count) for i in range(count)]),
                cells,
                lax.ppermute(head, axis, [((i + 1) % count, i) for i in range(count)]),
            ],
            axis=dim,
        )
    return cells


def conserved(physical_variables_vector):
    matter_per_volume = physical_variables_vector[0]
    flow_speed = physical_variables_vector[1:4]
    pressure = physical_variables_vector[4]
    kinetic = (
        0.5
        * matter_per_volume
        * (
            flow_speed[0] * flow_speed[0]
            + flow_speed[1] * flow_speed[1]
            + flow_speed[2] * flow_speed[2]
        )
    )
    return jnp.concatenate(
        [
            matter_per_volume[None],
            matter_per_volume[None] * flow_speed,
            (pressure / (GAMMA - 1.0) + kinetic)[None],
        ],
        axis=0,
    )


def euler_flux(physical_variables_vector, amounts, direction):
    normal_speed = physical_variables_vector[1 + direction]
    pressure = physical_variables_vector[4]
    entries = [amounts[1 + direction]]
    for component in range(3):
        momentum = amounts[1 + component] * normal_speed
        if component == direction:
            momentum = momentum + pressure
        entries.append(momentum)
    entries.append((amounts[4] + pressure) * normal_speed)
    return jnp.stack(entries)


def rusanov(left, left_amounts, right, right_amounts, direction):
    left_speed = jnp.abs(left[1 + direction]) + jnp.sqrt(GAMMA * left[4] / left[0])
    right_speed = jnp.abs(right[1 + direction]) + jnp.sqrt(GAMMA * right[4] / right[0])
    fastest = jnp.maximum(left_speed, right_speed)
    average = 0.5 * (
        euler_flux(left, left_amounts, direction) + euler_flux(right, right_amounts, direction)
    )
    return average - 0.5 * fastest * (right_amounts - left_amounts)


def energy_source(physical_variables_vector, bins, heat_rate, cool_rate):
    matter_per_volume = physical_variables_vector[0]
    thermal_kelvin = physical_variables_vector[4] / matter_per_volume
    blending_share = thermal_kelvin / (1.0 + thermal_kelvin)
    heating = (1.0 - blending_share) * jnp.take(heat_rate, bins) + blending_share * jnp.take(
        heat_rate, bins + 1
    )
    cooling = (1.0 - blending_share) * jnp.take(cool_rate, bins) + blending_share * jnp.take(
        cool_rate, bins + 1
    )
    return matter_per_volume * heating - matter_per_volume * matter_per_volume * cooling


def spread_pairs(columns):
    return jnp.repeat(jnp.repeat(columns, 2, axis=2), 2, axis=3)


def fine_batch(primitive, rim, bins, heat_rate, cool_rate):
    width = primitive.shape[2]
    half = width // 2
    depth = primitive.shape[4] // 2
    batch = primitive.shape[1]
    ghost_low_x = spread_pairs(rim[:, :, 0:half])
    ghost_high_x = spread_pairs(rim[:, :, half : 2 * half])
    ghost_low_y = spread_pairs(rim[:, :, 2 * half : 3 * half])
    ghost_high_y = spread_pairs(rim[:, :, 3 * half : 4 * half])
    amounts = conserved(primitive)
    along_x = jnp.concatenate(
        [ghost_low_x[:, :, None], primitive, ghost_high_x[:, :, None]], axis=2
    )
    amounts_x = jnp.concatenate(
        [conserved(ghost_low_x)[:, :, None], amounts, conserved(ghost_high_x)[:, :, None]], axis=2
    )
    flux_x = rusanov(
        along_x[:, :, :-1], amounts_x[:, :, :-1], along_x[:, :, 1:], amounts_x[:, :, 1:], 0
    )
    along_y = jnp.concatenate(
        [ghost_low_y[:, :, :, None], primitive, ghost_high_y[:, :, :, None]], axis=3
    )
    amounts_y = jnp.concatenate(
        [conserved(ghost_low_y)[:, :, :, None], amounts, conserved(ghost_high_y)[:, :, :, None]],
        axis=3,
    )
    flux_y = rusanov(
        along_y[:, :, :, :-1],
        amounts_y[:, :, :, :-1],
        along_y[:, :, :, 1:],
        amounts_y[:, :, :, 1:],
        1,
    )
    flux_z = rusanov(primitive, amounts, jnp.roll(primitive, -1, 4), jnp.roll(amounts, -1, 4), 2)
    change = (
        flux_x[:, :, 1:]
        - flux_x[:, :, :-1]
        + (flux_y[:, :, :, 1:] - flux_y[:, :, :, :-1])
        + (flux_z - jnp.roll(flux_z, 1, 4))
    )
    updated = amounts - FINE_STEP * change
    updated = updated.at[4].add(
        STEP * energy_source(primitive, bins[:, :, :, None], heat_rate, cool_rate)
    )
    averaged = updated.reshape(5, batch, half, 2, half, 2, depth, 2).sum(axis=(3, 5, 7)) * 0.125
    averaged = averaged.reshape(5, batch, half * half, depth)

    def face_mean(face):
        return face.reshape(5, batch, half, 2, depth, 2).sum(axis=(3, 5)) * 0.25

    sums = jnp.concatenate(
        [
            averaged,
            face_mean(flux_x[:, :, 0]),
            face_mean(flux_x[:, :, width]),
            face_mean(flux_y[:, :, :, 0]),
            face_mean(flux_y[:, :, :, width]),
        ],
        axis=2,
    )
    return (updated, sums)


def cut_boxes(source, start_x, start_y, reverse_direction, foot):
    depth = source.shape[3]

    def one_box(lowest_abscissa, corner_y):
        return lax.dynamic_slice(
            source,
            (0, lowest_abscissa - reverse_direction, corner_y - reverse_direction, 0),
            (5, foot + 2, foot + 2, depth),
        )

    boxes = jax.vmap(one_box)(start_x.reshape(-1), start_y.reshape(-1))
    return boxes.reshape(start_x.shape + (5, foot + 2, foot + 2, depth))


def rim_columns(box):
    last = box.shape[-3] - 1
    return jnp.concatenate(
        [
            box[..., 0, 1:last, :],
            box[..., last, 1:last, :],
            box[..., 1:last, 0, :],
            box[..., 1:last, last, :],
        ],
        axis=-2,
    )


def coarse_update(padded, physical_variables_vector, coarse_bins, heat_rate, cool_rate):
    amounts_pad = conserved(padded)
    amounts = amounts_pad[:, 1:-1, 1:-1]
    flux_x = rusanov(
        padded[:, :-1, 1:-1],
        amounts_pad[:, :-1, 1:-1],
        padded[:, 1:, 1:-1],
        amounts_pad[:, 1:, 1:-1],
        0,
    )
    flux_y = rusanov(
        padded[:, 1:-1, :-1],
        amounts_pad[:, 1:-1, :-1],
        padded[:, 1:-1, 1:],
        amounts_pad[:, 1:-1, 1:],
        1,
    )
    flux_z = rusanov(
        physical_variables_vector,
        amounts,
        jnp.roll(physical_variables_vector, -1, 3),
        jnp.roll(amounts, -1, 3),
        2,
    )
    change = (
        flux_x[:, 1:]
        - flux_x[:, :-1]
        + (flux_y[:, :, 1:] - flux_y[:, :, :-1])
        + (flux_z - jnp.roll(flux_z, 1, 3))
    )
    updated = amounts - STEP * change
    updated = updated.at[4].add(
        STEP
        * energy_source(physical_variables_vector, coarse_bins[:, :, None], heat_rate, cool_rate)
    )
    return (updated, flux_x, flux_y)


def local(
    coarse_density,
    coarse_velocity,
    coarse_pressure,
    coarse_bins,
    fine_density,
    fine_velocity,
    fine_pressure,
    fine_bins,
    patch_host,
    patch_spot,
    heat_rate,
    cool_rate,
):
    groups = lax.axis_size("yz")
    row_index = lax.axis_index("gx")
    participant = lax.axis_index("yz")
    physical_variables_vector = jnp.concatenate(
        [coarse_density[None], coarse_velocity, coarse_pressure[None]], axis=0
    )
    width_x = physical_variables_vector.shape[1]
    width_y = physical_variables_vector.shape[2]
    depth = physical_variables_vector.shape[3]
    count = fine_density.shape[0]
    capacity = max(2, 2 * count // groups)
    spots_y = (width_y - 1) // 5
    foot = fine_density.shape[1] // 2
    row_hosts = lax.dynamic_slice_in_dim(
        patch_host, row_index * groups * count, groups * count
    ).reshape(groups, count)
    row_spots = lax.dynamic_slice_in_dim(
        patch_spot, row_index * groups * count, groups * count
    ).reshape(groups, count)
    positions = jnp.arange(count, dtype=jnp.int32)
    same_host = row_hosts[:, :, None] == row_hosts[:, None, :]
    earlier = positions[None, :] < positions[:, None]
    host_rank = jnp.sum((same_host & earlier[None]).astype(jnp.int32), axis=2)
    slot_index_list = jnp.arange(capacity, dtype=jnp.int32)
    chosen = (row_hosts[:, None, :] == participant) & (
        host_rank[:, None, :] == slot_index_list[None, :, None]
    )
    occupied = jnp.any(chosen, axis=2)
    slot_spot = jnp.sum(jnp.where(chosen, row_spots[:, None, :], 0), axis=2)
    start_x = 1 + 5 * (slot_spot // spots_y)
    start_y = 1 + 5 * (slot_spot % spots_y)
    padded = with_halo(physical_variables_vector, (("gx", 1), ("yz", 2)), 1)
    cut = cut_boxes(padded, start_x, start_y, 0, foot)
    own_host = row_hosts[participant]
    own_rank = host_rank[participant]
    arrived = lax.all_to_all(cut, "yz", split_axis=0, concat_axis=0, tiled=True)
    rims = rim_columns(arrived[own_host, own_rank])
    fine_primitive = jnp.concatenate(
        [fine_density[None], fine_velocity, fine_pressure[None]], axis=0
    )
    fine_new, sums = fine_batch(
        fine_primitive, jnp.moveaxis(rims, 1, 0), fine_bins, heat_rate, cool_rate
    )
    back_buffer = (
        jnp.zeros((groups, capacity, 5) + sums.shape[2:], jnp.float32)
        .at[own_host, own_rank]
        .set(jnp.moveaxis(sums, 0, 1))
    )
    returned = lax.all_to_all(back_buffer, "yz", split_axis=0, concat_axis=0, tiled=True)
    updated, flux_x, flux_y = coarse_update(
        padded, physical_variables_vector, coarse_bins, heat_rate, cool_rate
    )
    offsets = jnp.arange(foot, dtype=jnp.int32)
    low = jnp.zeros_like(offsets)
    lowest_abscissa = start_x[..., None]
    corner_y = start_y[..., None]
    coarse_xlo = flux_x[:, lowest_abscissa + low, corner_y + offsets]
    coarse_xhi = flux_x[:, lowest_abscissa + foot + low, corner_y + offsets]
    coarse_ylo = flux_y[:, lowest_abscissa + offsets, corner_y + low]
    coarse_yhi = flux_y[:, lowest_abscissa + offsets, corner_y + foot + low]
    got = jnp.moveaxis(returned, 2, 0)
    cells = foot * foot
    deltas = jnp.concatenate(
        [
            STEP * (coarse_xlo - got[:, :, :, cells : cells + foot]),
            STEP * (got[:, :, :, cells + foot : cells + 2 * foot] - coarse_xhi),
            STEP * (coarse_ylo - got[:, :, :, cells + 2 * foot : cells + 3 * foot]),
            STEP * (got[:, :, :, cells + 3 * foot : cells + 4 * foot] - coarse_yhi),
        ],
        axis=3,
    )
    plane = width_x * width_y
    outside = 5 * plane
    components = jnp.arange(5, dtype=jnp.int32).reshape(5, 1, 1, 1) * plane
    rim_x = jnp.concatenate(
        [
            lowest_abscissa - 1 + low,
            lowest_abscissa + foot + low,
            lowest_abscissa + offsets,
            lowest_abscissa + offsets,
        ],
        axis=-1,
    )
    rim_y = jnp.concatenate(
        [corner_y + offsets, corner_y + offsets, corner_y - 1 + low, corner_y + foot + low], axis=-1
    )
    rim_rows = jnp.where(
        occupied[None, :, :, None], components + (rim_x * width_y + rim_y)[None], outside
    )
    flat_rows = updated.reshape(5 * plane, depth)
    flat_rows = flat_rows.at[rim_rows.reshape(-1)].add(deltas.reshape(-1, depth), mode="drop")
    squares = jnp.arange(cells, dtype=jnp.int32)
    foot_x = lowest_abscissa + squares // foot
    foot_y = corner_y + squares % foot
    foot_rows = jnp.where(
        occupied[None, :, :, None], components + (foot_x * width_y + foot_y)[None], outside
    )
    flat_rows = flat_rows.at[foot_rows.reshape(-1)].set(
        got[:, :, :, 0:cells].reshape(-1, depth), mode="drop"
    )
    return (flat_rows.reshape(5, width_x, width_y, depth), fine_new)


def solution(mesh):
    placed = (
        P("gx", "yz", None),
        P(None, "gx", "yz", None),
        P("gx", "yz", None),
        P("gx", "yz"),
        P(("gx", "yz"), None, None, None),
        P(None, ("gx", "yz"), None, None, None),
        P(("gx", "yz"), None, None, None),
        P(("gx", "yz"), None, None),
        P(),
        P(),
        P(),
        P(),
    )
    return jax.shard_map(
        local,
        mesh=mesh,
        in_specs=placed,
        out_specs=(P(None, "gx", "yz", None), P(None, ("gx", "yz"), None, None, None)),
        check_vma=False,
    )
```

profile of v0, /device:TPU:0, one launch (start us, length us, event | category | flops | bytes accessed | tf_op | source)
XLA Modules:
  0.0 1010.3 jit_solution(8953989205389877050)
XLA Ops:
  9.6 10.5 %gather_fusion.6 = f32[1024]{0:T(1024)} fusion(f32[2000]{0:T(1024)S(1)} %copy-done, s32[1024]{0:T(1024)S(1)} %get-tuple-element.173), kind=kCustom, calls=%fused_computation.clone | custom fusion | bytes 12288 | tf_op jit(solution)/shard_map/jit(_take)/gather | solution.py:77
  20.2 10.5 %gather_fusion.7 = f32[1024]{0:T(1024)} fusion(f32[2000]{0:T(1024)S(1)} %copy-done, s32[1024]{0:T(1024)S(1)} %get-tuple-element.172), kind=kCustom, calls=%fused_computation.2.clone | custom fusion | bytes 12288 | tf_op jit(solution)/shard_map/jit(_take)/gather | solution.py:77
  30.7 10.5 %gather_fusion.9 = f32[1024]{0:T(1024)} fusion(f32[2000]{0:T(1024)S(1)} %copy-done.2, s32[1024]{0:T(1024)S(1)} %get-tuple-element.172), kind=kCustom, calls=%fused_computation.4.clone | custom fusion | bytes 12288 | tf_op jit(solution)/shard_map/jit(_take)/gather | solution.py:80
  41.2 10.5 %gather_fusion.8 = f32[1024]{0:T(1024)} fusion(f32[2000]{0:T(1024)S(1)} %copy-done.2, s32[1024]{0:T(1024)S(1)} %get-tuple-element.173), kind=kCustom, calls=%fused_computation.3.clone | custom fusion | bytes 12288 | tf_op jit(solution)/shard_map/jit(_take)/gather | solution.py:80
  63.6 6.2 fusion.83
  77.8 7.9 fusion.17
  85.7 5.8 slice.1141
  91.5 10.8 %slice.1140 = f32[5,32,8,8,255]{4,3,2,1,0:T(8,128)} slice(f32[5,32,8,8,256]{4,3,2,1,0:T(8,128)} %get-tuple-element.100), slice={[0:5], [0:32], [0:8], [0:8], [1:256]} | slice | bytes 20889600 | tf_op jit(solution)/shard_map/jit(_roll_static)/slice | solution.py:123
  105.3 6.7 slice.1146
  112.9 20.5 %gather_fusion.11 = f32[2048]{0:T(1024)} fusion(f32[2000]{0:T(1024)S(1)} %copy-done, s32[2048]{0:T(1024)S(1)} %get-tuple-element.170), kind=kCustom, calls=%fused_computation.5.clone | custom fusion | bytes 24576 | tf_op jit(solution)/shard_map/jit(_take)/gather | solution.py:77
  133.4 11.8 %gather_fusion.13 = f32[2048]{0:T(1024)S(1)} fusion(f32[2000]{0:T(1024)S(1)} %copy-done.2, s32[2048]{0:T(1024)S(1)} %get-tuple-element.170), kind=kCustom, calls=%fused_computation.7.clone | custom fusion | bytes 24576 | tf_op jit(solution)/shard_map/jit(_take)/gather | solution.py:80
  145.2 11.8 %gather_fusion.10 = f32[2048]{0:T(1024)S(1)} fusion(f32[2000]{0:T(1024)S(1)} %copy-done, s32[2048]{0:T(1024)S(1)} %get-tuple-element.171), kind=kCustom, calls=%fused_computation.1.clone | custom fusion | bytes 24576 | tf_op jit(solution)/shard_map/jit(_take)/gather | solution.py:77
  157.0 11.8 %gather_fusion.12 = f32[2048]{0:T(1024)S(1)} fusion(f32[2000]{0:T(1024)S(1)} %copy-done.2, s32[2048]{0:T(1024)S(1)} %get-tuple-element.171), kind=kCustom, calls=%fused_computation.6.clone | custom fusion | bytes 24576 | tf_op jit(solution)/shard_map/jit(_take)/gather | solution.py:80
  178.7 7.8 fusion.81
  195.1 13.8 %fusion.20 = f32[5,32,8,8,256]{4,3,2,1,0:T(8,128)} fusion(f32[5,32,8,8,1]{4,3,2,1,0:T(8,128)S(1)} %bitcast.333, f32[5,32,8,8,256]{4,3,2,1,0:T(8,128)} %get-tuple-element.41, f32[5,32,8,8,256]{4,3,2,1,0:T(8,128)} %fusion.74, f32[5,32,8,8,255]{4,3,2,1,0:T(8,128)S(1)} %bitcast.331, f32[32,8,8,256]{3,2,1,0:T(8,128)} %get-tuple-element.38, ...), kind=kLoop, calls=%fused_computation.54 | loop fusion | flops 20971520 | bytes 54525952 | tf_op jit(solution)/shard_map/sub | solution.py:70
  208.9 6.3 slice.1152
  250.1 7.1 gather_fusion.1
  257.2 10.9 %copy.485 = f32[32,2,5,6,6,128]{5,1,4,3,2,0:T(2,128)} copy(f32[32,2,5,6,6,128]{5,2,4,3,1,0:T(8,128)} %bitcast.378) | data formatting | bytes 11796480 | tf_op jit(solution)/shard_map/reshape | solution.py:164
  282.3 10.5 %stack.39 = f32[5,32,32,128]{3,0,2,1:T(8,128)} concatenate(f32[1,32,32,128]{3,0,2,1:T(1,128)} %bitcast.437, f32[1,32,32,128]{3,0,2,1:T(1,128)} %bitcast.440, f32[1,32,32,128]{3,0,2,1:T(1,128)} %bitcast.439, f32[1,32,32,128]{3,0,2,1:T(1,128)} %bitcast.436, f32[1,32,32,128]{3,0,2,1:T(1,128)} %bitcast.438), dimensions={0} | concatenate | bytes 5242880 | tf_op jit(solution)/shard_map/stack | solution.py:60
  306.4 15.1 %fusion.26 = f32[5,32,32,128]{3,0,2,1:T(8,128)} fusion(f32[5,32,32,128]{3,2,1,0:T(8,128)S(1)} %copy-done.38, f32[5,32,32,128]{3,2,1,0:T(8,128)S(1)} %pad_maximum_fusion.18, f32[5,32,32,128]{3,0,2,1:T(8,128)S(1)} %copy-done.45, f32[5,32,32,128]{3,2,1,0:T(8,128)S(1)} %fusion.147, f32[32,32,128]{2,1,0:T(8,128)S(1)} %get-tuple-element.132), kind=kLoop, calls=%fused_computation.70 | loop fusion | flops 3276800 | bytes 13631488 | tf_op jit(solution)/shard_map/sub | solution.py:70
  321.5 24.8 %all-to-all-done = f32[32,2,5,6,6,128]{5,1,4,3,2,0:T(2,128)} async-done(((f32[32,2,5,6,6,128]{5,1,4,3,2,0:T(2,128)}), f32[32,2,5,6,6,128]{5,1,4,3,2,0:T(2,128)}, u32[]{:S(2)}, u32[]{:S(2)}) %all-to-all-start) | async-done | bytes 5898272 | tf_op jit(solution)/shard_map/all_to_all | solution.py:267
  346.3 6.9 copy.486
  353.3 6.1 gather_fusion.2
  432.3 38.2 %fusion.3 = (f32[5,32,8,9,256]{4,3,2,1,0:T(8,128)}, f32[5,32,8,9,256]{4,3,2,1,0:T(8,128)}, f32[5,32,8,9,256]{4,3,2,1,0:T(8,128)}, f32[5,32,8,9,256]{4,3,2,1,0:T(8,128)}) fusion(f32[1,32,8,8,256]{4,3,2,1,0:T(8,128)S(1)} %bitcast.336, f32[5,32,8,1,256]{4,3,2,1,0:T(1,128)} %copy.529, f32[1,32,8,8,256]{4,3,2,1,0:T(8,128)S(1)} %bitcast.354, ...), kind=kLoop, calls=%fused_computation.24 | loop fusion | flops 35389440 | bytes 71303168 | tf_op jit(solution)/shard_map/concatenate | solution.py:109
  475.5 6.8 fusion.41
  482.3 8.7 add_dynamic-update-slice_fusion.1
  495.9 7.0 fusion.37
  503.0 8.5 add_dynamic-update-slice_fusion
  558.0 27.6 %fusion.11 = (f32[5,32,9,8,256]{4,3,2,1,0:T(8,128)}, f32[5,32,9,8,256]{4,3,2,1,0:T(8,128)}, f32[5,32,9,8,256]{4,3,2,1,0:T(8,128)}, f32[5,32,9,8,256]{4,3,2,1,0:T(8,128)}) fusion(f32[1,32,8,8,256]{4,3,2,1,0:T(8,128)S(1)} %bitcast.337, f32[5,32,1,8,256]{4,3,2,1,0:T(8,128)} %copy.509, f32[1,32,8,8,256]{4,3,2,1,0:T(8,128)} %bitcast.352, ...), kind=kLoop, calls=%fused_computation.44 | loop fusion | flops 35389440 | bytes 71303168 | tf_op jit(solution)/shard_map/concatenate | solution.py:100
  614.9 8.6 fusion.57
  625.2 13.0 %multiply_subtract_fusion.1 = f32[5,32,9,8,256]{4,3,2,1,0:T(8,128)} fusion(f32[5,32,9,8,256]{4,3,2,1,0:T(8,128)} %get-tuple-element.184, f32[5,32,9,8,256]{4,3,2,1,0:T(8,128)} %get-tuple-element.183, f32[32,9,8,256]{3,2,1,0:T(8,128)S(1)} %copy-done.53, f32[1,32,8,8,256]{4,3,2,1,0:T(8,128)S(1)} %bitcast.349, f32[3,32,8,8,256]{4,3,2,1,0:T(8,128)S(1)} %bitcast.329, ...), kind=kLoop, calls=%fused_computation.49 | loop fusion | flops 32440320 | bytes 50855936 | tf_op jit(solution)/shard_map/sub | solution.py:70
  641.3 17.8 %fusion.31 = (f32[32,8,9,256]{3,2,1,0:T(8,128)}, f32[5,32,8,9,256]{4,3,2,1,0:T(8,128)}, f32[5,32,8,9,256]{4,3,2,1,0:T(8,128)}) fusion(f32[5,32,8,9,256]{4,3,2,1,0:T(8,128)} %get-tuple-element.77, f32[5,32,8,9,256]{4,3,2,1,0:T(8,128)} %get-tuple-element.78, f32[5,32,8,9,256]{4,3,2,1,0:T(8,128)} %add_dynamic-update-slice_fusion.1, ...), kind=kLoop, calls=%fused_computation.76 | loop fusion | flops 7077888 | bytes 46137344 | tf_op jit(solution)/shard_map/mul | solution.py:70
  659.1 13.8 %fusion.35 = (f32[5,32,8,9,256]{4,3,2,1,0:T(8,128)}, f32[5,32,8,9,256]{4,3,2,1,0:T(8,128)}) fusion(f32[5,32,8,9,256]{4,3,2,1,0:T(8,128)} %get-tuple-element.67, f32[5,32,8,9,256]{4,3,2,1,0:T(8,128)} %get-tuple-element.104, f32[5,32,8,9,256]{4,3,2,1,0:T(8,128)} %get-tuple-element.77, f32[5,32,8,9,256]{4,3,2,1,0:T(8,128)} %get-tuple-element.66, ...), kind=kLoop, calls=%fused_computation.82 | loop fusion | flops 2359296 | bytes 33554432 | tf_op jit(solution)/shard_map/stack | solution.py:60
  672.9 22.5 %multiply_subtract_fusion = f32[5,32,8,9,256]{4,3,2,1,0:T(8,128)} fusion(f32[5,32,8,9,256]{4,3,2,1,0:T(8,128)} %get-tuple-element.182, f32[5,32,8,9,256]{4,3,2,1,0:T(8,128)} %get-tuple-element.181, f32[32,8,9,256]{3,2,1,0:T(8,128)S(1)} %copy-done.46, f32[1,32,8,8,256]{4,3,2,1,0:T(8,128)S(1)} %bitcast.350, f32[3,32,8,8,256]{4,3,2,1,0:T(8,128)S(1)} %bitcast.329, ...), kind=kLoop, calls=%fused_computation.29 | loop fusion | flops 32440320 | bytes 50855936 | tf_op jit(solution)/shard_map/sub | solution.py:70
  695.4 11.0 %fusion.191 = (f32[5,32,8,1,256]{4,3,2,1,0:T(1,128)}, f32[5,32,8,1,256]{4,3,2,1,0:T(1,128)}) fusion(f32[5,32,8,9,256]{4,3,2,1,0:T(8,128)} %multiply_subtract_fusion), kind=kLoop, calls=%fused_computation.481 | loop fusion | bytes 5242880 | tf_op jit(solution)/shard_map/slice | solution.py:146
  706.4 32.8 %fusion.24 = f32[5,32,8,8,256]{4,3,2,1,0:T(8,128)} fusion(f32[5,32,8,9,256]{4,3,2,1,0:T(8,128)} %multiply_subtract_fusion, f32[5,32,9,8,256]{4,3,2,1,0:T(8,128)} %multiply_subtract_fusion.1, f32[5,32,8,8,256]{4,3,2,1,0:T(8,128)} %fusion.20, f32[5,32,8,8,255]{4,3,2,1,0:T(8,128)} %bitcast.351, f32[5,32,8,8,1]{4,3,2,1,0:T(8,128)} %slice.1152, ...), kind=kLoop, calls=%fused_computation.59 | loop fusion | flops 26214400 | bytes 83886080 | tf_op jit(solution)/shard_map/sub | solution.py:130
  744.2 24.3 %copy.532 = f32[5,32,8,8,256]{1,4,3,2,0:T(8,128)} copy(f32[5,32,8,8,256]{4,3,2,1,0:T(8,128)} %fusion.75) | data formatting | bytes 20971520 | tf_op jit(solution)/shard_map/scatter-add | solution.py:131
  768.5 30.1 %reduce_sum.65 = f32[5,32,4,4,128]{1,4,3,2,0:T(8,128)} reduce(f32[5,32,4,2,4,2,128,2]{1,7,6,5,4,3,2,0:T(2,128)} %bitcast.343, f32[]{:T(128)} %constant.217.clone.1), dimensions={3,5,7}, to_apply=%region_3.6 | reduce | flops 2293760 | bytes 11796484 | tf_op jit(solution)/shard_map/reduce_sum | solution.py:134
  813.1 6.9 reduce_sum.66
  825.4 7.0 reduce_sum.67
  837.1 7.0 reduce_sum.68
  849.6 6.9 reduce_sum.69
  857.9 7.3 concatenate.172
  868.2 6.2 scatter_fusion
  907.2 9.3 copy_subtract_fusion
  919.4 14.3 %scatter-add.14 = f32[5,32,32,128]{3,0,2,1:T(8,128)} dynamic-update-slice(f32[5,32,32,128]{3,0,2,1:T(8,128)} %copy-done.40, f32[1,32,32,128]{3,0,2,1:T(1,128)S(1)} %slice_add_fusion.9, s32[]{:T(128)} %constant.203.clone.1, s32[]{:T(128)} %constant.204.clone.1, s32[]{:T(128)} %constant.204.clone.1, s32[]{:T(128)} %constant.204.clone.1) | dynamic-update-slice | bytes 1048580 | tf_op jit(solution)/shard_map/scatter-add | solution.py:211
  964.6 29.3 %scatter_fusion.1 = f32[5120,128]{1,0:T(8,128)S(1)} fusion(f32[5120,128]{1,0:T(8,128)S(1)} %bitcast.324, s32[5120]{0:T(1024)S(1)} %bitcast.443, f32[5120,128]{1,0:T(8,128)} %bitcast.398), kind=kCustom, calls=%fused_computation.15 | custom fusion | flops 655360 | bytes 7884800 | tf_op jit(solution)/shard_map/scatter-add | solution.py:322
  993.9 14.4 %scatter_fusion.2 = f32[5120,128]{1,0:T(8,128)S(1)} fusion(f32[5120,128]{1,0:T(8,128)S(1)} %scatter_fusion.1, s32[5120]{0:T(1024)S(1)} %bitcast.444, f32[5120,128]{1,0:T(8,128)} %bitcast.397), kind=kCustom, calls=%fused_computation.16 | custom fusion | bytes 7884800 | tf_op jit(solution)/shard_map/scatter | solution.py:329
  (565 shorter events, 383.0 us)
Async XLA Ops:
  0.6 9.0 copy-start
  0.7 8.8 copy-start.102
  2.3 223.3 %collective-permute-start.1 = (f32[5,1,32,128]{3,2,1,0:T(8,128)}, f32[5,1,32,128]{3,2,1,0:T(8,128)}, u32[]{:S(2)}, u32[]{:S(2)}) collective-permute-start(f32[5,1,32,128]{3,2,1,0:T(8,128)} %get-tuple-element.98), channel_id=1, source_target_pairs={{32,0},{64,32},{96,64},{0,96},{33,1},{65,33},{97,65},{1,97},{34,2}... | collective-permute-start | bytes 245768 | tf_op jit(solution)/shard_map/ppermute | solution.py:20
  6.4 219.2 %collective-permute-start = (f32[5,1,32,128]{3,2,1,0:T(8,128)}, f32[5,1,32,128]{3,2,1,0:T(8,128)}, u32[]{:S(2)}, u32[]{:S(2)}) collective-permute-start(f32[5,1,32,128]{3,2,1,0:T(8,128)} %get-tuple-element.97), channel_id=1, source_target_pairs={{0,32},{32,64},{64,96},{96,0},{1,33},{33,65},{65,97},{97,1},{2,34}... | collective-permute-start | bytes 245768 | tf_op jit(solution)/shard_map/ppermute | solution.py:18
  20.2 10.5 %copy-start.2 = (f32[2000]{0:T(1024)S(1)}, f32[2000]{0:T(1024)}, u32[]{:S(2)}) copy-start(f32[2000]{0:T(1024)} %param.31) | copy-start | bytes 24004
  41.2 17.3 %copy-start.5 = (f32[32,8,8,256]{3,2,1,0:T(8,128)S(1)}, f32[32,8,8,256]{3,2,1,0:T(8,128)}, u32[]{:S(2)}) copy-start(f32[32,8,8,256]{3,2,1,0:T(8,128)} %param.24) | copy-start | bytes 6291460
  53.6 8.5 copy-start.85
  62.1 15.7 %copy-start.4 = (f32[3,32,8,8,256]{4,3,2,1,0:T(8,128)}, f32[3,32,8,8,256]{4,3,2,1,0:T(8,128)S(1)}, u32[]{:S(2)}) copy-start(f32[3,32,8,8,256]{4,3,2,1,0:T(8,128)S(1)} %broadcast_multiply_fusion) | copy-start | bytes 18874372
  62.1 11.3 %slice-start.9 = ((s8[6291456]{0:T(1024)(128)(4,1)}), s8[4194304]{0:T(1024)(128)(4,1)S(1)}, s32[]{:S(2)}) async-start(s8[6291456]{0:T(1024)(128)(4,1)} %bitcast.341), calls=%async_computation.11 | async-start | bytes 8388608
  63.6 9.8 slice-start.10
  85.7 16.7 %slice-start.14 = ((s8[10485760]{0:T(1024)(128)(4,1)}), s8[4194304]{0:T(1024)(128)(4,1)S(1)}, s32[]{:S(2)}) async-start(s8[10485760]{0:T(1024)(128)(4,1)} %bitcast.358), calls=%async_computation.16 | async-start | bytes 8388608
  91.5 10.8 %slice-start.15 = ((s8[10485760]{0:T(1024)(128)(4,1)}), s8[4194304]{0:T(1024)(128)(4,1)S(1)}, s32[]{:S(2)}) async-start(s8[10485760]{0:T(1024)(128)(4,1)} %bitcast.358), calls=%async_computation.17 | async-start | bytes 8388608
  91.5 10.8 %slice-start.16 = ((s8[10485760]{0:T(1024)(128)(4,1)}), s8[2097152]{0:T(1024)(128)(4,1)S(1)}, s32[]{:S(2)}) async-start(s8[10485760]{0:T(1024)(128)(4,1)} %bitcast.358), calls=%async_computation.18 | async-start | bytes 4194304
  157.0 11.8 %copy-start.106 = (s32[32,2]{0,1:T(2,128)S(1)}, s32[32,2]{0,1:T(2,128)}, u32[]{:S(2)}) copy-start(s32[32,2]{0,1:T(2,128)} %copy-done.105) | copy-start | bytes 772
  157.0 11.8 %copy-start.108 = (s32[32,2]{0,1:T(2,128)S(1)}, s32[32,2]{0,1:T(2,128)}, u32[]{:S(2)}) copy-start(s32[32,2]{0,1:T(2,128)} %copy-done.107) | copy-start | bytes 772
  157.0 12.0 %copy-start.32 = (f32[5,32,32,128]{3,2,1,0:T(8,128)S(1)}, f32[5,32,32,128]{3,2,1,0:T(8,128)}, u32[]{:S(2)}) copy-start(f32[5,32,32,128]{3,2,1,0:T(8,128)} %pad_maximum_fusion.13) | copy-start | bytes 7864324
  174.8 11.8 %slice-start.4 = ((s8[10485760]{0:T(1024)(128)(4,1)}), s8[4194304]{0:T(1024)(128)(4,1)S(1)}, s32[]{:S(2)}) async-start(s8[10485760]{0:T(1024)(128)(4,1)} %bitcast.330), calls=%async_computation.6 | async-start | bytes 8388608
  174.8 11.8 %slice-start.5 = ((s8[10485760]{0:T(1024)(128)(4,1)}), s8[4194304]{0:T(1024)(128)(4,1)S(1)}, s32[]{:S(2)}) async-start(s8[10485760]{0:T(1024)(128)(4,1)} %bitcast.330), calls=%async_computation.7 | async-start | bytes 8388608
  174.8 11.8 %slice-start.7 = ((s8[5242880]{0:T(1024)(128)(4,1)}), s8[4194304]{0:T(1024)(128)(4,1)S(1)}, s32[]{:S(2)}) async-start(s8[5242880]{0:T(1024)(128)(4,1)} %bitcast.332), calls=%async_computation.9 | async-start | bytes 8388608
  178.7 8.5 slice-start.6
  178.7 8.8 slice-start.8
  208.9 11.6 %copy-start.103 = (s32[32,32]{1,0:T(8,128)S(1)}, s32[32,32]{1,0:T(8,128)}, u32[]{:S(2)}) copy-start(s32[32,32]{1,0:T(8,128)} %param.23) | copy-start | bytes 12292
  208.9 11.7 %copy-start.80 = (s32[32,8,8]{2,1,0:T(8,128)S(1)}, s32[32,8,8]{2,1,0:T(8,128)}, u32[]{:S(2)}) copy-start(s32[32,8,8]{2,1,0:T(8,128)} %copy-done.79) | copy-start | bytes 24580
  226.6 6.5 collective-permute-start.3
  231.0 7.4 collective-permute-start.2
  268.1 78.2 %all-to-all-start = ((f32[32,2,5,6,6,128]{5,1,4,3,2,0:T(2,128)}), f32[32,2,5,6,6,128]{5,1,4,3,2,0:T(2,128)}, u32[]{:S(2)}, u32[]{:S(2)}) async-start(f32[32,2,5,6,6,128]{5,1,4,3,2,0:T(2,128)} %copy.485), calls=%async_computation | async-start | bytes 11796480 | tf_op jit(solution)/shard_map/all_to_all | solution.py:267
  404.2 28.1 %copy-start.48 = (f32[5,32,8,1,256]{4,3,2,1,0:T(1,128)}, f32[5,32,8,1,256]{4,3,2,1,0:T(1,128)S(1)}, u32[]{:S(2)}) copy-start(f32[5,32,8,1,256]{4,3,2,1,0:T(1,128)S(1)} %copy.517) | copy-start | bytes 3932164
  432.3 38.3 %copy-start.50 = (f32[5,32,8,1,256]{4,3,2,1,0:T(1,128)}, f32[5,32,8,1,256]{4,3,2,1,0:T(1,128)S(1)}, u32[]{:S(2)}) copy-start(f32[5,32,8,1,256]{4,3,2,1,0:T(1,128)S(1)} %copy.527) | copy-start | bytes 3932164
  585.7 9.2 copy-start.25
  589.1 13.2 %slice-start.11 = ((s8[11796480]{0:T(1024)(128)(4,1)}), s8[4194304]{0:T(1024)(128)(4,1)S(1)}, s32[]{:S(2)}) async-start(s8[11796480]{0:T(1024)(128)(4,1)} %bitcast.355), calls=%async_computation.13 | async-start | bytes 8388608
  589.1 13.2 %slice-start.12 = ((s8[11796480]{0:T(1024)(128)(4,1)}), s8[4194304]{0:T(1024)(128)(4,1)S(1)}, s32[]{:S(2)}) async-start(s8[11796480]{0:T(1024)(128)(4,1)} %bitcast.355), calls=%async_computation.14 | async-start | bytes 8388608
  614.9 8.7 slice-start.2
  614.9 8.7 slice-start.3
  614.9 8.7 copy-start.17
  614.9 9.5 copy-start.47
  614.9 10.3 %copy-start.53 = (f32[32,9,8,256]{3,2,1,0:T(8,128)S(1)}, f32[32,9,8,256]{3,2,1,0:T(8,128)}, u32[]{:S(2)}) copy-start(f32[32,9,8,256]{3,2,1,0:T(8,128)} %get-tuple-element.70) | copy-start | bytes 7077892
  659.0 13.8 %copy-start.18 = (f32[32,8,8,256]{3,2,1,0:T(8,128)S(1)}, f32[32,8,8,256]{3,2,1,0:T(8,128)}, u32[]{:S(2)}) copy-start(f32[32,8,8,256]{3,2,1,0:T(8,128)} %copy-done.14) | copy-start | bytes 6291460
  659.0 13.8 %copy-start.46 = (f32[32,8,9,256]{3,2,1,0:T(8,128)S(1)}, f32[32,8,9,256]{3,2,1,0:T(8,128)}, u32[]{:S(2)}) copy-start(f32[32,8,9,256]{3,2,1,0:T(8,128)} %get-tuple-element.65) | copy-start | bytes 7077892
  659.0 13.8 %copy-start.49 = (f32[5,32,8,1,256]{4,3,2,1,0:T(1,128)S(1)}, f32[5,32,8,1,256]{4,3,2,1,0:T(1,128)}, u32[]{:S(2)}) copy-start(f32[5,32,8,1,256]{4,3,2,1,0:T(1,128)} %copy-done.48) | copy-start | bytes 3932164
  659.1 13.8 %copy-start.51 = (f32[5,32,8,1,256]{4,3,2,1,0:T(1,128)S(1)}, f32[5,32,8,1,256]{4,3,2,1,0:T(1,128)}, u32[]{:S(2)}) copy-start(f32[5,32,8,1,256]{4,3,2,1,0:T(1,128)} %copy-done.50) | copy-start | bytes 3932164
  706.4 32.8 %copy-start.84 = (f32[32,8,8]{2,1,0:T(8,128)S(1)}, f32[32,8,8]{2,1,0:T(8,128)}, u32[]{:S(2)}) copy-start(f32[32,8,8]{2,1,0:T(8,128)} %select_bitcast_fusion) | copy-start | bytes 24580
  874.5 79.1 %all-to-all-start.1 = ((f32[32,2,5,32,128]{4,3,2,1,0:T(8,128)}), f32[32,2,5,32,128]{4,3,2,1,0:T(8,128)}, u32[]{:S(2)}, u32[]{:S(2)}) async-start(f32[32,2,5,32,128]{4,3,2,1,0:T(8,128)} %scatter_fusion), calls=%async_computation.1 | async-start | bytes 10485760 | tf_op jit(solution)/shard_map/all_to_all | solution.py:280
  907.2 9.4 copy-start.29
  907.2 11.3 %copy-start.75 = (f32[32,32,128]{2,1,0:T(8,128)S(1)}, f32[32,32,128]{2,1,0:T(8,128)}, u32[]{:S(2)}) copy-start(f32[32,32,128]{2,1,0:T(8,128)} %get-tuple-element.131) | copy-start | bytes 1572868
  933.7 11.3 %copy-start.43 = (s32[256]{0:T(256)S(1)}, s32[256]{0:T(256)}, u32[]{:S(2)}) copy-start(s32[256]{0:T(256)} %reshape.1242) | copy-start | bytes 3076
  936.4 12.9 %copy-start.44 = (s32[256]{0:T(256)S(1)}, s32[256]{0:T(256)}, u32[]{:S(2)}) copy-start(s32[256]{0:T(256)} %reshape.1236) | copy-start | bytes 3076
  964.6 29.3 %copy-start.99 = (s32[5120,1]{0,1:T(1,128)S(1)}, s32[5120,1]{0,1:T(1,128)}, u32[]{:S(2)}) copy-start(s32[5120,1]{0,1:T(1,128)} %compare_select_fusion.4) | copy-start | bytes 61444
  993.9 15.9 %copy-start.1 = (f32[2000]{0:T(1024)S(1)}, f32[2000]{0:T(1024)}, u32[]{:S(2)}) copy-start(f32[2000]{0:T(1024)} %param.30) | copy-start | bytes 24004
  (99 other events, 373.2 us)
where the time goes:
time: 1020 us; the launch traced here: 1010 us
  other arithmetic  487 us (48%)
  local copies, waits for them, and re-layouts  470 us (46%)
  waiting for transfers between devices  30.8 us (3%)
  starting transfers between devices  19.2 us (2%)
    sub x6, other arithmetic, rusanov(): return average - 0.5 * fastest * (right_amounts - left_amounts)  73.5 us
    unnamed x37, other arithmetic  72.3 us
    unnamed x291, local copies, waits for them, and re-layouts  40.9 us
    mul x5, other arithmetic, rusanov(): return average - 0.5 * fastest * (right_amounts - left_amounts)  38.9 us
    concatenate x1, other arithmetic, fine_batch(): jnp.concatenate([ghost_low_y[:, :, :, None], primitive, ghost_high_y[:, :...  38.2 us
    sub x1, other arithmetic, fine_batch(): updated = amounts - FINE_STEP * change  32.8 us
    gather x4, local copies, waits for them, and re-layouts, energy_source(): jnp.take(heat_rate, bins + 1)  31.2 us
    reduce_sum x1, other arithmetic, fine_batch(): updated.reshape(5, batch, half, 2, half, 2, depth, 2).sum(axis=(3, 5, 7))  30.1 us
  transfers between devices with their start and end apart: 6, of which 3 were waited for; matrix products, arithmetic and copies ran while one was open for 33% of the time, Pallas kernels for 0%

commit v1 on v0

v1 whole, which is shorter than its diff:
```python
import functools

import jax
import jax.numpy as jnp
from jax import lax
from jax.experimental import pallas as pl
from jax.experimental.pallas import tpu as pltpu
from jax.sharding import PartitionSpec as P

GAMMA = 5.0 / 3.0
STEP = 0.02
HALF = 0.5 * STEP
FOOT = 4
SIDE = 5
CAP = 2
F32 = jnp.float32
VMEM = pltpu.VMEM
SMEM = pltpu.SMEM
MIB = 1024 * 1024
GRANT = 56 * MIB


def conserve(rho, ux, uy, uz, p):
    mx, my, mz = rho * ux, rho * uy, rho * uz
    xx, yy, zz = mx * ux, my * uy, mz * uz
    energy = 1.5 * p + 0.5 * (xx + yy + zz)
    return {
        "amounts": (rho, mx, my, mz, energy),
        "speed": (ux, uy, uz),
        "p": p,
        "square": (xx, yy, zz),
        "cross": {},
    }


def sound_of(p, rho):
    square = GAMMA * (p / rho)
    return square * lax.rsqrt(square)


def derive(prim):
    rho, p = prim[0], prim[4]
    both = rho + p
    common = p / (rho * both)
    square = GAMMA * (common * both)
    cell = conserve(*prim)
    cell["sound"] = square * lax.rsqrt(square)
    cell["share"] = common * rho
    return cell


def again(rho, ux, uy, uz, p, sound):
    cell = conserve(rho, ux, uy, uz, p)
    cell["sound"] = sound
    return cell


def directed(cell, d):
    amounts, p = cell["amounts"], cell["p"]
    u = cell["speed"][d]
    flux = [amounts[1 + d]]
    for k in range(3):
        if k == d:
            flux.append(cell["square"][d] + p)
            continue
        pair = (min(k, d), max(k, d))
        if pair not in cell["cross"]:
            cell["cross"][pair] = amounts[1 + pair[0]] * cell["speed"][pair[1]]
        flux.append(cell["cross"][pair])
    flux.append((amounts[4] + p) * u)
    return (amounts, flux, jnp.abs(u) + cell["sound"])


def twice_flux(left, right):
    fastest = jnp.maximum(left[2], right[2])
    return [
        (left[1][c] + right[1][c]) - fastest * (right[0][c] - left[0][c]) for c in range(5)
    ]


def shifted(cell, shift, axis):
    rho, p = cell["amounts"][0], cell["p"]
    values = (rho,) + cell["speed"] + (p, cell["sound"])
    return again(*[pltpu.roll(v, shift, axis) for v in values])


def source_term(rho, share, rates):
    heat, heat_slope, cool, cool_slope = rates
    return rho * ((heat + share * heat_slope) - rho * (cool + share * cool_slope))


def lane_pick(tile, lane):
    index = jnp.full((8, 128), lane, jnp.int32)
    return jnp.take_along_axis(tile, index, axis=1, mode="promise_in_bounds")


def pack_kernel(
    corner_ref, rho_hbm, vel_hbm, p_hbm, rim_ref, xa_ref, xb_ref, ya_ref, yb_ref, cell_ref, sem
):
    sources = [rho_hbm, vel_hbm.at[0], vel_hbm.at[1], vel_hbm.at[2], p_hbm]
    copies = [pltpu.make_async_copy(f, cell_ref.at[c], sem.at[c]) for c, f in enumerate(sources)]
    for copy in copies:
        copy.start()
    for copy in copies:
        copy.wait()
    fields = [cell_ref.at[c] for c in range(5)]
    width = 32
    rows = cell_ref.shape[1]

    def one(s, carry):
        base = corner_ref[s]

        @pl.when(base >= 0)
        def _():
            for c, f in enumerate(fields):
                rim_ref[s, c, 0:4, :] = f[pl.ds(base - width, 4), :]
                rim_ref[s, c, 4:8, :] = f[pl.ds(base + FOOT * width, 4), :]
                rim_ref[s, c, 8:12, :] = f[pl.ds(base - 1, 4, stride=width), :]
                rim_ref[s, c, 12:16, :] = f[pl.ds(base + FOOT, 4, stride=width), :]

        return carry

    for c, f in enumerate(fields):
        xa_ref[c] = f[0:width, :]
        xb_ref[c] = f[rows - width : rows, :]
        ya_ref[c] = f[pl.ds(0, width, stride=width), :]
        yb_ref[c] = f[pl.ds(width - 1, width, stride=width), :]
    lax.fori_loop(0, rim_ref.shape[0], one, 0)


def pack(corners, rho, vel, p, slots):
    whole = pl.BlockSpec(memory_space=VMEM)
    edge = jax.ShapeDtypeStruct((5, 32, 128), F32)
    return pl.pallas_call(
        pack_kernel,
        out_shape=[jax.ShapeDtypeStruct((slots, 5, 16, 128), F32), edge, edge, edge, edge],
        in_specs=[pl.BlockSpec(memory_space=SMEM)] + [pl.BlockSpec(memory_space=pl.ANY)] * 3,
        out_specs=[whole] * 5,
        scratch_shapes=[pltpu.VMEM((5,) + rho.shape, F32), pltpu.SemaphoreType.DMA((5,))],
        compiler_params=pltpu.CompilerParams(vmem_limit_bytes=GRANT),
        cost_estimate=pl.CostEstimate(flops=0, bytes_accessed=6 * MIB, transcendentals=0),
        name="pack_rims",
    )(corners, rho, vel, p)


def rates_kernel(bins_ref, table_ref, out_ref):
    for g in range(bins_ref.shape[0] // 8):
        rows = slice(8 * g, 8 * g + 8)
        low = None
        for step in range(2):
            b = bins_ref[rows, :] + step
            line = b // 128
            lane = b - line * 128
            found = [jnp.zeros((8, 128), F32) for _ in range(2)]
            for r in range(16):
                hit = line == r
                for t in range(2):
                    entry = jnp.broadcast_to(table_ref[t, r : r + 1, :], (8, 128))
                    value = jnp.take_along_axis(entry, lane, axis=1, mode="promise_in_bounds")
                    found[t] = jnp.where(hit, value, found[t])
            for t in range(2):
                entry = found[t] if step == 0 else found[t] - low[t]
                out_ref[2 * t + step, rows, :] = STEP * entry
            low = found


def look_up(bins, tables):
    whole = pl.BlockSpec(memory_space=VMEM)
    return pl.pallas_call(
        rates_kernel,
        out_shape=jax.ShapeDtypeStruct((4,) + bins.shape, F32),
        in_specs=[whole, whole],
        out_specs=whole,
        cost_estimate=pl.CostEstimate(flops=MIB, bytes_accessed=MIB, transcendentals=0),
        name="rate_lookup",
    )(bins, tables)


PITCH = 48
LOW = 8


def coarse_kernel(
    corner_ref, rho_ref, vel_ref, p_ref, xlo_ref, xhi_ref, ylo_ref, yhi_ref, rate_ref,
    out_ref, cell_ref, fx_ref, fy_ref,
):
    width = 32
    fields = [rho_ref, vel_ref.at[0], vel_ref.at[1], vel_ref.at[2], p_ref]

    def keep(prim, index):
        for n, v in enumerate(prim):
            cell_ref[n, index, :] = v
        cell_ref[5, index, :] = sound_of(prim[4], prim[0])

    def fill(x, carry):
        for q in range(4):
            rows = pl.ds(x * width + 8 * q, 8)
            keep([f[rows, :] for f in fields], pl.ds((x + 1) * PITCH + LOW + 8 * q, 8))
        return carry

    lax.fori_loop(0, width, fill, 0)
    for q in range(4):
        rows = slice(8 * q, 8 * q + 8)
        keep([xlo_ref[c, rows, :] for c in range(5)], pl.ds(LOW + 8 * q, 8))
        keep([xhi_ref[c, rows, :] for c in range(5)], pl.ds(33 * PITCH + LOW + 8 * q, 8))
        first = (8 * q + 1) * PITCH + LOW
        keep([ylo_ref[c, rows, :] for c in range(5)], pl.ds(first - 1, 8, stride=PITCH))
        keep([yhi_ref[c, rows, :] for c in range(5)], pl.ds(first + width, 8, stride=PITCH))

    def fetch(row):
        return again(*[cell_ref[n, pl.ds(row, 8), :] for n in range(6)])

    def step(x, carry):
        result = []
        for q in range(4):
            below = carry[5 * q : 5 * q + 5]
            row = (x + 1) * PITCH + LOW + 8 * q
            here = fetch(row)
            above = twice_flux(directed(here, 0), directed(fetch(row + PITCH), 0))
            y_here = directed(here, 1)
            y_high = twice_flux(y_here, directed(fetch(row + 1), 1))
            y_low = twice_flux(directed(fetch(row - 1), 1), y_here)
            z_high = twice_flux(directed(here, 2), directed(shifted(here, 127, 1), 2))
            rates = [lane_pick(rate_ref[t, 16 + 8 * q : 24 + 8 * q, :], x) for t in range(4)]
            rho = here["amounts"][0]
            gain = source_term(rho, here["p"] / (rho + here["p"]), rates)
            flat = pl.ds(x * width + 8 * q, 8)
            for c in range(5):
                change = (
                    (above[c] - below[c])
                    + (y_high[c] - y_low[c])
                    + (z_high[c] - pltpu.roll(z_high[c], 1, 1))
                )
                value = here["amounts"][c] - HALF * change
                if c == 4:
                    value = value + gain
                out_ref[c, flat, :] = value
                fx_ref[c, flat, :] = above[c]
                fy_ref[c, flat, :] = y_high[c]
            result += above
        return tuple(result)

    first = []
    for q in range(4):
        row = LOW + 8 * q
        first += twice_flux(directed(fetch(row), 0), directed(fetch(row + PITCH), 0))
    lax.fori_loop(0, width, step, tuple(first))

    def reflux(s, carry):
        base = corner_ref[s]

        @pl.when(base >= 0)
        def _():
            places = (
                (pl.ds(base - width, 4), pl.ds(base - width, 4), fx_ref, HALF),
                (
                    pl.ds(base + FOOT * width, 4),
                    pl.ds(base + (FOOT - 1) * width, 4),
                    fx_ref,
                    -HALF,
                ),
                (
                    pl.ds(base - 1, 4, stride=width),
                    pl.ds(base - 1, 4, stride=width),
                    fy_ref,
                    HALF,
                ),
                (
                    pl.ds(base + FOOT, 4, stride=width),
                    pl.ds(base + FOOT - 1, 4, stride=width),
                    fy_ref,
                    -HALF,
                ),
            )
            values = [
                [out_ref[c, a, :] + w * f[c, b, :] for a, b, f, w in places] for c in range(5)
            ]
            for c in range(5):
                for n in range(4):
                    out_ref[c, places[n][0], :] = values[c][n]

        return carry

    lax.fori_loop(0, corner_ref.shape[0], reflux, 0)


def coarse_step(corners, rho, vel, p, xlo, xhi, ylo, yhi, rates):
    whole = pl.BlockSpec(memory_space=VMEM)
    cells = rho.shape[0]
    return pl.pallas_call(
        coarse_kernel,
        out_shape=jax.ShapeDtypeStruct((5, cells, 128), F32),
        in_specs=[pl.BlockSpec(memory_space=SMEM)] + [whole] * 8,
        out_specs=whole,
        scratch_shapes=[
            pltpu.VMEM((6, 34 * PITCH, 128), F32),
            pltpu.VMEM((5, cells, 128), F32),
            pltpu.VMEM((5, cells, 128), F32),
        ],
        compiler_params=pltpu.CompilerParams(vmem_limit_bytes=32 * MIB),
        cost_estimate=pl.CostEstimate(
            flops=300 * cells * 128, bytes_accessed=30 * MIB, transcendentals=0
        ),
        name="coarse_step",
    )(corners, rho, vel, p, xlo, xhi, ylo, yhi, rates)


def take_lanes(tile, index):
    return jnp.take_along_axis(tile, index, axis=1, mode="promise_in_bounds")


def fold(even, odd):
    row = lax.broadcasted_iota(jnp.int32, (8, 128), 0)
    lane = lax.broadcasted_iota(jnp.int32, (8, 128), 1)
    halves = []
    for h in range(2):
        a, b = even[:, 128 * h : 128 * h + 128], odd[:, 128 * h : 128 * h + 128]
        a = a + pltpu.roll(a, 7, 0)
        b = b + pltpu.roll(b, 1, 0)
        m = jnp.where(row % 2 == 0, a, b)
        halves.append(m + pltpu.roll(m, 127 if h == 0 else 1, 1))
    mixed = jnp.where(lane % 2 == 0, halves[0], halves[1])
    return take_lanes(mixed, jnp.where(lane < 64, 2 * lane, 2 * lane - 127))


def patch_update(prim_refs, p_index, rates_at, faces, emit, on_plane=None):
    row = lax.broadcasted_iota(jnp.int32, (8, 256), 0)

    def plane(i):
        return [f[p_index, 8 * i : 8 * i + 8, :] for f in prim_refs]

    prim = plane(0)
    if on_plane is not None:
        on_plane(0, prim)
    here = derive(prim)
    below = None if faces is None else [faces(c, 0, slice(0, 8)) for c in range(5)]
    for i in range(8):
        if i < 7:
            prim = plane(i + 1)
            if on_plane is not None:
                on_plane(i + 1, prim)
            after = derive(prim)
            above = twice_flux(directed(here, 0), directed(after, 0))
        else:
            after = None
            above = None if faces is None else [faces(c, 1, slice(0, 8)) for c in range(5)]
        y_here = directed(here, 1)
        y_flux = twice_flux(y_here, directed(shifted(here, 7, 0), 1))
        z_here = directed(here, 2)
        z_flux = twice_flux(z_here, directed(shifted(here, 255, 1), 2))
        gain = source_term(here["amounts"][0], here["share"], rates_at(i))
        result = []
        for c in range(5):
            if faces is None:
                y_high, y_low = 0.0, 0.0
            else:
                y_high = jnp.broadcast_to(faces(c, 3, slice(i, i + 1)), (8, 256))
                y_low = jnp.broadcast_to(faces(c, 2, slice(i, i + 1)), (8, 256))
            change = jnp.where(row == 7, y_high, y_flux[c]) - jnp.where(
                row == 0, y_low, pltpu.roll(y_flux[c], 1, 0)
            )
            change = change + (z_flux[c] - pltpu.roll(z_flux[c], 1, 1))
            if above is not None:
                change = change + above[c]
            if below is not None:
                change = change - below[c]
            value = here["amounts"][c] - STEP * change
            if c == 4:
                value = value + gain
            result.append(value)
        emit(i, result)
        here, below = after, above


def rates_reader(rate_ref, patch):
    half = patch // 16
    start = pl.multiple_of(8 * half, 8)
    shift = 128 - 8 * (patch - 16 * half)
    tiles = [pltpu.roll(rate_ref[t, pl.ds(start, 8), :], shift, 1) for t in range(4)]

    def rates_at(i):
        return [jnp.broadcast_to(v[:, i : i + 1], (8, 256)) for v in tiles]

    return rates_at


PER = 4


def open_kernel(
    slot_ref, rho_ref, ux_ref, uy_ref, uz_ref, p_ref, rate_ref, mean_ref, edge_ref
):
    refs = [rho_ref, ux_ref.at[0], uy_ref.at[0], uz_ref.at[0], p_ref]

    def one(n, carry):
        patch = pl.program_id(0) * PER + n
        slot = slot_ref[patch]

        def on_plane(i, prim):
            for c in range(5):
                if i == 0:
                    edge_ref[n, c, 0] = prim[c]
                if i == 7:
                    edge_ref[n, c, 1] = prim[c]
                edge_ref[n, c, 2, i : i + 1, :] = prim[c][0:1, :]
                edge_ref[n, c, 3, i : i + 1, :] = prim[c][7:8, :]

        held = {}

        def emit(i, result):
            for c in range(5):
                at = (i // 2, c)
                held[at] = result[c] if i % 2 == 0 else held[at] + result[c]
                if i % 4 == 3:
                    value = fold(held.pop((i // 2 - 1, c)), held.pop(at))
                    mean_ref[slot, c, 8 * (i // 4) : 8 * (i // 4) + 8, :] = 0.125 * value

        patch_update(refs, n, rates_reader(rate_ref, patch), None, emit, on_plane)
        return carry

    lax.fori_loop(0, PER, one, 0)


def patch_specs(extra):
    one = pl.BlockSpec((PER, 64, 256), lambda i: (i, 0, 0))
    speed = [pl.BlockSpec((1, PER, 64, 256), lambda i, d=d: (d, i, 0, 0)) for d in range(3)]
    return [pl.BlockSpec(memory_space=SMEM)] * extra + [one] + speed + [one]


def open_patches(slot, rho, vel, p, rates, slots):
    count = rho.shape[0]
    return pl.pallas_call(
        open_kernel,
        grid=(count // PER,),
        out_shape=[
            jax.ShapeDtypeStruct((slots, 5, 32, 128), F32),
            jax.ShapeDtypeStruct((count, 5, 4, 8, 256), F32),
        ],
        in_specs=patch_specs(1) + [pl.BlockSpec(memory_space=VMEM)],
        out_specs=[
            pl.BlockSpec((slots, 5, 16, 128), lambda i: (0, 0, 0, 0)),
            pl.BlockSpec((PER, 5, 4, 8, 256), lambda i: (i, 0, 0, 0, 0)),
        ],
        compiler_params=pltpu.CompilerParams(vmem_limit_bytes=GRANT),
        cost_estimate=pl.CostEstimate(
            flops=250 * count * 64 * 256, bytes_accessed=18 * MIB, transcendentals=0
        ),
        name="open_patches",
    )(slot, rho, vel, vel, vel, p, rates)


BATCH = 4


def side_fluxes(rim, edge, ghost_ref):
    lane = lax.broadcasted_iota(jnp.int32, (16, 128), 1) // 2
    coarse = list(rim)
    coarse.append(sound_of(coarse[4], coarse[0]))
    for c in range(6):
        for h in range(2):
            wide = take_lanes(coarse[c], lane + 64 * h)
            ghost_ref[c, h, pl.ds(0, 16, stride=2), :] = wide
            ghost_ref[c, h, pl.ds(1, 16, stride=2), :] = wide
    sides = []
    for side in range(4):
        rows = slice(8 * side, 8 * side + 8)
        outer = [
            jnp.concatenate([ghost_ref[c, 0, rows, :], ghost_ref[c, 1, rows, :]], axis=1)
            for c in range(6)
        ]
        d = side // 2
        ghost = directed(again(*outer), d)
        prim = edge(side)
        inner = directed(again(*prim, sound_of(prim[4], prim[0])), d)
        sides.append(twice_flux(ghost, inner) if side % 2 == 0 else twice_flux(inner, ghost))
    return sides


def face_kernel(slot_ref, rim_ref, edge_ref, _, sum_ref, ghost_ref):
    first = pl.program_id(0) * BATCH
    for n in range(BATCH):
        slot = slot_ref[first + n]
        sides = side_fluxes(
            [rim_ref[slot, c] for c in range(5)],
            lambda side, n=n: [edge_ref[n, c, side] for c in range(5)],
            ghost_ref.at[n],
        )
        for c in range(5):
            for d in range(2):
                value = fold(sides[2 * d][c], sides[2 * d + 1][c])
                sum_ref[slot, c, 8 * d : 8 * d + 8, :] = (0.125 * STEP) * value


def face_fluxes(slot, rims, edges, buffer):
    count = edges.shape[0]
    slots = rims.shape[0]
    return pl.pallas_call(
        face_kernel,
        grid=(count // BATCH,),
        out_shape=jax.ShapeDtypeStruct(buffer.shape, F32),
        in_specs=[
            pl.BlockSpec(memory_space=SMEM),
            pl.BlockSpec((slots, 5, 16, 128), lambda i: (0, 0, 0, 0)),
            pl.BlockSpec((BATCH, 5, 4, 8, 256), lambda i: (i, 0, 0, 0, 0)),
            pl.BlockSpec(memory_space=pl.ANY),
        ],
        out_specs=pl.BlockSpec((slots, 5, 16, 128), lambda i: (0, 0, 1, 0)),
        input_output_aliases={3: 0},
        scratch_shapes=[pltpu.VMEM((BATCH, 6, 2, 32, 128), F32)],
        compiler_params=pltpu.CompilerParams(vmem_limit_bytes=GRANT),
        cost_estimate=pl.CostEstimate(
            flops=100 * count * 32 * 256, bytes_accessed=11 * MIB, transcendentals=0
        ),
        name="face_fluxes",
    )(slot, rims, edges, buffer)


def close_kernel(
    slot_ref, rho_ref, ux_ref, uy_ref, uz_ref, p_ref, rate_ref, rim_ref, edge_ref,
    out_ref, ghost_ref, rows_ref,
):
    refs = [rho_ref, ux_ref.at[0], uy_ref.at[0], uz_ref.at[0], p_ref]

    def one(n, carry):
        patch = pl.program_id(0) * PER + n
        slot = slot_ref[patch]
        sides = side_fluxes(
            [rim_ref[slot, c] for c in range(5)],
            lambda side: [edge_ref[n, c, side] for c in range(5)],
            ghost_ref,
        )
        for c in range(5):
            for d in range(2):
                rows_ref[c, d] = sides[2 + d][c]

        def faces(c, side, rows):
            return sides[side][c] if side < 2 else rows_ref[c, side - 2, rows, :]

        def emit(i, result):
            for c in range(5):
                out_ref[c, n, 8 * i : 8 * i + 8, :] = result[c]

        patch_update(refs, n, rates_reader(rate_ref, patch), faces, emit)
        return carry

    lax.fori_loop(0, PER, one, 0)


def close_patches(slot, rho, vel, p, rates, rims, edges):
    count = rho.shape[0]
    return pl.pallas_call(
        close_kernel,
        grid=(count // PER,),
        out_shape=jax.ShapeDtypeStruct((5,) + rho.shape, F32),
        in_specs=patch_specs(1)
        + [
            pl.BlockSpec(memory_space=VMEM),
            pl.BlockSpec(rims.shape, lambda i: (0, 0, 0, 0)),
            pl.BlockSpec((PER, 5, 4, 8, 256), lambda i: (i, 0, 0, 0, 0)),
        ],
        out_specs=pl.BlockSpec((5, PER, 64, 256), lambda i: (0, i, 0, 0)),
        scratch_shapes=[
            pltpu.VMEM((6, 2, 32, 128), F32),
            pltpu.VMEM((5, 2, 8, 256), F32),
        ],
        compiler_params=pltpu.CompilerParams(vmem_limit_bytes=GRANT),
        cost_estimate=pl.CostEstimate(
            flops=250 * count * 64 * 256, bytes_accessed=29 * MIB, transcendentals=0
        ),
        name="close_patches",
    )(slot, rho, vel, vel, vel, p, rates, rims, edges)


def merge_kernel(corner_ref, base_ref, got_ref, out_ref):
    width = 32
    out_ref[...] = base_ref[...]
    row = lax.broadcasted_iota(jnp.int32, (4, 128), 0)

    def one(s, carry):
        base = corner_ref[s]

        @pl.when(base >= 0)
        def _():
            rims = (
                pl.ds(base - width, 4),
                pl.ds(base + FOOT * width, 4),
                pl.ds(base - 1, 4, stride=width),
                pl.ds(base + FOOT, 4, stride=width),
            )
            result = []
            for c in range(5):
                flux = [
                    got_ref[s, c, pl.ds(16 + 8 * (n // 2) + n % 2, 4, stride=2), :]
                    for n in range(4)
                ]
                rim = [out_ref[c, at, :] for at in rims]
                rim = [rim[n] + flux[n] if n % 2 else rim[n] - flux[n] for n in range(4)]
                foot = []
                for i in range(4):
                    v = got_ref[s, c, pl.ds(8 * (i // 2) + i % 2, 4, stride=2), :]
                    if i == 0:
                        v = v + flux[0]
                    if i == 3:
                        v = v - flux[1]
                    low = jnp.broadcast_to(flux[2][i : i + 1, :], (4, 128))
                    high = jnp.broadcast_to(flux[3][i : i + 1, :], (4, 128))
                    v = v + jnp.where(row == 0, low, 0.0) - jnp.where(row == 3, high, 0.0)
                    foot.append(v)
                result.append((rim, foot))
            for c in range(5):
                rim, foot = result[c]
                for at, v in zip(rims, rim):
                    out_ref[c, at, :] = v
                for i in range(4):
                    out_ref[c, pl.ds(base + i * width, 4), :] = foot[i]

        return carry

    lax.fori_loop(0, corner_ref.shape[0], one, 0)


def merge(corners, base, got):
    whole = pl.BlockSpec(memory_space=VMEM)
    return pl.pallas_call(
        merge_kernel,
        out_shape=jax.ShapeDtypeStruct(base.shape, F32),
        in_specs=[pl.BlockSpec(memory_space=SMEM), whole, whole],
        out_specs=whole,
        compiler_params=pltpu.CompilerParams(vmem_limit_bytes=24 * MIB),
        cost_estimate=pl.CostEstimate(flops=MIB, bytes_accessed=11 * MIB, transcendentals=0),
        name="merge_patches",
    )(corners, base, got)


def exchange(buffer, groups):
    shape = buffer.shape
    rows = buffer.size // (groups * 128)
    moved = lax.all_to_all(
        buffer.reshape(groups, rows, 128), "yz", split_axis=0, concat_axis=0, tiled=True
    )
    return moved.reshape(shape)


def local(
    coarse_density,
    coarse_velocity,
    coarse_pressure,
    coarse_bins,
    fine_density,
    fine_velocity,
    fine_pressure,
    fine_bins,
    patch_host,
    patch_spot,
    heat_rate,
    cool_rate,
):
    groups = lax.axis_size("yz")
    rows = lax.axis_size("gx")
    gx = lax.axis_index("gx")
    me = lax.axis_index("yz")
    count = fine_density.shape[0]
    slots = CAP * groups

    total = groups * count
    hosts = lax.dynamic_slice_in_dim(patch_host, gx * total, total).reshape(groups, count)
    places = lax.dynamic_slice_in_dim(patch_spot, gx * total, total).reshape(groups, count)
    corner = (1 + SIDE * (places // 6)) * 32 + (1 + SIDE * (places % 6))
    order = jnp.arange(count, dtype=jnp.int32)
    earlier = order[None, :] < order[:, None]
    mine = hosts == me
    rank = jnp.sum((mine[:, None, :] & earlier[None]).astype(jnp.int32), axis=2)
    corners = jnp.stack(
        [jnp.max(jnp.where(mine & (rank == r), corner, -1), axis=1) for r in range(CAP)], axis=1
    ).reshape(slots)
    own = lax.dynamic_slice_in_dim(patch_host, (gx * groups + me) * count, count)
    own_rank = jnp.sum(((own[:, None] == own[None, :]) & earlier).astype(jnp.int32), axis=1)
    slot = CAP * own + own_rank

    rho = coarse_density.reshape(-1, 128)
    vel = coarse_velocity.reshape(3, -1, 128)
    press = coarse_pressure.reshape(-1, 128)
    rims, x_first, x_last, y_first, y_last = pack(corners, rho, vel, press, slots)
    arrived = exchange(rims, groups)

    up_x = [(i, (i + 1) % rows) for i in range(rows)]
    down_x = [((i + 1) % rows, i) for i in range(rows)]
    up_y = [(i, (i + 1) % groups) for i in range(groups)]
    down_y = [((i + 1) % groups, i) for i in range(groups)]
    x_low = lax.ppermute(x_last, "gx", up_x)
    x_high = lax.ppermute(x_first, "gx", down_x)
    y_low = lax.ppermute(y_last, "yz", up_y)
    y_high = lax.ppermute(y_first, "yz", down_y)

    fine_columns = fine_bins.reshape(2, 16, 8, 8).transpose(0, 3, 1, 2).reshape(16, 128)
    coarse_columns = jnp.pad(coarse_bins.T, ((0, 0), (0, 128 - coarse_bins.shape[0])))
    tables = jnp.pad(jnp.stack([heat_rate, cool_rate]), ((0, 0), (0, 48))).reshape(2, 16, 128)
    rates = look_up(jnp.concatenate([fine_columns, coarse_columns], axis=0), tables)

    f_rho = fine_density.reshape(count, 64, 256)
    f_vel = fine_velocity.reshape(3, count, 64, 256)
    f_press = fine_pressure.reshape(count, 64, 256)
    means, edges = open_patches(slot, f_rho, f_vel, f_press, rates, slots)
    sums = face_fluxes(slot, arrived, edges, means)
    sums, x_low, x_high, y_low, y_high = lax.optimization_barrier(
        (sums, x_low, x_high, y_low, y_high)
    )
    got = exchange(sums, groups)
    base = coarse_step(corners, rho, vel, press, x_low, x_high, y_low, y_high, rates)
    fine_new = close_patches(slot, f_rho, f_vel, f_press, rates, arrived, edges)
    coarse_new = merge(corners, base, got)
    return (
        coarse_new.reshape((5,) + coarse_density.shape),
        fine_new.reshape((5,) + fine_density.shape),
    )


def solution(mesh):
    placed = (
        P("gx", "yz", None),
        P(None, "gx", "yz", None),
        P("gx", "yz", None),
        P("gx", "yz"),
        P(("gx", "yz"), None, None, None),
        P(None, ("gx", "yz"), None, None, None),
        P(("gx", "yz"), None, None, None),
        P(("gx", "yz"), None, None),
        P(),
        P(),
        P(),
        P(),
    )
    return jax.shard_map(
        local,
        mesh=mesh,
        in_specs=placed,
        out_specs=(P(None, "gx", "yz", None), P(None, ("gx", "yz"), None, None, None)),
        check_vma=False,
    )
```

time: 1020 us -> 149 us (0.15)
  other arithmetic: 487 us -> 4.27 us
  local copies, waits for them, and re-layouts: 470 us -> 8.25 us
  Pallas kernels: 0 us -> 86.6 us
    gather x22 -> x0, local copies, waits for them, and re-layouts: 129 us -> none  [the longest x4 31.2 us: energy_source(): jnp.take(heat_rate, bins + 1)]
    sub x9 -> x0, other arithmetic: 118 us -> none  [the longest x6 73.5 us: rusanov(): return average - 0.5 * fastest * (right_amounts - left_amounts)]
    slice x34 -> x0, local copies, waits for them, and re-layouts: 95.8 us -> none  [the longest x2 16.7 us: fine_batch(): jnp.roll(amounts, -1, 4)]
    pallas_call x0 -> x7, Pallas kernels: none -> 86.6 us  [the longest x1 26.4 us: close_patches(): pl.pallas_call(close_kernel, grid=(count // PER,), out_shape=jax.ShapeDty...]
    concatenate x11 -> x1, other arithmetic: 84.6 us -> 0.61 us  [local(): jnp.concatenate([fine_columns, coarse_columns], axis=0)]
    unnamed x37 -> x1, other arithmetic: 72.3 us -> 0.02 us
    mul x26 -> x0, other arithmetic: 65.6 us -> none  [the longest x5 38.9 us: rusanov(): return average - 0.5 * fastest * (right_amounts - left_amounts)]
    reduce_sum x7 -> x2, other arithmetic: 58.8 us -> 0.8 us  [the longest x1 0.62 us: local(): rank = jnp.sum((mine[:, None, :] & earlier[None]).astype(jnp.int32), axis=2)]
  transfers between devices with their start and end apart: 6 -> 6, of which waited for: 3 -> 1; matrix products, arithmetic and copies ran while one was open for 33% -> 3% of each run, Pallas kernels for 0% -> 50%
where the time goes in v1:
time: 149 us; the launch traced here: 148 us
  Pallas kernels  86.6 us (58%)
  waiting for transfers between devices  26.2 us (18%)
  starting transfers between devices  21.7 us (15%)
  local copies, waits for them, and re-layouts  8.25 us (6%)
  other arithmetic  4.27 us (3%)
    pallas_call x1, Pallas kernels, close_patches(): pl.pallas_call(close_kernel, grid=(count // PER,), out_shape=jax.ShapeDty...  26.4 us
    all_to_all x2, waiting for transfers between devices, exchange(): lax.all_to_all(buffer.reshape(groups, rows, 128), 'yz', split_axis=0, con...  26.2 us
    pallas_call x1, Pallas kernels, open_patches(): pl.pallas_call(open_kernel, grid=(count // PER,), out_shape=[jax.ShapeDty...  25.8 us
    all_to_all x2, starting transfers between devices, exchange(): lax.all_to_all(buffer.reshape(groups, rows, 128), 'yz', split_axis=0, con...  12.5 us
    pallas_call x1, Pallas kernels, face_fluxes(): pl.pallas_call(face_kernel, grid=(count // BATCH,), out_shape=jax.ShapeDt...  10.7 us
    pallas_call x1, Pallas kernels, coarse_step(): pl.pallas_call(coarse_kernel, out_shape=jax.ShapeDtypeStruct((5, cells, 1...  9.78 us
    pallas_call x1, Pallas kernels, merge(): pl.pallas_call(merge_kernel, out_shape=jax.ShapeDtypeStruct(base.shape, F...  6.53 us
    unnamed x34, local copies, waits for them, and re-layouts  6.15 us
  transfers between devices with their start and end apart: 6, of which 1 were waited for; matrix products, arithmetic and copies ran while one was open for 3% of the time, Pallas kernels for 50%

profile of v1, /device:TPU:0, one launch (start us, length us, event | category | flops | bytes accessed | tf_op | source)
XLA Modules:
  0.0 148.0 jit_solution(851330233038824939)
XLA Ops:
  0.7 0.7 dynamic-slice_divide_fusion
  1.4 0.7 sign_compare_fusion
  2.1 0.1 ne.27
  2.1 0.1 eq.39
  2.2 0.1 div.10
  2.3 0.1 rem.19
  2.4 0.6 convert_reduce_fusion
  3.0 0.1 select_reduce_fusion.1
  3.1 0.1 copy.21
  3.2 0.6 reshape.82.corner_ref
  3.9 5.4 %pack_rims.1 = (f32[64,5,16,128]{3,2,1,0:T(8,128)}, f32[5,32,128]{2,1,0:T(8,128)}, f32[5,32,128]{2,1,0:T(8,128)}, f32[5,32,128]{2,1,0:T(8,128)}, f32[5,32,128]{2,1,0:T(8,128)}) custom-call(s32[64]{0:T(128)} %reshape.82.corner_ref, f32[1024,128]{1,0:T(8,128)} %bitcast.29, f32[3,1024,128]{2,1,0:T(8,128)} %bitcast.27, f32[1024,128]{1,0:T(8,128)} %bitcast.31), custom_call_target="tpu_custom_call" | custom-call | bytes 6291456 | tf_op jit(solution)/shard_map/pack_rims/pallas_call | solution.py:134
  9.3 0.0 copy-start.14
  9.3 0.0 copy-start.9
  9.4 0.0 copy-start.10
  9.4 0.0 copy-start.11
  9.4 0.0 copy-start.8
  9.4 7.6 %all-to-all-start = ((f32[32,160,128]{2,1,0:T(8,128)}), f32[32,160,128]{2,1,0:T(8,128)S(1)}, u32[]{:S(2)}, u32[]{:S(2)}) async-start(f32[32,160,128]{2,1,0:T(8,128)} %bitcast.47), calls=%async_computation | async-start | bytes 5242880 | tf_op jit(solution)/shard_map/all_to_all | solution.py:638
  17.0 2.0 %collective-permute-start = (f32[5,32,128]{2,1,0:T(8,128)S(1)}, f32[5,32,128]{2,1,0:T(8,128)S(1)}, u32[]{:S(2)}, u32[]{:S(2)}) collective-permute-start(f32[5,32,128]{2,1,0:T(8,128)S(1)} %copy-done.15), channel_id=1, source_target_pairs={{0,32},{32,64},{64,96},{96,0},{1,33},{33,65},{65,97},{97,1},{2,34}... | collective-permute-start | bytes 245768 | tf_op jit(solution)/shard_map/ppermute | solution.py:690
  19.0 2.2 %collective-permute-start.1 = (f32[5,32,128]{2,1,0:T(8,128)S(1)}, f32[5,32,128]{2,1,0:T(8,128)S(1)}, u32[]{:S(2)}, u32[]{:S(2)}) collective-permute-start(f32[5,32,128]{2,1,0:T(8,128)S(1)} %copy-done.14), channel_id=1, source_target_pairs={{32,0},{64,32},{96,64},{0,96},{33,1},{65,33},{97,65},{1,97},{34,2}... | collective-permute-start | bytes 245768 | tf_op jit(solution)/shard_map/ppermute | solution.py:691
  21.2 0.0 collective-permute-start.2
  21.2 5.1 %collective-permute-start.3 = (f32[5,32,128]{2,1,0:T(8,128)S(1)}, f32[5,32,128]{2,1,0:T(8,128)S(1)}, u32[]{:S(2)}, u32[]{:S(2)}) collective-permute-start(f32[5,32,128]{2,1,0:T(8,128)S(1)} %copy-done.12), channel_id=1, source_target_pairs={{1,0},{2,1},{3,2},{4,3},{5,4},{6,5},{7,6},{8,7},{9,8},{10,9},{11,1... | collective-permute-start | bytes 245768 | tf_op jit(solution)/shard_map/ppermute | solution.py:693
  26.3 0.8 dynamic_slice.11
  27.0 0.1 copy.23
  27.1 0.6 copy.26
  27.8 0.1 reshape.91
  27.9 0.1 copy.22
  28.0 0.1 reshape.92
  28.1 0.2 convert_reduce_fusion.1
  28.3 1.3 multiply_add_fusion.slot_ref
  29.5 0.6 pad_add_fusion.bins_ref
  30.2 1.9 %rate_lookup.1.rate_ref = f32[4,48,128]{2,1,0:T(8,128)} custom-call(s32[48,128]{1,0:T(8,128)} %pad_add_fusion.bins_ref, f32[2,16,128]{2,1,0:T(8,128)} %bitcast.50), custom_call_target="tpu_custom_call" | custom-call | flops 1048576 | bytes 1048576 | tf_op jit(solution)/shard_map/rate_lookup/pallas_call | solution.py:169
  32.1 25.8 %open_patches.1 = (f32[64,5,32,128]{3,2,1,0:T(8,128)}, f32[32,5,4,8,256]{4,3,2,1,0:T(8,128)}) custom-call(s32[32]{0:T(128)} %multiply_add_fusion.slot_ref, f32[32,64,256]{2,1,0:T(8,128)} %bitcast.43, f32[3,32,64,256]{3,2,1,0:T(8,128)} %bitcast.33, f32[3,32,64,256]{3,2,1,0:T(8,128)} %bitcast.34, f32[3,32,64,256]{3,2,1,0:T(8,128)} %bitcast.35, ...), custom_call_target="tpu_custom_call" | custom-call | flops 131072000 | bytes 18874368 | tf_op jit(solution)/shard_map/open_patches/pallas_call | solution.py:432
  57.9 0.0 all-to-all-done
  57.9 0.0 copy-start.7
  57.9 1.5 %copy-done.7 = f32[32,160,128]{2,1,0:T(8,128)} copy-done((f32[32,160,128]{2,1,0:T(8,128)}, f32[32,160,128]{2,1,0:T(8,128)S(1)}, u32[]{:S(2)}) %copy-start.7) | copy-done | bytes 2621464
  59.4 10.7 %face_fluxes.1 = f32[64,5,32,128]{3,2,1,0:T(8,128)} custom-call(s32[32]{0:T(128)} %multiply_add_fusion.slot_ref, f32[64,5,16,128]{3,2,1,0:T(8,128)} %bitcast.39, f32[32,5,4,8,256]{4,3,2,1,0:T(8,128)} %get-tuple-element.15.edge_ref, f32[64,5,32,128]{3,2,1,0:T(8,128)} %get-tuple-element.16._), custom_call_target="tpu_custom_call", output_to_operand_aliasing={{}: (3, {})} | custom-call | flops 26214400 | bytes 11534336 | tf_op jit(solution)/shard_map/face_fluxes/pallas_call | solution.py:497
  70.2 0.0 copy-start.4
  70.2 0.0 copy-start.1
  70.2 0.6 copy-done.4
  70.8 4.9 %all-to-all-start.1 = ((f32[32,320,128]{2,1,0:T(8,128)}), f32[32,320,128]{2,1,0:T(8,128)}, u32[]{:S(2)}, u32[]{:S(2)}) async-start(f32[32,320,128]{2,1,0:T(8,128)} %bitcast.41), calls=%async_computation.1 | async-start | bytes 10485760 | tf_op jit(solution)/shard_map/all_to_all | solution.py:638
  75.7 0.0 copy-start
  75.7 1.4 copy-done
  77.1 1.0 copy-done.2
  78.2 0.9 copy-done.5
  79.1 9.8 %coarse_step.1.base_ref = f32[5,1024,128]{2,1,0:T(8,128)S(1)} custom-call(s32[64]{0:T(128)S(1)} %copy-done.6, f32[1024,128]{1,0:T(8,128)S(1)} %bitcast.30, f32[3,1024,128]{2,1,0:T(8,128)S(1)} %bitcast.28, f32[1024,128]{1,0:T(8,128)S(1)} %bitcast.32, f32[5,32,128]{2,1,0:T(8,128)S(1)} %collective-permute-done.xlo_ref, ...), custom_call_target="tpu_custom_call" | custom-call | flops 39321600 | bytes 31457280 | tf_op jit(solution)/shard_map/coarse_step/pallas_call | solution.py:290
  88.8 26.4 %close_patches.1 = f32[5,32,64,256]{3,2,1,0:T(8,128)} custom-call(s32[32]{0:T(128)} %multiply_add_fusion.slot_ref, f32[32,64,256]{2,1,0:T(8,128)} %bitcast.44, f32[3,32,64,256]{3,2,1,0:T(8,128)} %bitcast.36, f32[3,32,64,256]{3,2,1,0:T(8,128)} %bitcast.37, f32[3,32,64,256]{3,2,1,0:T(8,128)} %bitcast.38, f32[32,64,256]{2,1,0:T(8,128)} %bitcast.46, ...), custom_call_target="tpu_custom_call" | custom-call | flops 131072000 | bytes 30408704 | tf_op jit(solution)/shard_map/close_patches/pallas_call | solution.py:551
  115.2 26.2 %all-to-all-done.1 = f32[32,320,128]{2,1,0:T(8,128)} async-done(((f32[32,320,128]{2,1,0:T(8,128)}), f32[32,320,128]{2,1,0:T(8,128)}, u32[]{:S(2)}, u32[]{:S(2)}) %all-to-all-start.1) | async-done | bytes 5242912 | tf_op jit(solution)/shard_map/all_to_all | solution.py:638
  141.4 6.5 %merge_patches.1 = f32[5,1024,128]{2,1,0:T(8,128)} custom-call(s32[64]{0:T(128)S(1)} %copy-done.6, f32[5,1024,128]{2,1,0:T(8,128)S(1)} %coarse_step.1.base_ref, f32[64,5,32,128]{3,2,1,0:T(8,128)} %bitcast.15.got_ref), custom_call_target="tpu_custom_call" | custom-call | flops 1048576 | bytes 11534336 | tf_op jit(solution)/shard_map/merge_patches/pallas_call | solution.py:624
  (25 shorter events, 0.1 us)
Async XLA Ops:
  9.3 7.7 %copy-start.15 = (f32[5,32,128]{2,1,0:T(8,128)S(1)}, f32[5,32,128]{2,1,0:T(8,128)}, u32[]{:S(2)}) copy-start(f32[5,32,128]{2,1,0:T(8,128)} %get-tuple-element.17) | copy-start | bytes 245764
  9.3 9.7 %copy-start.14 = (f32[5,32,128]{2,1,0:T(8,128)S(1)}, f32[5,32,128]{2,1,0:T(8,128)}, u32[]{:S(2)}) copy-start(f32[5,32,128]{2,1,0:T(8,128)} %get-tuple-element.18) | copy-start | bytes 245764
  9.3 11.9 %copy-start.13 = (f32[5,32,128]{2,1,0:T(8,128)S(1)}, f32[5,32,128]{2,1,0:T(8,128)}, u32[]{:S(2)}) copy-start(f32[5,32,128]{2,1,0:T(8,128)} %get-tuple-element.19) | copy-start | bytes 245764
  9.3 11.9 %copy-start.12 = (f32[5,32,128]{2,1,0:T(8,128)S(1)}, f32[5,32,128]{2,1,0:T(8,128)}, u32[]{:S(2)}) copy-start(f32[5,32,128]{2,1,0:T(8,128)} %get-tuple-element.20) | copy-start | bytes 245764
  9.3 17.7 %copy-start.9 = (s32[32,32]{1,0:T(8,128)S(1)}, s32[32,32]{1,0:T(8,128)}, u32[]{:S(2)}) copy-start(s32[32,32]{1,0:T(8,128)} %param.15) | copy-start | bytes 12292
  9.4 17.8 %copy-start.10 = (f32[2000]{0:T(1024)S(1)}, f32[2000]{0:T(1024)}, u32[]{:S(2)}) copy-start(f32[2000]{0:T(1024)} %param.23) | copy-start | bytes 24004
  9.4 17.7 %copy-start.11 = (f32[2000]{0:T(1024)S(1)}, f32[2000]{0:T(1024)}, u32[]{:S(2)}) copy-start(f32[2000]{0:T(1024)} %param.22) | copy-start | bytes 24004
  9.4 18.4 %copy-start.8 = (s32[32,8,8]{0,2,1:T(8,128)S(1)}, s32[32,8,8]{0,2,1:T(8,128)}, u32[]{:S(2)}) copy-start(s32[32,8,8]{0,2,1:T(8,128)} %param.19) | copy-start | bytes 24580
  9.4 48.5 %all-to-all-start = ((f32[32,160,128]{2,1,0:T(8,128)}), f32[32,160,128]{2,1,0:T(8,128)S(1)}, u32[]{:S(2)}, u32[]{:S(2)}) async-start(f32[32,160,128]{2,1,0:T(8,128)} %bitcast.47), calls=%async_computation | async-start | bytes 5242880 | tf_op jit(solution)/shard_map/all_to_all | solution.py:638
  17.0 53.1 %collective-permute-start = (f32[5,32,128]{2,1,0:T(8,128)S(1)}, f32[5,32,128]{2,1,0:T(8,128)S(1)}, u32[]{:S(2)}, u32[]{:S(2)}) collective-permute-start(f32[5,32,128]{2,1,0:T(8,128)S(1)} %copy-done.15), channel_id=1, source_target_pairs={{0,32},{32,64},{64,96},{96,0},{1,33},{33,65},{65,97},{97,1},{2,34}... | collective-permute-start | bytes 245768 | tf_op jit(solution)/shard_map/ppermute | solution.py:690
  19.0 51.2 %collective-permute-start.1 = (f32[5,32,128]{2,1,0:T(8,128)S(1)}, f32[5,32,128]{2,1,0:T(8,128)S(1)}, u32[]{:S(2)}, u32[]{:S(2)}) collective-permute-start(f32[5,32,128]{2,1,0:T(8,128)S(1)} %copy-done.14), channel_id=1, source_target_pairs={{32,0},{64,32},{96,64},{0,96},{33,1},{65,33},{97,65},{1,97},{34,2}... | collective-permute-start | bytes 245768 | tf_op jit(solution)/shard_map/ppermute | solution.py:691
  21.2 48.9 %collective-permute-start.2 = (f32[5,32,128]{2,1,0:T(8,128)S(1)}, f32[5,32,128]{2,1,0:T(8,128)S(1)}, u32[]{:S(2)}, u32[]{:S(2)}) collective-permute-start(f32[5,32,128]{2,1,0:T(8,128)S(1)} %copy-done.13), channel_id=1, source_target_pairs={{0,1},{1,2},{2,3},{3,4},{4,5},{5,6},{6,7},{7,8},{8,9},{9,10},{10,1... | collective-permute-start | bytes 245768 | tf_op jit(solution)/shard_map/ppermute | solution.py:692
  21.2 48.9 %collective-permute-start.3 = (f32[5,32,128]{2,1,0:T(8,128)S(1)}, f32[5,32,128]{2,1,0:T(8,128)S(1)}, u32[]{:S(2)}, u32[]{:S(2)}) collective-permute-start(f32[5,32,128]{2,1,0:T(8,128)S(1)} %copy-done.12), channel_id=1, source_target_pairs={{1,0},{2,1},{3,2},{4,3},{5,4},{6,5},{7,6},{8,7},{9,8},{10,9},{11,1... | collective-permute-start | bytes 245768 | tf_op jit(solution)/shard_map/ppermute | solution.py:693
  57.9 1.5 %copy-start.7 = (f32[32,160,128]{2,1,0:T(8,128)}, f32[32,160,128]{2,1,0:T(8,128)S(1)}, u32[]{:S(2)}) copy-start(f32[32,160,128]{2,1,0:T(8,128)S(1)} %all-to-all-done) | copy-start | bytes 7864324
  70.2 0.6 copy-start.4
  70.2 5.5 %copy-start.1 = (f32[32,32,128]{2,1,0:T(8,128)S(1)}, f32[32,32,128]{2,1,0:T(8,128)}, u32[]{:S(2)}) copy-start(f32[32,32,128]{2,1,0:T(8,128)} %param.12) | copy-start | bytes 1572868
  70.2 5.5 %copy-start.3 = (f32[4,48,128]{2,1,0:T(8,128)S(1)}, f32[4,48,128]{2,1,0:T(8,128)}, u32[]{:S(2)}) copy-start(f32[4,48,128]{2,1,0:T(8,128)} %rate_lookup.1.rate_ref) | copy-start | bytes 294916
  70.2 5.5 %copy-start.6 = (s32[64]{0:T(128)S(1)}, s32[64]{0:T(128)}, u32[]{:S(2)}) copy-start(s32[64]{0:T(128)} %reshape.82.corner_ref) | copy-start | bytes 772
  70.8 70.6 %all-to-all-start.1 = ((f32[32,320,128]{2,1,0:T(8,128)}), f32[32,320,128]{2,1,0:T(8,128)}, u32[]{:S(2)}, u32[]{:S(2)}) async-start(f32[32,320,128]{2,1,0:T(8,128)} %bitcast.41), calls=%async_computation.1 | async-start | bytes 10485760 | tf_op jit(solution)/shard_map/all_to_all | solution.py:638
  75.7 1.4 copy-start
  77.1 1.0 copy-start.2
  78.2 0.9 copy-start.5

commit v2 on v1

--- a/solution.py
+++ b/solution.py
@@ -94,13 +94,54 @@
     return jnp.take_along_axis(tile, index, axis=1, mode="promise_in_bounds")
 
 
+def plan_places(place_ref, host_ref, spot_ref, corner_ref, slot_ref):
+    gx, me = place_ref[0], place_ref[1]
+    rows = pl.ds(pl.multiple_of(8 * gx, 8), 8)
+    hosts, spots = host_ref[rows, :], spot_ref[rows, :]
+    lane = lax.broadcasted_iota(jnp.int32, (8, 128), 1)
+    row = lax.broadcasted_iota(jnp.int32, (8, 128), 0)
+    place_x = (spots * 43) >> 8
+    corner = (1 + SIDE * place_x) * 32 + 1 + SIDE * (spots - 6 * place_x)
+    key = jnp.where(hosts == me, lane * 1024 + corner, -1)
+    table = jnp.full((8, 128), -1, jnp.int32)
+    far = 1 << 20
+    for q in range(4):
+        inside = (lane // 32 == q) & (key >= 0)
+        last = jnp.max(jnp.where(inside, key, -1), axis=1, keepdims=True)
+        first = jnp.min(jnp.where(inside, key, far), axis=1, keepdims=True)
+        none = last < 0
+        single = none | (first == last)
+        table = jnp.where(lane == 2 * q, jnp.where(none, -1, first & 1023), table)
+        table = jnp.where(lane == 2 * q + 1, jnp.where(single, -1, last & 1023), table)
+    corner_ref[...] = table
+    own = jnp.sum(jnp.where(row == me // 4, hosts, 0), axis=0, keepdims=True)
+    own = pltpu.roll(jnp.broadcast_to(own, (8, 128)), lax.rem(128 - 32 * lax.rem(me, 4), 128), 1)
+    own = jnp.broadcast_to(own[0:1, :], (32, 128))
+    lane = lax.broadcasted_iota(jnp.int32, (32, 128), 1)
+    row = lax.broadcasted_iota(jnp.int32, (32, 128), 0)
+    mine = jnp.sum(jnp.where(lane == row, own, 0), axis=1, keepdims=True)
+    rank = jnp.sum(jnp.where((own == mine) & (lane < row), 1, 0), axis=1, keepdims=True)
+    slot_ref[...] = jnp.broadcast_to(CAP * mine + rank, (32, 128))
+
+
+def corner_at(corner_ref, s):
+    line = s // 8
+    return corner_ref[line, s - 8 * line]
+
+
 def pack_kernel(
-    corner_ref, rho_hbm, vel_hbm, p_hbm, rim_ref, xa_ref, xb_ref, ya_ref, yb_ref, cell_ref, sem
+    place_ref, host_ref, spot_ref, rho_hbm, vel_hbm, p_hbm,
+    rim_ref, xa_ref, xb_ref, ya_ref, yb_ref, corner_ref, slot_ref,
+    cell_ref, table_ref, sem, table_sem,
 ):
     sources = [rho_hbm, vel_hbm.at[0], vel_hbm.at[1], vel_hbm.at[2], p_hbm]
     copies = [pltpu.make_async_copy(f, cell_ref.at[c], sem.at[c]) for c, f in enumerate(sources)]
     for copy in copies:
         copy.start()
+    plan_places(place_ref, host_ref, spot_ref, corner_ref, slot_ref)
+    move = pltpu.make_async_copy(corner_ref, table_ref, table_sem)
+    move.start()
+    move.wait()
     for copy in copies:
         copy.wait()
     fields = [cell_ref.at[c] for c in range(5)]
@@ -108,7 +149,7 @@
     rows = cell_ref.shape[1]
 
     def one(s, carry):
-        base = corner_ref[s]
+        base = corner_at(table_ref, s)
 
         @pl.when(base >= 0)
         def _():
@@ -120,27 +161,34 @@
 
         return carry
 
+    lax.fori_loop(0, rim_ref.shape[0], one, 0)
     for c, f in enumerate(fields):
         xa_ref[c] = f[0:width, :]
         xb_ref[c] = f[rows - width : rows, :]
         ya_ref[c] = f[pl.ds(0, width, stride=width), :]
         yb_ref[c] = f[pl.ds(width - 1, width, stride=width), :]
-    lax.fori_loop(0, rim_ref.shape[0], one, 0)
-
-
-def pack(corners, rho, vel, p, slots):
+
+
+def pack(place, hosts, spots, rho, vel, p, slots):
     whole = pl.BlockSpec(memory_space=VMEM)
     edge = jax.ShapeDtypeStruct((5, 32, 128), F32)
     return pl.pallas_call(
         pack_kernel,
-        out_shape=[jax.ShapeDtypeStruct((slots, 5, 16, 128), F32), edge, edge, edge, edge],
-        in_specs=[pl.BlockSpec(memory_space=SMEM)] + [pl.BlockSpec(memory_space=pl.ANY)] * 3,
-        out_specs=[whole] * 5,
-        scratch_shapes=[pltpu.VMEM((5,) + rho.shape, F32), pltpu.SemaphoreType.DMA((5,))],
+        out_shape=[jax.ShapeDtypeStruct((slots, 5, 16, 128), F32), edge, edge, edge, edge]
+        + [jax.ShapeDtypeStruct((8, 128), jnp.int32), jax.ShapeDtypeStruct((32, 128), jnp.int32)],
+        in_specs=[pl.BlockSpec(memory_space=SMEM), whole, whole]
+        + [pl.BlockSpec(memory_space=pl.ANY)] * 3,
+        out_specs=[whole] * 7,
+        scratch_shapes=[
+            pltpu.VMEM((5,) + rho.shape, F32),
+            pltpu.SMEM((8, 128), jnp.int32),
+            pltpu.SemaphoreType.DMA((5,)),
+            pltpu.SemaphoreType.DMA,
+        ],
         compiler_params=pltpu.CompilerParams(vmem_limit_bytes=GRANT),
         cost_estimate=pl.CostEstimate(flops=0, bytes_accessed=6 * MIB, transcendentals=0),
         name="pack_rims",
-    )(corners, rho, vel, p)
+    )(place, hosts, spots, rho, vel, p)
 
 
 def rates_kernel(bins_ref, table_ref, out_ref):
@@ -247,7 +295,7 @@
     lax.fori_loop(0, width, step, tuple(first))
 
     def reflux(s, carry):
-        base = corner_ref[s]
+        base = corner_at(corner_ref, s)
 
         @pl.when(base >= 0)
         def _():
@@ -281,7 +329,7 @@
 
         return carry
 
-    lax.fori_loop(0, corner_ref.shape[0], reflux, 0)
+    lax.fori_loop(0, 8 * corner_ref.shape[0], reflux, 0)
 
 
 def coarse_step(corners, rho, vel, p, xlo, xhi, ylo, yhi, rates):
@@ -340,7 +388,9 @@
             if on_plane is not None:
                 on_plane(i + 1, prim)
             after = derive(prim)
-            above = twice_flux(directed(here, 0), directed(after, 0))
+            above = None
+            if faces is not None or i % 2 == 1:
+                above = twice_flux(directed(here, 0), directed(after, 0))
         else:
             after = None
             above = None if faces is None else [faces(c, 1, slice(0, 8)) for c in range(5)]
@@ -394,7 +444,7 @@
 
     def one(n, carry):
         patch = pl.program_id(0) * PER + n
-        slot = slot_ref[patch]
+        slot = slot_ref[patch, 0]
 
         def on_plane(i, prim):
             for c in range(5):
@@ -479,7 +529,7 @@
 def face_kernel(slot_ref, rim_ref, edge_ref, _, sum_ref, ghost_ref):
     first = pl.program_id(0) * BATCH
     for n in range(BATCH):
-        slot = slot_ref[first + n]
+        slot = slot_ref[first + n, 0]
         sides = side_fluxes(
             [rim_ref[slot, c] for c in range(5)],
             lambda side, n=n: [edge_ref[n, c, side] for c in range(5)],
@@ -507,7 +557,7 @@
         out_specs=pl.BlockSpec((slots, 5, 16, 128), lambda i: (0, 0, 1, 0)),
         input_output_aliases={3: 0},
         scratch_shapes=[pltpu.VMEM((BATCH, 6, 2, 32, 128), F32)],
-        compiler_params=pltpu.CompilerParams(vmem_limit_bytes=GRANT),
+        compiler_params=pltpu.CompilerParams(vmem_limit_bytes=20 * MIB),
         cost_estimate=pl.CostEstimate(
             flops=100 * count * 32 * 256, bytes_accessed=11 * MIB, transcendentals=0
         ),
@@ -523,7 +573,7 @@
 
     def one(n, carry):
         patch = pl.program_id(0) * PER + n
-        slot = slot_ref[patch]
+        slot = slot_ref[patch, 0]
         sides = side_fluxes(
             [rim_ref[slot, c] for c in range(5)],
             lambda side: [edge_ref[n, c, side] for c in range(5)],
@@ -573,11 +623,16 @@
 
 def merge_kernel(corner_ref, base_ref, got_ref, out_ref):
     width = 32
-    out_ref[...] = base_ref[...]
+    count = got_ref.shape[0]
+
+    @pl.when(pl.program_id(0) == 0)
+    def _():
+        out_ref[...] = base_ref[...]
+
     row = lax.broadcasted_iota(jnp.int32, (4, 128), 0)
 
     def one(s, carry):
-        base = corner_ref[s]
+        base = corner_at(corner_ref, pl.program_id(0) * count + s)
 
         @pl.when(base >= 0)
         def _():
@@ -616,15 +671,21 @@
 
         return carry
 
-    lax.fori_loop(0, corner_ref.shape[0], one, 0)
+    lax.fori_loop(0, count, one, 0)
 
 
 def merge(corners, base, got):
-    whole = pl.BlockSpec(memory_space=VMEM)
+    slots = got.shape[0]
+    whole = pl.BlockSpec(base.shape, lambda i: (0, 0, 0))
     return pl.pallas_call(
         merge_kernel,
+        grid=(4,),
         out_shape=jax.ShapeDtypeStruct(base.shape, F32),
-        in_specs=[pl.BlockSpec(memory_space=SMEM), whole, whole],
+        in_specs=[
+            pl.BlockSpec(memory_space=SMEM),
+            whole,
+            pl.BlockSpec((slots // 4, 5, 32, 128), lambda i: (i, 0, 0, 0)),
+        ],
         out_specs=whole,
         compiler_params=pltpu.CompilerParams(vmem_limit_bytes=24 * MIB),
         cost_estimate=pl.CostEstimate(flops=MIB, bytes_accessed=11 * MIB, transcendentals=0),
@@ -662,25 +723,14 @@
     count = fine_density.shape[0]
     slots = CAP * groups
 
-    total = groups * count
-    hosts = lax.dynamic_slice_in_dim(patch_host, gx * total, total).reshape(groups, count)
-    places = lax.dynamic_slice_in_dim(patch_spot, gx * total, total).reshape(groups, count)
-    corner = (1 + SIDE * (places // 6)) * 32 + (1 + SIDE * (places % 6))
-    order = jnp.arange(count, dtype=jnp.int32)
-    earlier = order[None, :] < order[:, None]
-    mine = hosts == me
-    rank = jnp.sum((mine[:, None, :] & earlier[None]).astype(jnp.int32), axis=2)
-    corners = jnp.stack(
-        [jnp.max(jnp.where(mine & (rank == r), corner, -1), axis=1) for r in range(CAP)], axis=1
-    ).reshape(slots)
-    own = lax.dynamic_slice_in_dim(patch_host, (gx * groups + me) * count, count)
-    own_rank = jnp.sum(((own[:, None] == own[None, :]) & earlier).astype(jnp.int32), axis=1)
-    slot = CAP * own + own_rank
-
     rho = coarse_density.reshape(-1, 128)
     vel = coarse_velocity.reshape(3, -1, 128)
     press = coarse_pressure.reshape(-1, 128)
-    rims, x_first, x_last, y_first, y_last = pack(corners, rho, vel, press, slots)
+    place = jnp.stack([gx, me]).astype(jnp.int32)
+    host_lines, spot_lines = patch_host.reshape(-1, 128), patch_spot.reshape(-1, 128)
+    rims, x_first, x_last, y_first, y_last, corners, slot = pack(
+        place, host_lines, spot_lines, rho, vel, press, slots
+    )
     arrived = exchange(rims, groups)
 
     up_x = [(i, (i + 1) % rows) for i in range(rows)]

time: 149 us -> 147 us (0.987)
  local copies, waits for them, and re-layouts: 8.25 us -> 13.2 us
  other arithmetic: 4.27 us -> 1.23 us
  Pallas kernels: 86.6 us -> 83.9 us
    unnamed x34 -> x42, local copies, waits for them, and re-layouts: 6.15 us -> 12.9 us
    pallas_call x1, Pallas kernels: 10.7 us -> 7.11 us  [face_fluxes(): pl.pallas_call(face_kernel, grid=(count // BATCH,), out_shape=jax.ShapeDt...]
  transfers between devices with their start and end apart: 6 -> 6, of which waited for: 1 -> 1; matrix products, arithmetic and copies ran while one was open for 3% -> 1% of each run, Pallas kernels for 50% -> 48%
where the time goes in v2:
time: 147 us
  Pallas kernels  83.9 us (57%)
  waiting for transfers between devices  25.5 us (17%)
  starting transfers between devices  21.8 us (15%)
  local copies, waits for them, and re-layouts  13.2 us (9%)
    pallas_call x1, Pallas kernels, close_patches(): pl.pallas_call(close_kernel, grid=(count // PER,), out_shape=jax.ShapeDty...  26.3 us
    all_to_all x2, waiting for transfers between devices, exchange(): lax.all_to_all(buffer.reshape(groups, rows, 128), 'yz', split_axis=0, con...  25.5 us
    pallas_call x1, Pallas kernels, open_patches(): pl.pallas_call(open_kernel, grid=(count // PER,), out_shape=[jax.ShapeDty...  25.2 us
    unnamed x42, local copies, waits for them, and re-layouts  12.9 us
    all_to_all x2, starting transfers between devices, exchange(): lax.all_to_all(buffer.reshape(groups, rows, 128), 'yz', split_axis=0, con...  12.6 us
    pallas_call x1, Pallas kernels, coarse_step(): pl.pallas_call(coarse_kernel, out_shape=jax.ShapeDtypeStruct((5, cells, 1...  10.5 us
    pallas_call x1, Pallas kernels, face_fluxes(): pl.pallas_call(face_kernel, grid=(count // BATCH,), out_shape=jax.ShapeDt...  7.11 us
    pallas_call x1, Pallas kernels, merge(): pl.pallas_call(merge_kernel, grid=(4,), out_shape=jax.ShapeDtypeStruct(ba...  6.79 us
  transfers between devices with their start and end apart: 6, of which 1 were waited for; matrix products, arithmetic and copies ran while one was open for 1% of the time, Pallas kernels for 48%

profile of v2, /device:TPU:0, one launch (start us, length us, event | category | flops | bytes accessed | tf_op | source)
XLA Modules:
  0.0 146.6 jit_solution(429467931192137508)
XLA Ops:
  0.6 0.6 pad_add_fusion.1.place_ref
  1.2 6.0 %pack_rims.1 = (f32[64,5,16,128]{3,2,1,0:T(8,128)}, f32[5,32,128]{2,1,0:T(8,128)}, f32[5,32,128]{2,1,0:T(8,128)}, f32[5,32,128]{2,1,0:T(8,128)}, f32[5,32,128]{2...) custom-call(s32[2]{0:T(128)} %pad_add_fusion.1.place_ref, s32[32,128]{1,0:T(8,128)} %bitcast.54, s32[32,128]{1,0:T(8,128)} %bitcast.55, ...), custom_call_target="tpu_custom_call" | custom-call | bytes 6291456 | tf_op jit(solution)/shard_map/pack_rims/pallas_call | solution.py:175
  7.3 0.0 copy-start.19
  7.3 0.0 copy-start.18
  7.3 0.0 copy-start.13
  7.3 0.0 copy-start.14
  7.3 0.0 copy-start.15
  7.4 0.0 copy-start.12
  7.4 7.5 %all-to-all-start = ((f32[32,160,128]{2,1,0:T(8,128)}), f32[32,160,128]{2,1,0:T(8,128)S(1)}, u32[]{:S(2)}, u32[]{:S(2)}) async-start(f32[32,160,128]{2,1,0:T(8,128)} %bitcast.49), calls=%async_computation | async-start | bytes 5242880 | tf_op jit(solution)/shard_map/all_to_all | solution.py:699
  14.9 2.1 %collective-permute-start = (f32[5,32,128]{2,1,0:T(8,128)S(1)}, f32[5,32,128]{2,1,0:T(8,128)S(1)}, u32[]{:S(2)}, u32[]{:S(2)}) collective-permute-start(f32[5,32,128]{2,1,0:T(8,128)S(1)} %copy-done.19), channel_id=1, source_target_pairs={{0,32},{32,64},{64,96},{96,0},{1,33},{33,65},{65,97},{97,1},{2,34}... | collective-permute-start | bytes 245768 | tf_op jit(solution)/shard_map/ppermute | solution.py:740
  17.0 2.1 %collective-permute-start.1 = (f32[5,32,128]{2,1,0:T(8,128)S(1)}, f32[5,32,128]{2,1,0:T(8,128)S(1)}, u32[]{:S(2)}, u32[]{:S(2)}) collective-permute-start(f32[5,32,128]{2,1,0:T(8,128)S(1)} %copy-done.18), channel_id=1, source_target_pairs={{32,0},{64,32},{96,64},{0,96},{33,1},{65,33},{97,65},{1,97},{34,2}... | collective-permute-start | bytes 245768 | tf_op jit(solution)/shard_map/ppermute | solution.py:741
  19.1 0.0 copy-done.17
  19.1 0.0 collective-permute-start.2
  19.1 5.1 %collective-permute-start.3 = (f32[5,32,128]{2,1,0:T(8,128)S(1)}, f32[5,32,128]{2,1,0:T(8,128)S(1)}, u32[]{:S(2)}, u32[]{:S(2)}) collective-permute-start(f32[5,32,128]{2,1,0:T(8,128)S(1)} %copy-done.16), channel_id=1, source_target_pairs={{1,0},{2,1},{3,2},{4,3},{5,4},{6,5},{7,6},{8,7},{9,8},{10,9},{11,1... | collective-permute-start | bytes 245768 | tf_op jit(solution)/shard_map/ppermute | solution.py:743
  24.2 0.1 copy.18
  24.3 0.0 copy-done.15
  24.3 0.6 copy.21
  24.9 0.0 copy-done.12
  24.9 0.1 reshape.65
  25.0 0.1 copy.17
  25.1 0.1 reshape.66
  25.2 0.6 pad_add_fusion.bins_ref
  25.8 1.9 %rate_lookup.1.rate_ref = f32[4,48,128]{2,1,0:T(8,128)} custom-call(s32[48,128]{1,0:T(8,128)} %pad_add_fusion.bins_ref, f32[2,16,128]{2,1,0:T(8,128)} %bitcast.52), custom_call_target="tpu_custom_call" | custom-call | flops 1048576 | bytes 1048576 | tf_op jit(solution)/shard_map/rate_lookup/pallas_call | solution.py:217
  27.7 25.2 %open_patches.1 = (f32[64,5,32,128]{3,2,1,0:T(8,128)}, f32[32,5,4,8,256]{4,3,2,1,0:T(8,128)}) custom-call(s32[32,128]{1,0:T(8,128)} %get-tuple-element.17.slot_ref, f32[32,64,256]{2,1,0:T(8,128)} %bitcast.45, f32[3,32,64,256]{3,2,1,0:T(8,128)} %bitcast.38, f32[3,32,64,256]{3,2,1,0:T(8,128)} %bitcast.39, f32[3,32,64,256]{3,2,1,0:T(8,128)} %bitcast.40, ...), custom_call_target="tpu_custom_call" | custom-call | flops 131072000 | bytes 18874368 | tf_op jit(solution)/shard_map/open_patches/pallas_call | solution.py:482
  53.0 0.0 all-to-all-done
  53.0 0.0 copy-start
  53.0 0.0 copy-start.1
  53.0 3.4 %copy-done.1 = f32[64,5,32,128]{3,2,1,0:T(8,128)S(1)} copy-done((f32[64,5,32,128]{3,2,1,0:T(8,128)S(1)}, f32[64,5,32,128]{3,2,1,0:T(8,128)}, u32[]{:S(2)}) %copy-start.1) | copy-done | bytes 5242904
  56.4 2.5 %copy-done.3 = f32[32,5,4,8,256]{4,3,2,1,0:T(8,128)S(1)} copy-done((f32[32,5,4,8,256]{4,3,2,1,0:T(8,128)S(1)}, f32[32,5,4,8,256]{4,3,2,1,0:T(8,128)}, u32[]{:S(2)}) %copy-start.3) | copy-done | bytes 5242904
  58.9 7.1 %face_fluxes.1 = f32[64,5,32,128]{3,2,1,0:T(8,128)S(1)} custom-call(s32[32,128]{1,0:T(8,128)S(1)} %copy-done.8, f32[64,5,16,128]{3,2,1,0:T(8,128)S(1)} %bitcast.29, f32[32,5,4,8,256]{4,3,2,1,0:T(8,128)S(1)} %copy-done.3, f32[64,5,32,128]{3,2,1,0:T(8,128)S(1)} %copy-done.1), custom_call_target="tpu_custom_call", output_to_operand_aliasing={{}: (3, {})} | custom-call | flops 26214400 | bytes 11534336 | tf_op jit(solution)/shard_map/face_fluxes/pallas_call | solution.py:547
  66.0 0.0 copy-done
  66.1 0.0 copy-start.2
  66.1 2.3 %copy-done.2 = f32[64,5,32,128]{3,2,1,0:T(8,128)} copy-done((f32[64,5,32,128]{3,2,1,0:T(8,128)}, f32[64,5,32,128]{3,2,1,0:T(8,128)S(1)}, u32[]{:S(2)}) %copy-start.2) | copy-done | bytes 5242904
  68.4 0.0 collective-permute-done.xlo_ref
  68.4 0.0 collective-permute-done.1.xhi_ref
  68.4 0.0 collective-permute-done.2.ylo_ref
  68.4 0.0 collective-permute-done.3.yhi_ref
  68.4 0.0 copy-start.9
  68.4 0.6 copy-done.9
  69.0 5.0 %all-to-all-start.1 = ((f32[32,320,128]{2,1,0:T(8,128)}), f32[32,320,128]{2,1,0:T(8,128)}, u32[]{:S(2)}, u32[]{:S(2)}) async-start(f32[32,320,128]{2,1,0:T(8,128)} %bitcast.31), calls=%async_computation.1 | async-start | bytes 10485760 | tf_op jit(solution)/shard_map/all_to_all | solution.py:699
  74.1 0.0 copy-start.4
  74.1 1.4 copy-done.4
  75.5 1.0 copy-done.6
  76.5 0.9 copy-done.10
  77.4 10.5 %coarse_step.1.base_ref = f32[5,1024,128]{2,1,0:T(8,128)S(1)} custom-call(s32[8,128]{1,0:T(8,128)S(1)} %copy-done.11, f32[1024,128]{1,0:T(8,128)S(1)} %bitcast.35, f32[3,1024,128]{2,1,0:T(8,128)S(1)} %bitcast.33, f32[1024,128]{1,0:T(8,128)S(1)} %bitcast.37, f32[5,32,128]{2,1,0:T(8,128)S(1)} %collective-permute-done.xlo_ref, ...), custom_call_target="tpu_custom_call" | custom-call | flops 39321600 | bytes 31457280 | tf_op jit(solution)/shard_map/coarse_step/pallas_call | solution.py:338
  87.9 26.3 %close_patches.1 = f32[5,32,64,256]{3,2,1,0:T(8,128)} custom-call(s32[32,128]{1,0:T(8,128)} %get-tuple-element.17.slot_ref, f32[32,64,256]{2,1,0:T(8,128)} %bitcast.46, f32[3,32,64,256]{3,2,1,0:T(8,128)} %bitcast.41, f32[3,32,64,256]{3,2,1,0:T(8,128)} %bitcast.42, f32[3,32,64,256]{3,2,1,0:T(8,128)} %bitcast.43, f32[32,64,256]{2,1,0:T(8,128)} %bitcast.48, ...), custom_call_target="tpu_custom_call" | custom-call | flops 131072000 | bytes 30408704 | tf_op jit(solution)/shard_map/close_patches/pallas_call | solution.py:601
  114.3 25.5 %all-to-all-done.1 = f32[32,320,128]{2,1,0:T(8,128)} async-done(((f32[32,320,128]{2,1,0:T(8,128)}), f32[32,320,128]{2,1,0:T(8,128)}, u32[]{:S(2)}, u32[]{:S(2)}) %all-to-all-start.1) | async-done | bytes 5242912 | tf_op jit(solution)/shard_map/all_to_all | solution.py:699
  139.8 6.8 %merge_patches.1 = f32[5,1024,128]{2,1,0:T(8,128)} custom-call(s32[8,128]{1,0:T(8,128)S(1)} %copy-done.11, f32[5,1024,128]{2,1,0:T(8,128)S(1)} %coarse_step.1.base_ref, f32[64,5,32,128]{3,2,1,0:T(8,128)} %bitcast.17.got_ref), custom_call_target="tpu_custom_call" | custom-call | flops 1048576 | bytes 11534336 | tf_op jit(solution)/shard_map/merge_patches/pallas_call | solution.py:680
  (19 shorter events, 0.1 us)
Async XLA Ops:
  7.3 7.6 %copy-start.19 = (f32[5,32,128]{2,1,0:T(8,128)S(1)}, f32[5,32,128]{2,1,0:T(8,128)}, u32[]{:S(2)}) copy-start(f32[5,32,128]{2,1,0:T(8,128)} %get-tuple-element.21) | copy-start | bytes 245764
  7.3 9.7 %copy-start.18 = (f32[5,32,128]{2,1,0:T(8,128)S(1)}, f32[5,32,128]{2,1,0:T(8,128)}, u32[]{:S(2)}) copy-start(f32[5,32,128]{2,1,0:T(8,128)} %get-tuple-element.22) | copy-start | bytes 245764
  7.3 11.8 %copy-start.17 = (f32[5,32,128]{2,1,0:T(8,128)S(1)}, f32[5,32,128]{2,1,0:T(8,128)}, u32[]{:S(2)}) copy-start(f32[5,32,128]{2,1,0:T(8,128)} %get-tuple-element.23) | copy-start | bytes 245764
  7.3 11.8 %copy-start.16 = (f32[5,32,128]{2,1,0:T(8,128)S(1)}, f32[5,32,128]{2,1,0:T(8,128)}, u32[]{:S(2)}) copy-start(f32[5,32,128]{2,1,0:T(8,128)} %get-tuple-element.24) | copy-start | bytes 245764
  7.3 16.9 %copy-start.13 = (s32[32,32]{1,0:T(8,128)S(1)}, s32[32,32]{1,0:T(8,128)}, u32[]{:S(2)}) copy-start(s32[32,32]{1,0:T(8,128)} %param.15) | copy-start | bytes 12292
  7.3 16.9 %copy-start.14 = (f32[2000]{0:T(1024)S(1)}, f32[2000]{0:T(1024)}, u32[]{:S(2)}) copy-start(f32[2000]{0:T(1024)} %param.23) | copy-start | bytes 24004
  7.3 16.9 %copy-start.15 = (f32[2000]{0:T(1024)S(1)}, f32[2000]{0:T(1024)}, u32[]{:S(2)}) copy-start(f32[2000]{0:T(1024)} %param.22) | copy-start | bytes 24004
  7.4 17.5 %copy-start.12 = (s32[32,8,8]{0,2,1:T(8,128)S(1)}, s32[32,8,8]{0,2,1:T(8,128)}, u32[]{:S(2)}) copy-start(s32[32,8,8]{0,2,1:T(8,128)} %param.19) | copy-start | bytes 24580
  7.4 45.6 %all-to-all-start = ((f32[32,160,128]{2,1,0:T(8,128)}), f32[32,160,128]{2,1,0:T(8,128)S(1)}, u32[]{:S(2)}, u32[]{:S(2)}) async-start(f32[32,160,128]{2,1,0:T(8,128)} %bitcast.49), calls=%async_computation | async-start | bytes 5242880 | tf_op jit(solution)/shard_map/all_to_all | solution.py:699
  14.9 53.4 %collective-permute-start = (f32[5,32,128]{2,1,0:T(8,128)S(1)}, f32[5,32,128]{2,1,0:T(8,128)S(1)}, u32[]{:S(2)}, u32[]{:S(2)}) collective-permute-start(f32[5,32,128]{2,1,0:T(8,128)S(1)} %copy-done.19), channel_id=1, source_target_pairs={{0,32},{32,64},{64,96},{96,0},{1,33},{33,65},{65,97},{97,1},{2,34}... | collective-permute-start | bytes 245768 | tf_op jit(solution)/shard_map/ppermute | solution.py:740
  17.0 51.4 %collective-permute-start.1 = (f32[5,32,128]{2,1,0:T(8,128)S(1)}, f32[5,32,128]{2,1,0:T(8,128)S(1)}, u32[]{:S(2)}, u32[]{:S(2)}) collective-permute-start(f32[5,32,128]{2,1,0:T(8,128)S(1)} %copy-done.18), channel_id=1, source_target_pairs={{32,0},{64,32},{96,64},{0,96},{33,1},{65,33},{97,65},{1,97},{34,2}... | collective-permute-start | bytes 245768 | tf_op jit(solution)/shard_map/ppermute | solution.py:741
  19.1 49.3 %collective-permute-start.2 = (f32[5,32,128]{2,1,0:T(8,128)S(1)}, f32[5,32,128]{2,1,0:T(8,128)S(1)}, u32[]{:S(2)}, u32[]{:S(2)}) collective-permute-start(f32[5,32,128]{2,1,0:T(8,128)S(1)} %copy-done.17), channel_id=1, source_target_pairs={{0,1},{1,2},{2,3},{3,4},{4,5},{5,6},{6,7},{7,8},{8,9},{9,10},{10,1... | collective-permute-start | bytes 245768 | tf_op jit(solution)/shard_map/ppermute | solution.py:742
  19.1 49.3 %collective-permute-start.3 = (f32[5,32,128]{2,1,0:T(8,128)S(1)}, f32[5,32,128]{2,1,0:T(8,128)S(1)}, u32[]{:S(2)}, u32[]{:S(2)}) collective-permute-start(f32[5,32,128]{2,1,0:T(8,128)S(1)} %copy-done.16), channel_id=1, source_target_pairs={{1,0},{2,1},{3,2},{4,3},{5,4},{6,5},{7,6},{8,7},{9,8},{10,9},{11,1... | collective-permute-start | bytes 245768 | tf_op jit(solution)/shard_map/ppermute | solution.py:743
  27.7 25.3 %copy-start.8 = (s32[32,128]{1,0:T(8,128)S(1)}, s32[32,128]{1,0:T(8,128)}, u32[]{:S(2)}) copy-start(s32[32,128]{1,0:T(8,128)} %get-tuple-element.17.slot_ref) | copy-start | bytes 49156
  53.0 13.1 %copy-start = (f32[32,160,128]{2,1,0:T(8,128)}, f32[32,160,128]{2,1,0:T(8,128)S(1)}, u32[]{:S(2)}) copy-start(f32[32,160,128]{2,1,0:T(8,128)S(1)} %all-to-all-done) | copy-start | bytes 7864324
  53.0 3.4 %copy-start.1 = (f32[64,5,32,128]{3,2,1,0:T(8,128)S(1)}, f32[64,5,32,128]{3,2,1,0:T(8,128)}, u32[]{:S(2)}) copy-start(f32[64,5,32,128]{3,2,1,0:T(8,128)} %get-tuple-element.20._) | copy-start | bytes 15728644
  56.4 2.5 %copy-start.3 = (f32[32,5,4,8,256]{4,3,2,1,0:T(8,128)S(1)}, f32[32,5,4,8,256]{4,3,2,1,0:T(8,128)}, u32[]{:S(2)}) copy-start(f32[32,5,4,8,256]{4,3,2,1,0:T(8,128)} %get-tuple-element.19.edge_ref) | copy-start | bytes 15728644
  66.1 2.3 %copy-start.2 = (f32[64,5,32,128]{3,2,1,0:T(8,128)}, f32[64,5,32,128]{3,2,1,0:T(8,128)S(1)}, u32[]{:S(2)}) copy-start(f32[64,5,32,128]{3,2,1,0:T(8,128)S(1)} %face_fluxes.1) | copy-start | bytes 15728644
  68.4 0.6 copy-start.9
  69.0 5.0 %copy-start.5 = (f32[32,32,128]{2,1,0:T(8,128)S(1)}, f32[32,32,128]{2,1,0:T(8,128)}, u32[]{:S(2)}) copy-start(f32[32,32,128]{2,1,0:T(8,128)} %param.12) | copy-start | bytes 1572868
  69.0 5.0 %copy-start.7 = (f32[4,48,128]{2,1,0:T(8,128)S(1)}, f32[4,48,128]{2,1,0:T(8,128)}, u32[]{:S(2)}) copy-start(f32[4,48,128]{2,1,0:T(8,128)} %rate_lookup.1.rate_ref) | copy-start | bytes 294916
  69.0 5.0 %copy-start.11 = (s32[8,128]{1,0:T(8,128)S(1)}, s32[8,128]{1,0:T(8,128)}, u32[]{:S(2)}) copy-start(s32[8,128]{1,0:T(8,128)} %get-tuple-element.16.corner_ref) | copy-start | bytes 12292
  69.0 70.8 %all-to-all-start.1 = ((f32[32,320,128]{2,1,0:T(8,128)}), f32[32,320,128]{2,1,0:T(8,128)}, u32[]{:S(2)}, u32[]{:S(2)}) async-start(f32[32,320,128]{2,1,0:T(8,128)} %bitcast.31), calls=%async_computation.1 | async-start | bytes 10485760 | tf_op jit(solution)/shard_map/all_to_all | solution.py:699
  74.1 1.4 copy-start.4
  75.5 1.0 copy-start.6
  76.5 0.9 copy-start.10

commit v3 on v2

--- a/solution.py
+++ b/solution.py
@@ -373,32 +373,33 @@
 
 def patch_update(prim_refs, p_index, rates_at, faces, emit, on_plane=None):
     row = lax.broadcasted_iota(jnp.int32, (8, 256), 0)
-
-    def plane(i):
-        return [f[p_index, 8 * i : 8 * i + 8, :] for f in prim_refs]
-
-    prim = plane(0)
-    if on_plane is not None:
-        on_plane(0, prim)
-    here = derive(prim)
-    below = None if faces is None else [faces(c, 0, slice(0, 8)) for c in range(5)]
-    for i in range(8):
+    cells, fluxes, x_flux = {}, {}, {}
+    x_flux[-1] = None if faces is None else [faces(c, 0, slice(0, 8)) for c in range(5)]
+    x_flux[7] = None if faces is None else [faces(c, 1, slice(0, 8)) for c in range(5)]
+
+    def enter(i):
+        prim = [f[p_index, 8 * i : 8 * i + 8, :] for f in prim_refs]
+        if on_plane is not None:
+            on_plane(i, prim)
+        here = derive(prim)
+        cells[i] = (here, shifted(here, 7, 0), shifted(here, 255, 1), rates_at(i))
+
+    def cross(i):
+        here, y_next, z_next, _ = cells[i]
+        y_flux = twice_flux(directed(here, 1), directed(y_next, 1))
+        z_flux = twice_flux(directed(here, 2), directed(z_next, 2))
+        y_back = [pltpu.roll(v, 1, 0) for v in y_flux]
+        z_back = [pltpu.roll(v, 1, 1) for v in z_flux]
+        fluxes[i] = (y_flux, y_back, z_flux, z_back)
         if i < 7:
-            prim = plane(i + 1)
-            if on_plane is not None:
-                on_plane(i + 1, prim)
-            after = derive(prim)
-            above = None
+            x_flux[i] = None
             if faces is not None or i % 2 == 1:
-                above = twice_flux(directed(here, 0), directed(after, 0))
-        else:
-            after = None
-            above = None if faces is None else [faces(c, 1, slice(0, 8)) for c in range(5)]
-        y_here = directed(here, 1)
-        y_flux = twice_flux(y_here, directed(shifted(here, 7, 0), 1))
-        z_here = directed(here, 2)
-        z_flux = twice_flux(z_here, directed(shifted(here, 255, 1), 2))
-        gain = source_term(here["amounts"][0], here["share"], rates_at(i))
+                x_flux[i] = twice_flux(directed(here, 0), directed(cells[i + 1][0], 0))
+
+    def leave(i):
+        here, _, _, rates = cells.pop(i)
+        y_flux, y_back, z_flux, z_back = fluxes.pop(i)
+        gain = source_term(here["amounts"][0], here["share"], rates)
         result = []
         for c in range(5):
             if faces is None:
@@ -407,19 +408,27 @@
                 y_high = jnp.broadcast_to(faces(c, 3, slice(i, i + 1)), (8, 256))
                 y_low = jnp.broadcast_to(faces(c, 2, slice(i, i + 1)), (8, 256))
             change = jnp.where(row == 7, y_high, y_flux[c]) - jnp.where(
-                row == 0, y_low, pltpu.roll(y_flux[c], 1, 0)
+                row == 0, y_low, y_back[c]
             )
-            change = change + (z_flux[c] - pltpu.roll(z_flux[c], 1, 1))
-            if above is not None:
-                change = change + above[c]
-            if below is not None:
-                change = change - below[c]
+            change = change + (z_flux[c] - z_back[c])
+            if x_flux[i] is not None:
+                change = change + x_flux[i][c]
+            if x_flux[i - 1] is not None:
+                change = change - x_flux[i - 1][c]
             value = here["amounts"][c] - STEP * change
             if c == 4:
                 value = value + gain
             result.append(value)
         emit(i, result)
-        here, below = after, above
+
+    enter(0)
+    for i in range(9):
+        if i < 7:
+            enter(i + 1)
+        if i < 8:
+            cross(i)
+        if i > 0:
+            leave(i - 1)
 
 
 def rates_reader(rate_ref, patch):
@@ -526,38 +535,71 @@
     return sides
 
 
-def face_kernel(slot_ref, rim_ref, edge_ref, _, sum_ref, ghost_ref):
-    first = pl.program_id(0) * BATCH
-    for n in range(BATCH):
-        slot = slot_ref[first + n, 0]
-        sides = side_fluxes(
-            [rim_ref[slot, c] for c in range(5)],
-            lambda side, n=n: [edge_ref[n, c, side] for c in range(5)],
-            ghost_ref.at[n],
-        )
-        for c in range(5):
-            for d in range(2):
-                value = fold(sides[2 * d][c], sides[2 * d + 1][c])
-                sum_ref[slot, c, 8 * d : 8 * d + 8, :] = (0.125 * STEP) * value
+def face_kernel(
+    slot_ref, rim_ref, edge_hbm, _, out_hbm, edge_ref, sum_ref, ghost_ref, edge_sem, sum_sem
+):
+    count = edge_ref.shape[0]
+
+    def load(g):
+        part = pl.ds(g * BATCH, BATCH)
+        return pltpu.make_async_copy(edge_hbm.at[part], edge_ref.at[part], edge_sem.at[g])
+
+    def save(p):
+        place = out_hbm.at[slot_ref[p, 0], :, pl.ds(16, 16), :]
+        return pltpu.make_async_copy(sum_ref.at[p], place, sum_sem.at[p])
+
+    for g in range(count // BATCH):
+        load(g).start()
+
+    def chunk(g, carry):
+        load(g).wait()
+        for n in range(BATCH):
+            p = g * BATCH + n
+            slot = slot_ref[p, 0]
+            sides = side_fluxes(
+                [rim_ref[slot, c] for c in range(5)],
+                lambda side, p=p: [edge_ref[p, c, side] for c in range(5)],
+                ghost_ref.at[n],
+            )
+            for c in range(5):
+                for d in range(2):
+                    value = fold(sides[2 * d][c], sides[2 * d + 1][c])
+                    sum_ref[p, c, 8 * d : 8 * d + 8, :] = (0.125 * STEP) * value
+        for n in range(BATCH):
+            save(g * BATCH + n).start()
+        return carry
+
+    lax.fori_loop(0, count // BATCH, chunk, 0)
+
+    def settle(p, carry):
+        save(p).wait()
+        return carry
+
+    lax.fori_loop(0, count, settle, 0)
 
 
 def face_fluxes(slot, rims, edges, buffer):
     count = edges.shape[0]
-    slots = rims.shape[0]
+    anywhere = pl.BlockSpec(memory_space=pl.ANY)
     return pl.pallas_call(
         face_kernel,
-        grid=(count // BATCH,),
         out_shape=jax.ShapeDtypeStruct(buffer.shape, F32),
         in_specs=[
             pl.BlockSpec(memory_space=SMEM),
-            pl.BlockSpec((slots, 5, 16, 128), lambda i: (0, 0, 0, 0)),
-            pl.BlockSpec((BATCH, 5, 4, 8, 256), lambda i: (i, 0, 0, 0, 0)),
-            pl.BlockSpec(memory_space=pl.ANY),
+            pl.BlockSpec(memory_space=VMEM),
+            anywhere,
+            anywhere,
         ],
-        out_specs=pl.BlockSpec((slots, 5, 16, 128), lambda i: (0, 0, 1, 0)),
+        out_specs=anywhere,
         input_output_aliases={3: 0},
-        scratch_shapes=[pltpu.VMEM((BATCH, 6, 2, 32, 128), F32)],
-        compiler_params=pltpu.CompilerParams(vmem_limit_bytes=20 * MIB),
+        scratch_shapes=[
+            pltpu.VMEM(edges.shape, F32),
+            pltpu.VMEM((count, 5, 16, 128), F32),
+            pltpu.VMEM((BATCH, 6, 2, 32, 128), F32),
+            pltpu.SemaphoreType.DMA((count // BATCH,)),
+            pltpu.SemaphoreType.DMA((count,)),
+        ],
+        compiler_params=pltpu.CompilerParams(vmem_limit_bytes=58 * MIB),
         cost_estimate=pl.CostEstimate(
             flops=100 * count * 32 * 256, bytes_accessed=11 * MIB, transcendentals=0
         ),
@@ -613,7 +655,7 @@
             pltpu.VMEM((6, 2, 32, 128), F32),
             pltpu.VMEM((5, 2, 8, 256), F32),
         ],
-        compiler_params=pltpu.CompilerParams(vmem_limit_bytes=GRANT),
+        compiler_params=pltpu.CompilerParams(vmem_limit_bytes=20 * MIB),
         cost_estimate=pl.CostEstimate(
             flops=250 * count * 64 * 256, bytes_accessed=29 * MIB, transcendentals=0
         ),
@@ -623,16 +665,11 @@
 
 def merge_kernel(corner_ref, base_ref, got_ref, out_ref):
     width = 32
-    count = got_ref.shape[0]
-
-    @pl.when(pl.program_id(0) == 0)
-    def _():
-        out_ref[...] = base_ref[...]
-
+    out_ref[...] = base_ref[...]
     row = lax.broadcasted_iota(jnp.int32, (4, 128), 0)
 
     def one(s, carry):
-        base = corner_at(corner_ref, pl.program_id(0) * count + s)
+        base = corner_at(corner_ref, s)
 
         @pl.when(base >= 0)
         def _():
@@ -671,21 +708,15 @@
 
         return carry
 
-    lax.fori_loop(0, count, one, 0)
+    lax.fori_loop(0, got_ref.shape[0], one, 0)
 
 
 def merge(corners, base, got):
-    slots = got.shape[0]
-    whole = pl.BlockSpec(base.shape, lambda i: (0, 0, 0))
+    whole = pl.BlockSpec(memory_space=VMEM)
     return pl.pallas_call(
         merge_kernel,
-        grid=(4,),
         out_shape=jax.ShapeDtypeStruct(base.shape, F32),
-        in_specs=[
-            pl.BlockSpec(memory_space=SMEM),
-            whole,
-            pl.BlockSpec((slots // 4, 5, 32, 128), lambda i: (i, 0, 0, 0)),
-        ],
+        in_specs=[pl.BlockSpec(memory_space=SMEM), whole, whole],
         out_specs=whole,
         compiler_params=pltpu.CompilerParams(vmem_limit_bytes=24 * MIB),
         cost_estimate=pl.CostEstimate(flops=MIB, bytes_accessed=11 * MIB, transcendentals=0),

time: 147 us -> 143 us (0.973)
  Pallas kernels: 83.9 us -> 81.6 us
  waiting for transfers between devices: 25.5 us -> 23.2 us
    pallas_call x1, Pallas kernels: 26.3 us -> 21.7 us  [close_patches(): pl.pallas_call(close_kernel, grid=(count // PER,), out_shape=jax.ShapeDty...]
    pallas_call x2, Pallas kernels: 13.9 us -> 17.2 us  [the longest x1 9.92 us: face_fluxes(): pl.pallas_call(face_kernel, out_shape=jax.ShapeDtypeStruct(buffer.shape,...]
    all_to_all x2, waiting for transfers between devices: 25.5 us -> 23.2 us  [exchange(): lax.all_to_all(buffer.reshape(groups, rows, 128), 'yz', split_axis=0, con...]
    unnamed x42 -> x46, local copies, waits for them, and re-layouts: 12.9 us -> 13 us
where the time goes in v3:
time: 143 us; the launch traced here: 142 us
  Pallas kernels  81.6 us (57%)
  waiting for transfers between devices  23.2 us (16%)
  starting transfers between devices  21.8 us (15%)
  local copies, waits for them, and re-layouts  13.3 us (9%)
    pallas_call x1, Pallas kernels, open_patches(): pl.pallas_call(open_kernel, grid=(count // PER,), out_shape=[jax.ShapeDty...  24.1 us
    all_to_all x2, waiting for transfers between devices, exchange(): lax.all_to_all(buffer.reshape(groups, rows, 128), 'yz', split_axis=0, con...  23.2 us
    pallas_call x1, Pallas kernels, close_patches(): pl.pallas_call(close_kernel, grid=(count // PER,), out_shape=jax.ShapeDty...  21.7 us
    unnamed x46, local copies, waits for them, and re-layouts  13 us
    all_to_all x2, starting transfers between devices, exchange(): lax.all_to_all(buffer.reshape(groups, rows, 128), 'yz', split_axis=0, con...  12.6 us
    pallas_call x1, Pallas kernels, coarse_step(): pl.pallas_call(coarse_kernel, out_shape=jax.ShapeDtypeStruct((5, cells, 1...  10.6 us
    pallas_call x1, Pallas kernels, face_fluxes(): pl.pallas_call(face_kernel, out_shape=jax.ShapeDtypeStruct(buffer.shape,...  9.92 us
    pallas_call x1, Pallas kernels, merge(): pl.pallas_call(merge_kernel, out_shape=jax.ShapeDtypeStruct(base.shape, F...  7.3 us
  transfers between devices with their start and end apart: 6, of which 1 were waited for; matrix products, arithmetic and copies ran while one was open for 1% of the time, Pallas kernels for 48%

profile of v3, /device:TPU:0, one launch (start us, length us, event | category | flops | bytes accessed | tf_op | source)
XLA Modules:
  0.0 142.1 jit_solution(14501211582194584616)
XLA Ops:
  0.6 0.6 pad_add_fusion.1.place_ref
  1.2 6.1 %pack_rims.1 = (f32[64,5,16,128]{3,2,1,0:T(8,128)}, f32[5,32,128]{2,1,0:T(8,128)}, f32[5,32,128]{2,1,0:T(8,128)}, f32[5,32,128]{2,1,0:T(8,128)}, f32[5,32,128]{2...) custom-call(s32[2]{0:T(128)} %pad_add_fusion.1.place_ref, s32[32,128]{1,0:T(8,128)} %bitcast.54, s32[32,128]{1,0:T(8,128)} %bitcast.55, ...), custom_call_target="tpu_custom_call" | custom-call | bytes 6291456 | tf_op jit(solution)/shard_map/pack_rims/pallas_call | solution.py:175
  7.3 0.0 copy-start.20
  7.3 0.0 copy-start.15
  7.3 0.0 copy-start.16
  7.3 0.0 copy-start.17
  7.4 0.0 copy-start.14
  7.4 7.5 %all-to-all-start = ((f32[32,160,128]{2,1,0:T(8,128)}), f32[32,160,128]{2,1,0:T(8,128)S(1)}, u32[]{:S(2)}, u32[]{:S(2)}) async-start(f32[32,160,128]{2,1,0:T(8,128)} %bitcast.49), calls=%async_computation | async-start | bytes 5242880 | tf_op jit(solution)/shard_map/all_to_all | solution.py:730
  14.9 2.0 %collective-permute-start = (f32[5,32,128]{2,1,0:T(8,128)S(1)}, f32[5,32,128]{2,1,0:T(8,128)S(1)}, u32[]{:S(2)}, u32[]{:S(2)}) collective-permute-start(f32[5,32,128]{2,1,0:T(8,128)S(1)} %copy-done.21), channel_id=1, source_target_pairs={{0,32},{32,64},{64,96},{96,0},{1,33},{33,65},{65,97},{97,1},{2,34}... | collective-permute-start | bytes 245768 | tf_op jit(solution)/shard_map/ppermute | solution.py:771
  16.9 2.2 %collective-permute-start.1 = (f32[5,32,128]{2,1,0:T(8,128)S(1)}, f32[5,32,128]{2,1,0:T(8,128)S(1)}, u32[]{:S(2)}, u32[]{:S(2)}) collective-permute-start(f32[5,32,128]{2,1,0:T(8,128)S(1)} %copy-done.20), channel_id=1, source_target_pairs={{32,0},{64,32},{96,64},{0,96},{33,1},{65,33},{97,65},{1,97},{34,2}... | collective-permute-start | bytes 245768 | tf_op jit(solution)/shard_map/ppermute | solution.py:772
  19.1 0.0 collective-permute-start.2
  19.1 5.1 %collective-permute-start.3 = (f32[5,32,128]{2,1,0:T(8,128)S(1)}, f32[5,32,128]{2,1,0:T(8,128)S(1)}, u32[]{:S(2)}, u32[]{:S(2)}) collective-permute-start(f32[5,32,128]{2,1,0:T(8,128)S(1)} %copy-done.18), channel_id=1, source_target_pairs={{1,0},{2,1},{3,2},{4,3},{5,4},{6,5},{7,6},{8,7},{9,8},{10,9},{11,1... | collective-permute-start | bytes 245768 | tf_op jit(solution)/shard_map/ppermute | solution.py:774
  24.2 0.0 copy-done.15
  24.2 0.1 copy.18
  24.3 0.0 copy-done.17
  24.3 0.6 copy.21
  24.9 0.1 reshape.65
  25.0 0.1 copy.17
  25.1 0.1 reshape.66
  25.2 0.6 pad_add_fusion.bins_ref
  25.8 1.9 %rate_lookup.1.rate_ref = f32[4,48,128]{2,1,0:T(8,128)} custom-call(s32[48,128]{1,0:T(8,128)} %pad_add_fusion.bins_ref, f32[2,16,128]{2,1,0:T(8,128)} %bitcast.52), custom_call_target="tpu_custom_call" | custom-call | flops 1048576 | bytes 1048576 | tf_op jit(solution)/shard_map/rate_lookup/pallas_call | solution.py:217
  27.7 24.1 %open_patches.1 = (f32[64,5,32,128]{3,2,1,0:T(8,128)}, f32[32,5,4,8,256]{4,3,2,1,0:T(8,128)}) custom-call(s32[32,128]{1,0:T(8,128)} %get-tuple-element.17.slot_ref, f32[32,64,256]{2,1,0:T(8,128)} %bitcast.37, f32[3,32,64,256]{3,2,1,0:T(8,128)} %bitcast.29, f32[3,32,64,256]{3,2,1,0:T(8,128)} %bitcast.30, f32[3,32,64,256]{3,2,1,0:T(8,128)} %bitcast.31, ...), custom_call_target="tpu_custom_call" | custom-call | flops 131072000 | bytes 18874368 | tf_op jit(solution)/shard_map/open_patches/pallas_call | solution.py:491
  51.9 0.0 all-to-all-done
  51.9 0.0 copy-start.1
  51.9 1.5 %copy-done.1 = f32[32,160,128]{2,1,0:T(8,128)} copy-done((f32[32,160,128]{2,1,0:T(8,128)}, f32[32,160,128]{2,1,0:T(8,128)S(1)}, u32[]{:S(2)}) %copy-start.1) | copy-done | bytes 2621464
  53.4 9.9 %face_fluxes.1 = f32[64,5,32,128]{3,2,1,0:T(8,128)} custom-call(s32[32,128]{1,0:T(8,128)} %get-tuple-element.17.slot_ref, f32[64,5,16,128]{3,2,1,0:T(8,128)} %bitcast.35, f32[32,5,4,8,256]{4,3,2,1,0:T(8,128)} %get-tuple-element.19.edge_hbm.edge_ref, f32[64,5,32,128]{3,2,1,0:T(8,128)} %get-tuple-element.20._), custom_call_target="tpu_custom_call", output_to_operand_aliasing={{}: (3, {})} | custom-call | flops 26214400 | bytes 11534336 | tf_op jit(solution)/shard_map/face_fluxes/pallas_call | solution.py:584
  63.3 0.0 collective-permute-done.xlo_ref
  63.3 0.0 collective-permute-done.1.xhi_ref
  63.3 0.0 collective-permute-done.2.ylo_ref
  63.3 0.0 collective-permute-done.3.yhi_ref
  63.3 0.0 copy-start.11
  63.4 0.6 copy-done.11
  64.0 5.0 %all-to-all-start.1 = ((f32[32,320,128]{2,1,0:T(8,128)}), f32[32,320,128]{2,1,0:T(8,128)}, u32[]{:S(2)}, u32[]{:S(2)}) async-start(f32[32,320,128]{2,1,0:T(8,128)} %bitcast.47), calls=%async_computation.1 | async-start | bytes 10485760 | tf_op jit(solution)/shard_map/all_to_all | solution.py:730
  69.0 0.0 copy-start.6
  69.0 1.4 copy-done.6
  70.4 1.0 copy-done.8
  71.5 0.9 copy-done.12
  72.4 10.6 %coarse_step.1.base_ref = f32[5,1024,128]{2,1,0:T(8,128)S(1)} custom-call(s32[8,128]{1,0:T(8,128)S(1)} %copy-done.13, f32[1024,128]{1,0:T(8,128)S(1)} %bitcast.44, f32[3,1024,128]{2,1,0:T(8,128)S(1)} %bitcast.42, f32[1024,128]{1,0:T(8,128)S(1)} %bitcast.46, f32[5,32,128]{2,1,0:T(8,128)S(1)} %collective-permute-done.xlo_ref, ...), custom_call_target="tpu_custom_call" | custom-call | flops 39321600 | bytes 31457280 | tf_op jit(solution)/shard_map/coarse_step/pallas_call | solution.py:338
  83.0 0.0 copy-done.2
  83.0 0.0 copy-done.4
  83.0 0.0 copy-done.10
  83.0 0.0 copy-start
  83.0 2.8 %copy-done = f32[3,32,8,8,256]{4,3,2,1,0:T(8,128)S(1)} copy-done((f32[3,32,8,8,256]{4,3,2,1,0:T(8,128)S(1)}, f32[3,32,8,8,256]{4,3,2,1,0:T(8,128)}, u32[]{:S(2)}) %copy-start) | copy-done | bytes 6291480
  85.8 2.5 %copy-done.3 = f32[32,5,4,8,256]{4,3,2,1,0:T(8,128)S(1)} copy-done((f32[32,5,4,8,256]{4,3,2,1,0:T(8,128)S(1)}, f32[32,5,4,8,256]{4,3,2,1,0:T(8,128)}, u32[]{:S(2)}) %copy-start.3) | copy-done | bytes 5242904
  88.3 1.6 %copy-done.5 = f32[32,8,8,256]{3,2,1,0:T(8,128)S(1)} copy-done((f32[32,8,8,256]{3,2,1,0:T(8,128)S(1)}, f32[32,8,8,256]{3,2,1,0:T(8,128)}, u32[]{:S(2)}) %copy-start.5) | copy-done | bytes 2097176
  89.9 21.7 %close_patches.1 = f32[5,32,64,256]{3,2,1,0:T(8,128)} custom-call(s32[32,128]{1,0:T(8,128)S(1)} %copy-done.10, f32[32,64,256]{2,1,0:T(8,128)S(1)} %bitcast.38, f32[3,32,64,256]{3,2,1,0:T(8,128)S(1)} %bitcast.32, f32[3,32,64,256]{3,2,1,0:T(8,128)S(1)} %bitcast.33, f32[3,32,64,256]{3,2,1,0:T(8,128)S(1)} %bitcast.34, f32[32,64,256]{2,1,0:T(8,128)S(1)} %bitcast.40, ...), custom_call_target="tpu_custom_call" | custom-call | flops 131072000 | bytes 30408704 | tf_op jit(solution)/shard_map/close_patches/pallas_call | solution.py:643
  111.6 23.2 %all-to-all-done.1 = f32[32,320,128]{2,1,0:T(8,128)} async-done(((f32[32,320,128]{2,1,0:T(8,128)}), f32[32,320,128]{2,1,0:T(8,128)}, u32[]{:S(2)}, u32[]{:S(2)}) %all-to-all-start.1) | async-done | bytes 5242912 | tf_op jit(solution)/shard_map/all_to_all | solution.py:730
  134.8 7.3 %merge_patches.1 = f32[5,1024,128]{2,1,0:T(8,128)} custom-call(s32[8,128]{1,0:T(8,128)S(1)} %copy-done.13, f32[5,1024,128]{2,1,0:T(8,128)S(1)} %coarse_step.1.base_ref, f32[64,5,32,128]{3,2,1,0:T(8,128)} %bitcast.17.got_ref), custom_call_target="tpu_custom_call" | custom-call | flops 1048576 | bytes 11534336 | tf_op jit(solution)/shard_map/merge_patches/pallas_call | solution.py:716
  (23 shorter events, 0.1 us)
Async XLA Ops:
  7.3 7.6 %copy-start.21 = (f32[5,32,128]{2,1,0:T(8,128)S(1)}, f32[5,32,128]{2,1,0:T(8,128)}, u32[]{:S(2)}) copy-start(f32[5,32,128]{2,1,0:T(8,128)} %get-tuple-element.21) | copy-start | bytes 245764
  7.3 9.6 %copy-start.20 = (f32[5,32,128]{2,1,0:T(8,128)S(1)}, f32[5,32,128]{2,1,0:T(8,128)}, u32[]{:S(2)}) copy-start(f32[5,32,128]{2,1,0:T(8,128)} %get-tuple-element.22) | copy-start | bytes 245764
  7.3 11.8 %copy-start.19 = (f32[5,32,128]{2,1,0:T(8,128)S(1)}, f32[5,32,128]{2,1,0:T(8,128)}, u32[]{:S(2)}) copy-start(f32[5,32,128]{2,1,0:T(8,128)} %get-tuple-element.23) | copy-start | bytes 245764
  7.3 11.8 %copy-start.18 = (f32[5,32,128]{2,1,0:T(8,128)S(1)}, f32[5,32,128]{2,1,0:T(8,128)}, u32[]{:S(2)}) copy-start(f32[5,32,128]{2,1,0:T(8,128)} %get-tuple-element.24) | copy-start | bytes 245764
  7.3 16.9 %copy-start.15 = (s32[32,32]{1,0:T(8,128)S(1)}, s32[32,32]{1,0:T(8,128)}, u32[]{:S(2)}) copy-start(s32[32,32]{1,0:T(8,128)} %param.15) | copy-start | bytes 12292
  7.3 16.9 %copy-start.16 = (f32[2000]{0:T(1024)S(1)}, f32[2000]{0:T(1024)}, u32[]{:S(2)}) copy-start(f32[2000]{0:T(1024)} %param.23) | copy-start | bytes 24004
  7.3 16.9 %copy-start.17 = (f32[2000]{0:T(1024)S(1)}, f32[2000]{0:T(1024)}, u32[]{:S(2)}) copy-start(f32[2000]{0:T(1024)} %param.22) | copy-start | bytes 24004
  7.4 17.5 %copy-start.14 = (s32[32,8,8]{0,2,1:T(8,128)S(1)}, s32[32,8,8]{0,2,1:T(8,128)}, u32[]{:S(2)}) copy-start(s32[32,8,8]{0,2,1:T(8,128)} %param.19) | copy-start | bytes 24580
  7.4 44.5 %all-to-all-start = ((f32[32,160,128]{2,1,0:T(8,128)}), f32[32,160,128]{2,1,0:T(8,128)S(1)}, u32[]{:S(2)}, u32[]{:S(2)}) async-start(f32[32,160,128]{2,1,0:T(8,128)} %bitcast.49), calls=%async_computation | async-start | bytes 5242880 | tf_op jit(solution)/shard_map/all_to_all | solution.py:730
  14.9 48.4 %collective-permute-start = (f32[5,32,128]{2,1,0:T(8,128)S(1)}, f32[5,32,128]{2,1,0:T(8,128)S(1)}, u32[]{:S(2)}, u32[]{:S(2)}) collective-permute-start(f32[5,32,128]{2,1,0:T(8,128)S(1)} %copy-done.21), channel_id=1, source_target_pairs={{0,32},{32,64},{64,96},{96,0},{1,33},{33,65},{65,97},{97,1},{2,34}... | collective-permute-start | bytes 245768 | tf_op jit(solution)/shard_map/ppermute | solution.py:771
  16.9 46.4 %collective-permute-start.1 = (f32[5,32,128]{2,1,0:T(8,128)S(1)}, f32[5,32,128]{2,1,0:T(8,128)S(1)}, u32[]{:S(2)}, u32[]{:S(2)}) collective-permute-start(f32[5,32,128]{2,1,0:T(8,128)S(1)} %copy-done.20), channel_id=1, source_target_pairs={{32,0},{64,32},{96,64},{0,96},{33,1},{65,33},{97,65},{1,97},{34,2}... | collective-permute-start | bytes 245768 | tf_op jit(solution)/shard_map/ppermute | solution.py:772
  19.1 44.2 %collective-permute-start.2 = (f32[5,32,128]{2,1,0:T(8,128)S(1)}, f32[5,32,128]{2,1,0:T(8,128)S(1)}, u32[]{:S(2)}, u32[]{:S(2)}) collective-permute-start(f32[5,32,128]{2,1,0:T(8,128)S(1)} %copy-done.19), channel_id=1, source_target_pairs={{0,1},{1,2},{2,3},{3,4},{4,5},{5,6},{6,7},{7,8},{8,9},{9,10},{10,1... | collective-permute-start | bytes 245768 | tf_op jit(solution)/shard_map/ppermute | solution.py:773
  19.1 44.2 %collective-permute-start.3 = (f32[5,32,128]{2,1,0:T(8,128)S(1)}, f32[5,32,128]{2,1,0:T(8,128)S(1)}, u32[]{:S(2)}, u32[]{:S(2)}) collective-permute-start(f32[5,32,128]{2,1,0:T(8,128)S(1)} %copy-done.18), channel_id=1, source_target_pairs={{1,0},{2,1},{3,2},{4,3},{5,4},{6,5},{7,6},{8,7},{9,8},{10,9},{11,1... | collective-permute-start | bytes 245768 | tf_op jit(solution)/shard_map/ppermute | solution.py:774
  51.9 1.5 %copy-start.1 = (f32[32,160,128]{2,1,0:T(8,128)}, f32[32,160,128]{2,1,0:T(8,128)S(1)}, u32[]{:S(2)}) copy-start(f32[32,160,128]{2,1,0:T(8,128)S(1)} %all-to-all-done) | copy-start | bytes 7864324
  63.3 0.6 copy-start.11
  64.0 5.0 %copy-start.7 = (f32[32,32,128]{2,1,0:T(8,128)S(1)}, f32[32,32,128]{2,1,0:T(8,128)}, u32[]{:S(2)}) copy-start(f32[32,32,128]{2,1,0:T(8,128)} %param.12) | copy-start | bytes 1572868
  64.0 5.0 %copy-start.9 = (f32[4,48,128]{2,1,0:T(8,128)S(1)}, f32[4,48,128]{2,1,0:T(8,128)}, u32[]{:S(2)}) copy-start(f32[4,48,128]{2,1,0:T(8,128)} %rate_lookup.1.rate_ref) | copy-start | bytes 294916
  64.0 5.0 %copy-start.13 = (s32[8,128]{1,0:T(8,128)S(1)}, s32[8,128]{1,0:T(8,128)}, u32[]{:S(2)}) copy-start(s32[8,128]{1,0:T(8,128)} %get-tuple-element.16.corner_ref) | copy-start | bytes 12292
  64.0 70.8 %all-to-all-start.1 = ((f32[32,320,128]{2,1,0:T(8,128)}), f32[32,320,128]{2,1,0:T(8,128)}, u32[]{:S(2)}, u32[]{:S(2)}) async-start(f32[32,320,128]{2,1,0:T(8,128)} %bitcast.47), calls=%async_computation.1 | async-start | bytes 10485760 | tf_op jit(solution)/shard_map/all_to_all | solution.py:730
  69.0 1.4 copy-start.6
  70.4 1.0 copy-start.8
  71.5 0.9 copy-start.12
  72.4 10.6 %copy-start.2 = (f32[32,160,128]{2,1,0:T(8,128)S(1)}, f32[32,160,128]{2,1,0:T(8,128)}, u32[]{:S(2)}) copy-start(f32[32,160,128]{2,1,0:T(8,128)} %copy-done.1) | copy-start | bytes 7864324
  72.4 10.6 %copy-start.4 = (f32[32,8,8,256]{3,2,1,0:T(8,128)S(1)}, f32[32,8,8,256]{3,2,1,0:T(8,128)}, u32[]{:S(2)}) copy-start(f32[32,8,8,256]{3,2,1,0:T(8,128)} %param.16) | copy-start | bytes 6291460
  72.4 10.6 %copy-start.10 = (s32[32,128]{1,0:T(8,128)S(1)}, s32[32,128]{1,0:T(8,128)}, u32[]{:S(2)}) copy-start(s32[32,128]{1,0:T(8,128)} %get-tuple-element.17.slot_ref) | copy-start | bytes 49156
  83.0 2.8 %copy-start = (f32[3,32,8,8,256]{4,3,2,1,0:T(8,128)S(1)}, f32[3,32,8,8,256]{4,3,2,1,0:T(8,128)}, u32[]{:S(2)}) copy-start(f32[3,32,8,8,256]{4,3,2,1,0:T(8,128)} %param.17) | copy-start | bytes 18874372
  85.8 2.5 %copy-start.3 = (f32[32,5,4,8,256]{4,3,2,1,0:T(8,128)S(1)}, f32[32,5,4,8,256]{4,3,2,1,0:T(8,128)}, u32[]{:S(2)}) copy-start(f32[32,5,4,8,256]{4,3,2,1,0:T(8,128)} %get-tuple-element.19.edge_hbm.edge_ref) | copy-start | bytes 15728644
  88.3 1.6 %copy-start.5 = (f32[32,8,8,256]{3,2,1,0:T(8,128)S(1)}, f32[32,8,8,256]{3,2,1,0:T(8,128)}, u32[]{:S(2)}) copy-start(f32[32,8,8,256]{3,2,1,0:T(8,128)} %param.18) | copy-start | bytes 6291460

commit v4 on v3

--- a/solution.py
+++ b/solution.py
@@ -536,7 +536,8 @@
 
 
 def face_kernel(
-    slot_ref, rim_ref, edge_hbm, _, out_hbm, edge_ref, sum_ref, ghost_ref, edge_sem, sum_sem
+    slot_ref, rim_hbm, edge_hbm, _, out_hbm,
+    rim_ref, edge_ref, sum_ref, ghost_ref, rim_sem, edge_sem, sum_sem,
 ):
     count = edge_ref.shape[0]
 
@@ -548,16 +549,22 @@
         place = out_hbm.at[slot_ref[p, 0], :, pl.ds(16, 16), :]
         return pltpu.make_async_copy(sum_ref.at[p], place, sum_sem.at[p])
 
+    def fetch(p):
+        return pltpu.make_async_copy(rim_hbm.at[slot_ref[p, 0]], rim_ref.at[p], rim_sem.at[p])
+
     for g in range(count // BATCH):
         load(g).start()
+        for n in range(BATCH):
+            fetch(g * BATCH + n).start()
 
     def chunk(g, carry):
         load(g).wait()
         for n in range(BATCH):
+            fetch(g * BATCH + n).wait()
+        for n in range(BATCH):
             p = g * BATCH + n
-            slot = slot_ref[p, 0]
             sides = side_fluxes(
-                [rim_ref[slot, c] for c in range(5)],
+                [rim_ref[p, c] for c in range(5)],
                 lambda side, p=p: [edge_ref[p, c, side] for c in range(5)],
                 ghost_ref.at[n],
             )
@@ -586,20 +593,22 @@
         out_shape=jax.ShapeDtypeStruct(buffer.shape, F32),
         in_specs=[
             pl.BlockSpec(memory_space=SMEM),
-            pl.BlockSpec(memory_space=VMEM),
+            anywhere,
             anywhere,
             anywhere,
         ],
         out_specs=anywhere,
         input_output_aliases={3: 0},
         scratch_shapes=[
+            pltpu.VMEM((count, 5, 16, 128), F32),
             pltpu.VMEM(edges.shape, F32),
             pltpu.VMEM((count, 5, 16, 128), F32),
             pltpu.VMEM((BATCH, 6, 2, 32, 128), F32),
+            pltpu.SemaphoreType.DMA((count,)),
             pltpu.SemaphoreType.DMA((count // BATCH,)),
             pltpu.SemaphoreType.DMA((count,)),
         ],
-        compiler_params=pltpu.CompilerParams(vmem_limit_bytes=58 * MIB),
+        compiler_params=pltpu.CompilerParams(vmem_limit_bytes=62 * MIB),
         cost_estimate=pl.CostEstimate(
             flops=100 * count * 32 * 256, bytes_accessed=11 * MIB, transcendentals=0
         ),
@@ -663,8 +672,21 @@
     )(slot, rho, vel, vel, vel, p, rates, rims, edges)
 
 
-def merge_kernel(corner_ref, base_ref, got_ref, out_ref):
+CHUNKS = 4
+
+
+def merge_kernel(corner_ref, base_ref, got_hbm, out_ref, got_ref, sem):
     width = 32
+    slots = got_ref.shape[0]
+
+    size = slots // CHUNKS
+
+    def fetch(g):
+        part = pl.ds(g * size, size)
+        return pltpu.make_async_copy(got_hbm.at[part], got_ref.at[part], sem.at[g])
+
+    for g in range(CHUNKS):
+        fetch(g).start()
     out_ref[...] = base_ref[...]
     row = lax.broadcasted_iota(jnp.int32, (4, 128), 0)
 
@@ -708,7 +730,9 @@
 
         return carry
 
-    lax.fori_loop(0, got_ref.shape[0], one, 0)
+    for g in range(CHUNKS):
+        fetch(g).wait()
+        lax.fori_loop(g * size, (g + 1) * size, one, 0)
 
 
 def merge(corners, base, got):
@@ -716,8 +740,9 @@
     return pl.pallas_call(
         merge_kernel,
         out_shape=jax.ShapeDtypeStruct(base.shape, F32),
-        in_specs=[pl.BlockSpec(memory_space=SMEM), whole, whole],
+        in_specs=[pl.BlockSpec(memory_space=SMEM), whole, pl.BlockSpec(memory_space=pl.ANY)],
         out_specs=whole,
+        scratch_shapes=[pltpu.VMEM(got.shape, F32), pltpu.SemaphoreType.DMA((CHUNKS,))],
         compiler_params=pltpu.CompilerParams(vmem_limit_bytes=24 * MIB),
         cost_estimate=pl.CostEstimate(flops=MIB, bytes_accessed=11 * MIB, transcendentals=0),
         name="merge_patches",

time: 143 us -> 140 us (0.979)
  local copies, waits for them, and re-layouts: 13.3 us -> 10.9 us
    unnamed x46 -> x42, local copies, waits for them, and re-layouts: 13 us -> 10.6 us
  transfers between devices with their start and end apart: 6 -> 6, of which waited for: 1 -> 1; matrix products, arithmetic and copies ran while one was open for 1% -> 1% of each run, Pallas kernels for 48% -> 50%
where the time goes in v4:
time: 140 us
  Pallas kernels  82 us (59%)
  waiting for transfers between devices  23 us (16%)
  starting transfers between devices  21.7 us (16%)
  local copies, waits for them, and re-layouts  10.9 us (8%)
    pallas_call x1, Pallas kernels, open_patches(): pl.pallas_call(open_kernel, grid=(count // PER,), out_shape=[jax.ShapeDty...  24.1 us
    all_to_all x2, waiting for transfers between devices, exchange(): lax.all_to_all(buffer.reshape(groups, rows, 128), 'yz', split_axis=0, con...  23 us
    pallas_call x1, Pallas kernels, close_patches(): pl.pallas_call(close_kernel, grid=(count // PER,), out_shape=jax.ShapeDty...  22.7 us
    all_to_all x2, starting transfers between devices, exchange(): lax.all_to_all(buffer.reshape(groups, rows, 128), 'yz', split_axis=0, con...  12.4 us
    pallas_call x1, Pallas kernels, coarse_step(): pl.pallas_call(coarse_kernel, out_shape=jax.ShapeDtypeStruct((5, cells, 1...  10.7 us
    unnamed x42, local copies, waits for them, and re-layouts  10.6 us
    pallas_call x1, Pallas kernels, face_fluxes(): pl.pallas_call(face_kernel, out_shape=jax.ShapeDtypeStruct(buffer.shape,...  9.87 us
    pallas_call x1, Pallas kernels, merge(): pl.pallas_call(merge_kernel, out_shape=jax.ShapeDtypeStruct(base.shape, F...  6.64 us
  transfers between devices with their start and end apart: 6, of which 1 were waited for; matrix products, arithmetic and copies ran while one was open for 1% of the time, Pallas kernels for 50%

profile of v4, /device:TPU:0, one launch (start us, length us, event | category | flops | bytes accessed | tf_op | source)
XLA Modules:
  0.0 139.9 jit_solution(5685371940514774069)
XLA Ops:
  0.6 0.6 pad_add_fusion.1.place_ref
  1.2 6.1 %pack_rims.1 = (f32[64,5,16,128]{3,2,1,0:T(8,128)}, f32[5,32,128]{2,1,0:T(8,128)}, f32[5,32,128]{2,1,0:T(8,128)}, f32[5,32,128]{2,1,0:T(8,128)}, f32[5,32,128]{2...) custom-call(s32[2]{0:T(128)} %pad_add_fusion.1.place_ref, s32[32,128]{1,0:T(8,128)} %bitcast.52, s32[32,128]{1,0:T(8,128)} %bitcast.53, ...), custom_call_target="tpu_custom_call" | custom-call | bytes 6291456 | tf_op jit(solution)/shard_map/pack_rims/pallas_call | solution.py:175
  7.3 0.0 copy-start.19
  7.4 0.0 copy-start.18
  7.4 0.0 copy-start.17
  7.4 0.0 copy-start.13
  7.4 0.0 copy-start.14
  7.4 0.0 copy-start.15
  7.4 0.0 copy-start.12
  7.4 7.6 %all-to-all-start = ((f32[32,160,128]{2,1,0:T(8,128)}), f32[32,160,128]{2,1,0:T(8,128)}, u32[]{:S(2)}, u32[]{:S(2)}) async-start(f32[32,160,128]{2,1,0:T(8,128)} %bitcast.47), calls=%async_computation | async-start | bytes 5242880 | tf_op jit(solution)/shard_map/all_to_all | solution.py:755
  15.0 2.0 %collective-permute-start = (f32[5,32,128]{2,1,0:T(8,128)S(1)}, f32[5,32,128]{2,1,0:T(8,128)S(1)}, u32[]{:S(2)}, u32[]{:S(2)}) collective-permute-start(f32[5,32,128]{2,1,0:T(8,128)S(1)} %copy-done.19), channel_id=1, source_target_pairs={{0,32},{32,64},{64,96},{96,0},{1,33},{33,65},{65,97},{97,1},{2,34}... | collective-permute-start | bytes 245768 | tf_op jit(solution)/shard_map/ppermute | solution.py:796
  17.0 2.3 %collective-permute-start.1 = (f32[5,32,128]{2,1,0:T(8,128)S(1)}, f32[5,32,128]{2,1,0:T(8,128)S(1)}, u32[]{:S(2)}, u32[]{:S(2)}) collective-permute-start(f32[5,32,128]{2,1,0:T(8,128)S(1)} %copy-done.18), channel_id=1, source_target_pairs={{32,0},{64,32},{96,64},{0,96},{33,1},{65,33},{97,65},{1,97},{34,2}... | collective-permute-start | bytes 245768 | tf_op jit(solution)/shard_map/ppermute | solution.py:797
  19.3 0.0 copy-done.17
  19.3 0.0 collective-permute-start.2
  19.3 5.1 %collective-permute-start.3 = (f32[5,32,128]{2,1,0:T(8,128)S(1)}, f32[5,32,128]{2,1,0:T(8,128)S(1)}, u32[]{:S(2)}, u32[]{:S(2)}) collective-permute-start(f32[5,32,128]{2,1,0:T(8,128)S(1)} %copy-done.16), channel_id=1, source_target_pairs={{1,0},{2,1},{3,2},{4,3},{5,4},{6,5},{7,6},{8,7},{9,8},{10,9},{11,1... | collective-permute-start | bytes 245768 | tf_op jit(solution)/shard_map/ppermute | solution.py:799
  24.3 0.1 copy.18
  24.4 0.6 copy.21
  25.0 0.1 reshape.65
  25.1 0.1 copy.17
  25.3 0.1 reshape.66
  25.4 0.6 pad_add_fusion.bins_ref
  26.0 1.9 %rate_lookup.1.rate_ref = f32[4,48,128]{2,1,0:T(8,128)} custom-call(s32[48,128]{1,0:T(8,128)} %pad_add_fusion.bins_ref, f32[2,16,128]{2,1,0:T(8,128)} %bitcast.50), custom_call_target="tpu_custom_call" | custom-call | flops 1048576 | bytes 1048576 | tf_op jit(solution)/shard_map/rate_lookup/pallas_call | solution.py:217
  27.9 24.1 %open_patches.1 = (f32[64,5,32,128]{3,2,1,0:T(8,128)}, f32[32,5,4,8,256]{4,3,2,1,0:T(8,128)}) custom-call(s32[32,128]{1,0:T(8,128)} %get-tuple-element.17.slot_ref, f32[32,64,256]{2,1,0:T(8,128)} %bitcast.35, f32[3,32,64,256]{3,2,1,0:T(8,128)} %bitcast.29, f32[3,32,64,256]{3,2,1,0:T(8,128)} %bitcast.30, f32[3,32,64,256]{3,2,1,0:T(8,128)} %bitcast.31, ...), custom_call_target="tpu_custom_call" | custom-call | flops 131072000 | bytes 18874368 | tf_op jit(solution)/shard_map/open_patches/pallas_call | solution.py:491
  52.0 0.0 all-to-all-done
  52.0 9.9 %face_fluxes.1 = f32[64,5,32,128]{3,2,1,0:T(8,128)} custom-call(s32[32,128]{1,0:T(8,128)} %get-tuple-element.17.slot_ref, f32[64,5,16,128]{3,2,1,0:T(8,128)} %bitcast.8.rim_hbm.rim_ref, f32[32,5,4,8,256]{4,3,2,1,0:T(8,128)} %get-tuple-element.19.edge_hbm.edge_ref, f32[64,5,32,128]{3,2,1,0:T(8,128)} %get-tuple-element.20._), custom_call_target="tpu_custom_call", output_to_operand_aliasing={{}: (3, {})} | custom-call | flops 26214400 | bytes 11534336 | tf_op jit(solution)/shard_map/face_fluxes/pallas_call | solution.py:591
  61.9 0.0 collective-permute-done.xlo_ref
  61.9 0.0 collective-permute-done.1.xhi_ref
  61.9 0.0 collective-permute-done.2.ylo_ref
  61.9 0.0 collective-permute-done.3.yhi_ref
  61.9 0.0 copy-start.9
  62.0 0.0 copy-start.5
  62.0 0.6 copy-done.9
  62.6 4.9 %all-to-all-start.1 = ((f32[32,320,128]{2,1,0:T(8,128)}), f32[32,320,128]{2,1,0:T(8,128)}, u32[]{:S(2)}, u32[]{:S(2)}) async-start(f32[32,320,128]{2,1,0:T(8,128)} %bitcast.45), calls=%async_computation.1 | async-start | bytes 10485760 | tf_op jit(solution)/shard_map/all_to_all | solution.py:755
  67.5 0.0 copy-done.5
  67.5 0.0 copy-done.7
  67.5 0.0 copy-done.11
  67.5 0.0 copy-start.4
  67.5 1.4 %copy-done.4 = f32[3,32,32,128]{3,2,1,0:T(8,128)S(1)} copy-done((f32[3,32,32,128]{3,2,1,0:T(8,128)S(1)}, f32[3,32,32,128]{3,2,1,0:T(8,128)}, u32[]{:S(2)}) %copy-start.4) | copy-done | bytes 1572888
  68.9 1.0 copy-done.6
  69.9 0.9 copy-done.10
  70.8 10.7 %coarse_step.1.base_ref = f32[5,1024,128]{2,1,0:T(8,128)S(1)} custom-call(s32[8,128]{1,0:T(8,128)S(1)} %copy-done.11, f32[1024,128]{1,0:T(8,128)S(1)} %bitcast.42, f32[3,1024,128]{2,1,0:T(8,128)S(1)} %bitcast.40, f32[1024,128]{1,0:T(8,128)S(1)} %bitcast.44, f32[5,32,128]{2,1,0:T(8,128)S(1)} %collective-permute-done.xlo_ref, ...), custom_call_target="tpu_custom_call" | custom-call | flops 39321600 | bytes 31457280 | tf_op jit(solution)/shard_map/coarse_step/pallas_call | solution.py:338
  81.5 0.0 copy-start
  81.6 2.8 %copy-done = f32[3,32,8,8,256]{4,3,2,1,0:T(8,128)S(1)} copy-done((f32[3,32,8,8,256]{4,3,2,1,0:T(8,128)S(1)}, f32[3,32,8,8,256]{4,3,2,1,0:T(8,128)}, u32[]{:S(2)}) %copy-start) | copy-done | bytes 6291480
  84.3 1.6 %copy-done.2 = f32[32,8,8,256]{3,2,1,0:T(8,128)S(1)} copy-done((f32[32,8,8,256]{3,2,1,0:T(8,128)S(1)}, f32[32,8,8,256]{3,2,1,0:T(8,128)}, u32[]{:S(2)}) %copy-start.2) | copy-done | bytes 2097176
  85.9 1.6 %copy-done.3 = f32[32,8,8,256]{3,2,1,0:T(8,128)S(1)} copy-done((f32[32,8,8,256]{3,2,1,0:T(8,128)S(1)}, f32[32,8,8,256]{3,2,1,0:T(8,128)}, u32[]{:S(2)}) %copy-start.3) | copy-done | bytes 2097176
  87.5 22.7 %close_patches.1 = f32[5,32,64,256]{3,2,1,0:T(8,128)} custom-call(s32[32,128]{1,0:T(8,128)S(1)} %copy-done.8, f32[32,64,256]{2,1,0:T(8,128)S(1)} %bitcast.36, f32[3,32,64,256]{3,2,1,0:T(8,128)S(1)} %bitcast.32, f32[3,32,64,256]{3,2,1,0:T(8,128)S(1)} %bitcast.33, f32[3,32,64,256]{3,2,1,0:T(8,128)S(1)} %bitcast.34, f32[32,64,256]{2,1,0:T(8,128)S(1)} %bitcast.38, ...), custom_call_target="tpu_custom_call" | custom-call | flops 131072000 | bytes 30408704 | tf_op jit(solution)/shard_map/close_patches/pallas_call | solution.py:652
  110.2 23.0 %all-to-all-done.1 = f32[32,320,128]{2,1,0:T(8,128)} async-done(((f32[32,320,128]{2,1,0:T(8,128)}), f32[32,320,128]{2,1,0:T(8,128)}, u32[]{:S(2)}, u32[]{:S(2)}) %all-to-all-start.1) | async-done | bytes 5242912 | tf_op jit(solution)/shard_map/all_to_all | solution.py:755
  133.2 6.6 %merge_patches.1 = f32[5,1024,128]{2,1,0:T(8,128)} custom-call(s32[8,128]{1,0:T(8,128)S(1)} %copy-done.11, f32[5,1024,128]{2,1,0:T(8,128)S(1)} %coarse_step.1.base_ref, f32[64,5,32,128]{3,2,1,0:T(8,128)} %bitcast.17.got_hbm), custom_call_target="tpu_custom_call" | custom-call | flops 1048576 | bytes 11534336 | tf_op jit(solution)/shard_map/merge_patches/pallas_call | solution.py:740
  (19 shorter events, 0.1 us)
Async XLA Ops:
  7.3 7.7 %copy-start.19 = (f32[5,32,128]{2,1,0:T(8,128)S(1)}, f32[5,32,128]{2,1,0:T(8,128)}, u32[]{:S(2)}) copy-start(f32[5,32,128]{2,1,0:T(8,128)} %get-tuple-element.21) | copy-start | bytes 245764
  7.4 9.6 %copy-start.18 = (f32[5,32,128]{2,1,0:T(8,128)S(1)}, f32[5,32,128]{2,1,0:T(8,128)}, u32[]{:S(2)}) copy-start(f32[5,32,128]{2,1,0:T(8,128)} %get-tuple-element.22) | copy-start | bytes 245764
  7.4 11.9 %copy-start.17 = (f32[5,32,128]{2,1,0:T(8,128)S(1)}, f32[5,32,128]{2,1,0:T(8,128)}, u32[]{:S(2)}) copy-start(f32[5,32,128]{2,1,0:T(8,128)} %get-tuple-element.23) | copy-start | bytes 245764
  7.4 11.9 %copy-start.16 = (f32[5,32,128]{2,1,0:T(8,128)S(1)}, f32[5,32,128]{2,1,0:T(8,128)}, u32[]{:S(2)}) copy-start(f32[5,32,128]{2,1,0:T(8,128)} %get-tuple-element.24) | copy-start | bytes 245764
  7.4 16.9 %copy-start.13 = (s32[32,32]{1,0:T(8,128)S(1)}, s32[32,32]{1,0:T(8,128)}, u32[]{:S(2)}) copy-start(s32[32,32]{1,0:T(8,128)} %param.15) | copy-start | bytes 12292
  7.4 17.0 %copy-start.14 = (f32[2000]{0:T(1024)S(1)}, f32[2000]{0:T(1024)}, u32[]{:S(2)}) copy-start(f32[2000]{0:T(1024)} %param.23) | copy-start | bytes 24004
  7.4 17.0 %copy-start.15 = (f32[2000]{0:T(1024)S(1)}, f32[2000]{0:T(1024)}, u32[]{:S(2)}) copy-start(f32[2000]{0:T(1024)} %param.22) | copy-start | bytes 24004
  7.4 17.6 %copy-start.12 = (s32[32,8,8]{0,2,1:T(8,128)S(1)}, s32[32,8,8]{0,2,1:T(8,128)}, u32[]{:S(2)}) copy-start(s32[32,8,8]{0,2,1:T(8,128)} %param.19) | copy-start | bytes 24580
  7.4 44.6 %all-to-all-start = ((f32[32,160,128]{2,1,0:T(8,128)}), f32[32,160,128]{2,1,0:T(8,128)}, u32[]{:S(2)}, u32[]{:S(2)}) async-start(f32[32,160,128]{2,1,0:T(8,128)} %bitcast.47), calls=%async_computation | async-start | bytes 5242880 | tf_op jit(solution)/shard_map/all_to_all | solution.py:755
  15.0 46.9 %collective-permute-start = (f32[5,32,128]{2,1,0:T(8,128)S(1)}, f32[5,32,128]{2,1,0:T(8,128)S(1)}, u32[]{:S(2)}, u32[]{:S(2)}) collective-permute-start(f32[5,32,128]{2,1,0:T(8,128)S(1)} %copy-done.19), channel_id=1, source_target_pairs={{0,32},{32,64},{64,96},{96,0},{1,33},{33,65},{65,97},{97,1},{2,34}... | collective-permute-start | bytes 245768 | tf_op jit(solution)/shard_map/ppermute | solution.py:796
  17.0 44.9 %collective-permute-start.1 = (f32[5,32,128]{2,1,0:T(8,128)S(1)}, f32[5,32,128]{2,1,0:T(8,128)S(1)}, u32[]{:S(2)}, u32[]{:S(2)}) collective-permute-start(f32[5,32,128]{2,1,0:T(8,128)S(1)} %copy-done.18), channel_id=1, source_target_pairs={{32,0},{64,32},{96,64},{0,96},{33,1},{65,33},{97,65},{1,97},{34,2}... | collective-permute-start | bytes 245768 | tf_op jit(solution)/shard_map/ppermute | solution.py:797
  19.3 42.7 %collective-permute-start.2 = (f32[5,32,128]{2,1,0:T(8,128)S(1)}, f32[5,32,128]{2,1,0:T(8,128)S(1)}, u32[]{:S(2)}, u32[]{:S(2)}) collective-permute-start(f32[5,32,128]{2,1,0:T(8,128)S(1)} %copy-done.17), channel_id=1, source_target_pairs={{0,1},{1,2},{2,3},{3,4},{4,5},{5,6},{6,7},{7,8},{8,9},{9,10},{10,1... | collective-permute-start | bytes 245768 | tf_op jit(solution)/shard_map/ppermute | solution.py:798
  19.3 42.7 %collective-permute-start.3 = (f32[5,32,128]{2,1,0:T(8,128)S(1)}, f32[5,32,128]{2,1,0:T(8,128)S(1)}, u32[]{:S(2)}, u32[]{:S(2)}) collective-permute-start(f32[5,32,128]{2,1,0:T(8,128)S(1)} %copy-done.16), channel_id=1, source_target_pairs={{1,0},{2,1},{3,2},{4,3},{5,4},{6,5},{7,6},{8,7},{9,8},{10,9},{11,1... | collective-permute-start | bytes 245768 | tf_op jit(solution)/shard_map/ppermute | solution.py:799
  61.9 0.6 copy-start.9
  62.0 5.5 %copy-start.5 = (f32[32,32,128]{2,1,0:T(8,128)S(1)}, f32[32,32,128]{2,1,0:T(8,128)}, u32[]{:S(2)}) copy-start(f32[32,32,128]{2,1,0:T(8,128)} %param.12) | copy-start | bytes 1572868
  62.0 5.5 %copy-start.7 = (f32[4,48,128]{2,1,0:T(8,128)S(1)}, f32[4,48,128]{2,1,0:T(8,128)}, u32[]{:S(2)}) copy-start(f32[4,48,128]{2,1,0:T(8,128)} %rate_lookup.1.rate_ref) | copy-start | bytes 294916
  62.0 5.5 %copy-start.11 = (s32[8,128]{1,0:T(8,128)S(1)}, s32[8,128]{1,0:T(8,128)}, u32[]{:S(2)}) copy-start(s32[8,128]{1,0:T(8,128)} %get-tuple-element.16.corner_ref) | copy-start | bytes 12292
  62.6 70.6 %all-to-all-start.1 = ((f32[32,320,128]{2,1,0:T(8,128)}), f32[32,320,128]{2,1,0:T(8,128)}, u32[]{:S(2)}, u32[]{:S(2)}) async-start(f32[32,320,128]{2,1,0:T(8,128)} %bitcast.45), calls=%async_computation.1 | async-start | bytes 10485760 | tf_op jit(solution)/shard_map/all_to_all | solution.py:755
  67.5 1.4 %copy-start.4 = (f32[3,32,32,128]{3,2,1,0:T(8,128)S(1)}, f32[3,32,32,128]{3,2,1,0:T(8,128)}, u32[]{:S(2)}) copy-start(f32[3,32,32,128]{3,2,1,0:T(8,128)} %param.13) | copy-start | bytes 4718596
  68.9 1.0 copy-start.6
  69.9 0.9 copy-start.10
  70.8 10.7 %copy-start.1 = (f32[32,5,4,8,256]{4,3,2,1,0:T(8,128)S(1)}, f32[32,5,4,8,256]{4,3,2,1,0:T(8,128)}, u32[]{:S(2)}) copy-start(f32[32,5,4,8,256]{4,3,2,1,0:T(8,128)} %get-tuple-element.19.edge_hbm.edge_ref) | copy-start | bytes 15728644
  70.8 10.7 %copy-start.8 = (s32[32,128]{1,0:T(8,128)S(1)}, s32[32,128]{1,0:T(8,128)}, u32[]{:S(2)}) copy-start(s32[32,128]{1,0:T(8,128)} %get-tuple-element.17.slot_ref) | copy-start | bytes 49156
  81.5 2.8 %copy-start = (f32[3,32,8,8,256]{4,3,2,1,0:T(8,128)S(1)}, f32[3,32,8,8,256]{4,3,2,1,0:T(8,128)}, u32[]{:S(2)}) copy-start(f32[3,32,8,8,256]{4,3,2,1,0:T(8,128)} %param.17) | copy-start | bytes 18874372
  84.3 1.6 %copy-start.2 = (f32[32,8,8,256]{3,2,1,0:T(8,128)S(1)}, f32[32,8,8,256]{3,2,1,0:T(8,128)}, u32[]{:S(2)}) copy-start(f32[32,8,8,256]{3,2,1,0:T(8,128)} %param.16) | copy-start | bytes 6291460
  85.9 1.6 %copy-start.3 = (f32[32,8,8,256]{3,2,1,0:T(8,128)S(1)}, f32[32,8,8,256]{3,2,1,0:T(8,128)}, u32[]{:S(2)}) copy-start(f32[32,8,8,256]{3,2,1,0:T(8,128)} %param.18) | copy-start | bytes 6291460

commit v5 on v4

--- a/solution.py
+++ b/solution.py
@@ -793,8 +793,6 @@
     down_x = [((i + 1) % rows, i) for i in range(rows)]
     up_y = [(i, (i + 1) % groups) for i in range(groups)]
     down_y = [((i + 1) % groups, i) for i in range(groups)]
-    x_low = lax.ppermute(x_last, "gx", up_x)
-    x_high = lax.ppermute(x_first, "gx", down_x)
     y_low = lax.ppermute(y_last, "yz", up_y)
     y_high = lax.ppermute(y_first, "yz", down_y)
 
@@ -808,12 +806,13 @@
     f_press = fine_pressure.reshape(count, 64, 256)
     means, edges = open_patches(slot, f_rho, f_vel, f_press, rates, slots)
     sums = face_fluxes(slot, arrived, edges, means)
-    sums, x_low, x_high, y_low, y_high = lax.optimization_barrier(
-        (sums, x_low, x_high, y_low, y_high)
-    )
+    sums, y_low, y_high = lax.optimization_barrier((sums, y_low, y_high))
     got = exchange(sums, groups)
+    fine_new = close_patches(slot, f_rho, f_vel, f_press, rates, arrived, edges)
+    fine_new, x_first, x_last = lax.optimization_barrier((fine_new, x_first, x_last))
+    x_low = lax.ppermute(x_last, "gx", up_x)
+    x_high = lax.ppermute(x_first, "gx", down_x)
     base = coarse_step(corners, rho, vel, press, x_low, x_high, y_low, y_high, rates)
-    fine_new = close_patches(slot, f_rho, f_vel, f_press, rates, arrived, edges)
     coarse_new = merge(corners, base, got)
     return (
         coarse_new.reshape((5,) + coarse_density.shape),

time: 140 us -> 139 us (level)
  local copies, waits for them, and re-layouts: 10.9 us -> 7.92 us
  waiting for transfers between devices: 23 us -> 24.5 us
    unnamed x42 -> x38, local copies, waits for them, and re-layouts: 10.6 us -> 7.61 us
    ppermute x1, waiting for transfers between devices: 0.01 us -> 2.63 us  [local(): x_low = lax.ppermute(x_last, 'gx', up_x)]
  transfers between devices with their start and end apart: 6 -> 6, of which waited for: 1 -> 3; matrix products, arithmetic and copies ran while one was open for 1% -> 1% of each run, Pallas kernels for 50% -> 50%
where the time goes in v5:
time: 139 us; the launch traced here: 138 us
  Pallas kernels  82 us (59%)
  waiting for transfers between devices  24.5 us (18%)
  starting transfers between devices  21.9 us (16%)
  local copies, waits for them, and re-layouts  7.92 us (6%)
    pallas_call x1, Pallas kernels, open_patches(): pl.pallas_call(open_kernel, grid=(count // PER,), out_shape=[jax.ShapeDty...  24.1 us
    pallas_call x1, Pallas kernels, close_patches(): pl.pallas_call(close_kernel, grid=(count // PER,), out_shape=jax.ShapeDty...  22.9 us
    all_to_all x2, waiting for transfers between devices, exchange(): lax.all_to_all(buffer.reshape(groups, rows, 128), 'yz', split_axis=0, con...  21.8 us
    all_to_all x2, starting transfers between devices, exchange(): lax.all_to_all(buffer.reshape(groups, rows, 128), 'yz', split_axis=0, con...  12.7 us
    pallas_call x1, Pallas kernels, coarse_step(): pl.pallas_call(coarse_kernel, out_shape=jax.ShapeDtypeStruct((5, cells, 1...  10.6 us
    pallas_call x1, Pallas kernels, face_fluxes(): pl.pallas_call(face_kernel, out_shape=jax.ShapeDtypeStruct(buffer.shape,...  9.85 us
    unnamed x38, local copies, waits for them, and re-layouts  7.61 us
    pallas_call x1, Pallas kernels, merge(): pl.pallas_call(merge_kernel, out_shape=jax.ShapeDtypeStruct(base.shape, F...  6.55 us
  transfers between devices with their start and end apart: 6, of which 3 were waited for; matrix products, arithmetic and copies ran while one was open for 1% of the time, Pallas kernels for 50%

profile of v5, /device:TPU:0, one launch (start us, length us, event | category | flops | bytes accessed | tf_op | source)
XLA Modules:
  0.0 138.4 jit_solution(3351327315725474157)
XLA Ops:
  0.6 0.6 pad_add_fusion.1.place_ref
  1.2 6.1 %pack_rims.1 = (f32[64,5,16,128]{3,2,1,0:T(8,128)}, f32[5,32,128]{2,1,0:T(8,128)}, f32[5,32,128]{2,1,0:T(8,128)}, f32[5,32,128]{2,1,0:T(8,128)}, f32[5,32,128]{2...) custom-call(s32[2]{0:T(128)} %pad_add_fusion.1.place_ref, s32[32,128]{1,0:T(8,128)} %bitcast.52, s32[32,128]{1,0:T(8,128)} %bitcast.53, ...), custom_call_target="tpu_custom_call" | custom-call | bytes 6291456 | tf_op jit(solution)/shard_map/pack_rims/pallas_call | solution.py:175
  7.3 0.0 copy-start.17
  7.3 0.0 copy-start.16
  7.3 0.0 copy-start.11
  7.3 0.0 copy-start.12
  7.3 0.0 copy-start.13
  7.4 0.0 copy-start.10
  7.4 7.6 %all-to-all-start = ((f32[32,160,128]{2,1,0:T(8,128)}), f32[32,160,128]{2,1,0:T(8,128)}, u32[]{:S(2)}, u32[]{:S(2)}) async-start(f32[32,160,128]{2,1,0:T(8,128)} %bitcast.47), calls=%async_computation | async-start | bytes 5242880 | tf_op jit(solution)/shard_map/all_to_all | solution.py:755
  15.0 0.0 copy-done.17
  15.0 0.3 collective-permute-start.2
  15.3 0.0 copy-done.16
  15.3 4.9 %collective-permute-start.3 = (f32[5,32,128]{2,1,0:T(8,128)S(1)}, f32[5,32,128]{2,1,0:T(8,128)S(1)}, u32[]{:S(2)}, u32[]{:S(2)}) collective-permute-start(f32[5,32,128]{2,1,0:T(8,128)S(1)} %copy-done.16), channel_id=1, source_target_pairs={{1,0},{2,1},{3,2},{4,3},{5,4},{6,5},{7,6},{8,7},{9,8},{10,9},{11,1... | collective-permute-start | bytes 245768 | tf_op jit(solution)/shard_map/ppermute | solution.py:797
  20.2 0.0 copy-done.11
  20.2 0.1 copy.18
  20.2 0.0 copy-done.12
  20.2 0.0 copy-done.13
  20.3 0.6 copy.21
  20.9 0.0 copy-done.10
  20.9 0.1 reshape.63
  21.0 0.1 copy.17
  21.1 0.1 reshape.64
  21.2 0.6 pad_add_fusion.bins_ref
  21.8 1.9 %rate_lookup.1.rate_ref = f32[4,48,128]{2,1,0:T(8,128)} custom-call(s32[48,128]{1,0:T(8,128)} %pad_add_fusion.bins_ref, f32[2,16,128]{2,1,0:T(8,128)} %bitcast.50), custom_call_target="tpu_custom_call" | custom-call | flops 1048576 | bytes 1048576 | tf_op jit(solution)/shard_map/rate_lookup/pallas_call | solution.py:217
  23.7 24.1 %open_patches.1 = (f32[64,5,32,128]{3,2,1,0:T(8,128)}, f32[32,5,4,8,256]{4,3,2,1,0:T(8,128)}) custom-call(s32[32,128]{1,0:T(8,128)} %get-tuple-element.18.slot_ref, f32[32,64,256]{2,1,0:T(8,128)} %bitcast.35, f32[3,32,64,256]{3,2,1,0:T(8,128)} %bitcast.29, f32[3,32,64,256]{3,2,1,0:T(8,128)} %bitcast.30, f32[3,32,64,256]{3,2,1,0:T(8,128)} %bitcast.31, ...), custom_call_target="tpu_custom_call" | custom-call | flops 131072000 | bytes 18874368 | tf_op jit(solution)/shard_map/open_patches/pallas_call | solution.py:491
  47.9 3.3 %all-to-all-done = f32[32,160,128]{2,1,0:T(8,128)} async-done(((f32[32,160,128]{2,1,0:T(8,128)}), f32[32,160,128]{2,1,0:T(8,128)}, u32[]{:S(2)}, u32[]{:S(2)}) %all-to-all-start) | async-done | bytes 2621472 | tf_op jit(solution)/shard_map/all_to_all | solution.py:755
  51.1 9.8 %face_fluxes.1 = f32[64,5,32,128]{3,2,1,0:T(8,128)} custom-call(s32[32,128]{1,0:T(8,128)} %get-tuple-element.18.slot_ref, f32[64,5,16,128]{3,2,1,0:T(8,128)} %bitcast.15.rim_ref.rim_hbm, f32[32,5,4,8,256]{4,3,2,1,0:T(8,128)} %get-tuple-element.20.edge_ref.edge_hbm, f32[64,5,32,128]{3,2,1,0:T(8,128)} %get-tuple-element.25._), custom_call_target="tpu_custom_call", output_to_operand_aliasing={{}: (3, {})} | custom-call | flops 26214400 | bytes 11534336 | tf_op jit(solution)/shard_map/face_fluxes/pallas_call | solution.py:591
  61.0 0.0 collective-permute-done.2.ylo_ref
  61.0 0.0 collective-permute-done.3.yhi_ref
  61.0 0.0 copy-start.2
  61.0 0.0 copy-start.7
  61.0 0.0 copy-start.8
  61.1 5.0 %all-to-all-start.1 = ((f32[32,320,128]{2,1,0:T(8,128)}), f32[32,320,128]{2,1,0:T(8,128)}, u32[]{:S(2)}, u32[]{:S(2)}) async-start(f32[32,320,128]{2,1,0:T(8,128)} %bitcast.45), calls=%async_computation.1 | async-start | bytes 10485760 | tf_op jit(solution)/shard_map/all_to_all | solution.py:755
  66.1 0.0 copy-done.2
  66.1 0.0 copy-done.7
  66.1 0.0 copy-start
  66.1 2.8 %copy-done = f32[3,32,8,8,256]{4,3,2,1,0:T(8,128)S(1)} copy-done((f32[3,32,8,8,256]{4,3,2,1,0:T(8,128)S(1)}, f32[3,32,8,8,256]{4,3,2,1,0:T(8,128)}, u32[]{:S(2)}) %copy-start) | copy-done | bytes 6291480
  68.9 2.5 %copy-done.1 = f32[32,5,4,8,256]{4,3,2,1,0:T(8,128)S(1)} copy-done((f32[32,5,4,8,256]{4,3,2,1,0:T(8,128)S(1)}, f32[32,5,4,8,256]{4,3,2,1,0:T(8,128)}, u32[]{:S(2)}) %copy-start.1) | copy-done | bytes 5242904
  71.4 1.6 %copy-done.3 = f32[32,8,8,256]{3,2,1,0:T(8,128)S(1)} copy-done((f32[32,8,8,256]{3,2,1,0:T(8,128)S(1)}, f32[32,8,8,256]{3,2,1,0:T(8,128)}, u32[]{:S(2)}) %copy-start.3) | copy-done | bytes 2097176
  73.0 0.0 copy-start.6
  73.0 22.9 %close_patches.1 = f32[5,32,64,256]{3,2,1,0:T(8,128)} custom-call(s32[32,128]{1,0:T(8,128)S(1)} %copy-done.8, f32[32,64,256]{2,1,0:T(8,128)S(1)} %bitcast.36, f32[3,32,64,256]{3,2,1,0:T(8,128)S(1)} %bitcast.32, f32[3,32,64,256]{3,2,1,0:T(8,128)S(1)} %bitcast.33, f32[3,32,64,256]{3,2,1,0:T(8,128)S(1)} %bitcast.34, f32[32,64,256]{2,1,0:T(8,128)S(1)} %bitcast.38, ...), custom_call_target="tpu_custom_call" | custom-call | flops 131072000 | bytes 30408704 | tf_op jit(solution)/shard_map/close_patches/pallas_call | solution.py:652
  95.9 1.9 %collective-permute-start = (f32[5,32,128]{2,1,0:T(8,128)S(1)}, f32[5,32,128]{2,1,0:T(8,128)S(1)}, u32[]{:S(2)}, u32[]{:S(2)}) collective-permute-start(f32[5,32,128]{2,1,0:T(8,128)S(1)} %copy-done.15), channel_id=1, source_target_pairs={{0,32},{32,64},{64,96},{96,0},{1,33},{33,65},{65,97},{97,1},{2,34}... | collective-permute-start | bytes 245768 | tf_op jit(solution)/shard_map/ppermute | solution.py:813
  97.8 2.2 %collective-permute-start.1 = (f32[5,32,128]{2,1,0:T(8,128)S(1)}, f32[5,32,128]{2,1,0:T(8,128)S(1)}, u32[]{:S(2)}, u32[]{:S(2)}) collective-permute-start(f32[5,32,128]{2,1,0:T(8,128)S(1)} %copy-done.14), channel_id=1, source_target_pairs={{32,0},{64,32},{96,64},{0,96},{33,1},{65,33},{97,65},{1,97},{34,2}... | collective-permute-start | bytes 245768 | tf_op jit(solution)/shard_map/ppermute | solution.py:814
  100.0 2.6 %collective-permute-done.xlo_ref = f32[5,32,128]{2,1,0:T(8,128)S(1)} collective-permute-done((f32[5,32,128]{2,1,0:T(8,128)S(1)}, f32[5,32,128]{2,1,0:T(8,128)S(1)}, u32[]{:S(2)}, u32[]{:S(2)}) %collective-permute-start) | collective-permute-done | bytes 81952 | tf_op jit(solution)/shard_map/ppermute | solution.py:813
  102.7 0.0 collective-permute-done.1.xhi_ref
  102.7 10.6 %coarse_step.1.base_ref = f32[5,1024,128]{2,1,0:T(8,128)S(1)} custom-call(s32[8,128]{1,0:T(8,128)S(1)} %copy-done.9, f32[1024,128]{1,0:T(8,128)S(1)} %bitcast.42, f32[3,1024,128]{2,1,0:T(8,128)S(1)} %bitcast.40, f32[1024,128]{1,0:T(8,128)S(1)} %bitcast.44, f32[5,32,128]{2,1,0:T(8,128)S(1)} %collective-permute-done.xlo_ref, ...), custom_call_target="tpu_custom_call" | custom-call | flops 39321600 | bytes 31457280 | tf_op jit(solution)/shard_map/coarse_step/pallas_call | solution.py:338
  113.3 18.6 %all-to-all-done.1 = f32[32,320,128]{2,1,0:T(8,128)} async-done(((f32[32,320,128]{2,1,0:T(8,128)}), f32[32,320,128]{2,1,0:T(8,128)}, u32[]{:S(2)}, u32[]{:S(2)}) %all-to-all-start.1) | async-done | bytes 5242912 | tf_op jit(solution)/shard_map/all_to_all | solution.py:755
  131.8 6.5 %merge_patches.1 = f32[5,1024,128]{2,1,0:T(8,128)} custom-call(s32[8,128]{1,0:T(8,128)S(1)} %copy-done.9, f32[5,1024,128]{2,1,0:T(8,128)S(1)} %coarse_step.1.base_ref, f32[64,5,32,128]{3,2,1,0:T(8,128)} %bitcast.17.got_hbm), custom_call_target="tpu_custom_call" | custom-call | flops 1048576 | bytes 11534336 | tf_op jit(solution)/shard_map/merge_patches/pallas_call | solution.py:740
  (15 shorter events, 0.0 us)
Async XLA Ops:
  7.3 7.7 %copy-start.17 = (f32[5,32,128]{2,1,0:T(8,128)S(1)}, f32[5,32,128]{2,1,0:T(8,128)}, u32[]{:S(2)}) copy-start(f32[5,32,128]{2,1,0:T(8,128)} %get-tuple-element.26) | copy-start | bytes 245764
  7.3 8.0 %copy-start.16 = (f32[5,32,128]{2,1,0:T(8,128)S(1)}, f32[5,32,128]{2,1,0:T(8,128)}, u32[]{:S(2)}) copy-start(f32[5,32,128]{2,1,0:T(8,128)} %get-tuple-element.27) | copy-start | bytes 245764
  7.3 12.9 %copy-start.11 = (s32[32,32]{1,0:T(8,128)S(1)}, s32[32,32]{1,0:T(8,128)}, u32[]{:S(2)}) copy-start(s32[32,32]{1,0:T(8,128)} %param.15) | copy-start | bytes 12292
  7.3 12.9 %copy-start.12 = (f32[2000]{0:T(1024)S(1)}, f32[2000]{0:T(1024)}, u32[]{:S(2)}) copy-start(f32[2000]{0:T(1024)} %param.23) | copy-start | bytes 24004
  7.3 12.9 %copy-start.13 = (f32[2000]{0:T(1024)S(1)}, f32[2000]{0:T(1024)}, u32[]{:S(2)}) copy-start(f32[2000]{0:T(1024)} %param.22) | copy-start | bytes 24004
  7.4 13.5 %copy-start.10 = (s32[32,8,8]{0,2,1:T(8,128)S(1)}, s32[32,8,8]{0,2,1:T(8,128)}, u32[]{:S(2)}) copy-start(s32[32,8,8]{0,2,1:T(8,128)} %param.19) | copy-start | bytes 24580
  7.4 43.8 %all-to-all-start = ((f32[32,160,128]{2,1,0:T(8,128)}), f32[32,160,128]{2,1,0:T(8,128)}, u32[]{:S(2)}, u32[]{:S(2)}) async-start(f32[32,160,128]{2,1,0:T(8,128)} %bitcast.47), calls=%async_computation | async-start | bytes 5242880 | tf_op jit(solution)/shard_map/all_to_all | solution.py:755
  15.0 46.0 %collective-permute-start.2 = (f32[5,32,128]{2,1,0:T(8,128)S(1)}, f32[5,32,128]{2,1,0:T(8,128)S(1)}, u32[]{:S(2)}, u32[]{:S(2)}) collective-permute-start(f32[5,32,128]{2,1,0:T(8,128)S(1)} %copy-done.17), channel_id=1, source_target_pairs={{0,1},{1,2},{2,3},{3,4},{4,5},{5,6},{6,7},{7,8},{8,9},{9,10},{10,1... | collective-permute-start | bytes 245768 | tf_op jit(solution)/shard_map/ppermute | solution.py:796
  15.3 45.7 %collective-permute-start.3 = (f32[5,32,128]{2,1,0:T(8,128)S(1)}, f32[5,32,128]{2,1,0:T(8,128)S(1)}, u32[]{:S(2)}, u32[]{:S(2)}) collective-permute-start(f32[5,32,128]{2,1,0:T(8,128)S(1)} %copy-done.16), channel_id=1, source_target_pairs={{1,0},{2,1},{3,2},{4,3},{5,4},{6,5},{7,6},{8,7},{9,8},{10,9},{11,1... | collective-permute-start | bytes 245768 | tf_op jit(solution)/shard_map/ppermute | solution.py:797
  61.0 5.1 %copy-start.2 = (f32[32,8,8,256]{3,2,1,0:T(8,128)S(1)}, f32[32,8,8,256]{3,2,1,0:T(8,128)}, u32[]{:S(2)}) copy-start(f32[32,8,8,256]{3,2,1,0:T(8,128)} %param.16) | copy-start | bytes 6291460
  61.0 5.1 %copy-start.7 = (f32[4,48,128]{2,1,0:T(8,128)S(1)}, f32[4,48,128]{2,1,0:T(8,128)}, u32[]{:S(2)}) copy-start(f32[4,48,128]{2,1,0:T(8,128)} %rate_lookup.1.rate_ref) | copy-start | bytes 294916
  61.0 5.1 %copy-start.8 = (s32[32,128]{1,0:T(8,128)S(1)}, s32[32,128]{1,0:T(8,128)}, u32[]{:S(2)}) copy-start(s32[32,128]{1,0:T(8,128)} %get-tuple-element.18.slot_ref) | copy-start | bytes 49156
  61.1 70.8 %all-to-all-start.1 = ((f32[32,320,128]{2,1,0:T(8,128)}), f32[32,320,128]{2,1,0:T(8,128)}, u32[]{:S(2)}, u32[]{:S(2)}) async-start(f32[32,320,128]{2,1,0:T(8,128)} %bitcast.45), calls=%async_computation.1 | async-start | bytes 10485760 | tf_op jit(solution)/shard_map/all_to_all | solution.py:755
  66.1 2.8 %copy-start = (f32[3,32,8,8,256]{4,3,2,1,0:T(8,128)S(1)}, f32[3,32,8,8,256]{4,3,2,1,0:T(8,128)}, u32[]{:S(2)}) copy-start(f32[3,32,8,8,256]{4,3,2,1,0:T(8,128)} %param.17) | copy-start | bytes 18874372
  68.9 2.5 %copy-start.1 = (f32[32,5,4,8,256]{4,3,2,1,0:T(8,128)S(1)}, f32[32,5,4,8,256]{4,3,2,1,0:T(8,128)}, u32[]{:S(2)}) copy-start(f32[32,5,4,8,256]{4,3,2,1,0:T(8,128)} %get-tuple-element.20.edge_ref.edge_hbm) | copy-start | bytes 15728644
  71.4 1.6 %copy-start.3 = (f32[32,8,8,256]{3,2,1,0:T(8,128)S(1)}, f32[32,8,8,256]{3,2,1,0:T(8,128)}, u32[]{:S(2)}) copy-start(f32[32,8,8,256]{3,2,1,0:T(8,128)} %param.18) | copy-start | bytes 6291460
  73.0 22.9 %copy-start.15 = (f32[5,32,128]{2,1,0:T(8,128)S(1)}, f32[5,32,128]{2,1,0:T(8,128)}, u32[]{:S(2)}) copy-start(f32[5,32,128]{2,1,0:T(8,128)} %get-tuple-element.23) | copy-start | bytes 245764
  73.0 24.8 %copy-start.14 = (f32[5,32,128]{2,1,0:T(8,128)S(1)}, f32[5,32,128]{2,1,0:T(8,128)}, u32[]{:S(2)}) copy-start(f32[5,32,128]{2,1,0:T(8,128)} %get-tuple-element.24) | copy-start | bytes 245764
  73.0 29.7 %copy-start.4 = (f32[3,32,32,128]{3,2,1,0:T(8,128)S(1)}, f32[3,32,32,128]{3,2,1,0:T(8,128)}, u32[]{:S(2)}) copy-start(f32[3,32,32,128]{3,2,1,0:T(8,128)} %param.13) | copy-start | bytes 4718596
  73.0 29.7 %copy-start.5 = (f32[32,32,128]{2,1,0:T(8,128)S(1)}, f32[32,32,128]{2,1,0:T(8,128)}, u32[]{:S(2)}) copy-start(f32[32,32,128]{2,1,0:T(8,128)} %param.12) | copy-start | bytes 1572868
  73.0 29.7 %copy-start.6 = (f32[32,32,128]{2,1,0:T(8,128)S(1)}, f32[32,32,128]{2,1,0:T(8,128)}, u32[]{:S(2)}) copy-start(f32[32,32,128]{2,1,0:T(8,128)} %param.14) | copy-start | bytes 1572868
  73.0 29.7 %copy-start.9 = (s32[8,128]{1,0:T(8,128)S(1)}, s32[8,128]{1,0:T(8,128)}, u32[]{:S(2)}) copy-start(s32[8,128]{1,0:T(8,128)} %get-tuple-element.17.corner_ref) | copy-start | bytes 12292
  95.9 6.8 %collective-permute-start = (f32[5,32,128]{2,1,0:T(8,128)S(1)}, f32[5,32,128]{2,1,0:T(8,128)S(1)}, u32[]{:S(2)}, u32[]{:S(2)}) collective-permute-start(f32[5,32,128]{2,1,0:T(8,128)S(1)} %copy-done.15), channel_id=1, source_target_pairs={{0,32},{32,64},{64,96},{96,0},{1,33},{33,65},{65,97},{97,1},{2,34}... | collective-permute-start | bytes 245768 | tf_op jit(solution)/shard_map/ppermute | solution.py:813
  97.8 4.8 %collective-permute-start.1 = (f32[5,32,128]{2,1,0:T(8,128)S(1)}, f32[5,32,128]{2,1,0:T(8,128)S(1)}, u32[]{:S(2)}, u32[]{:S(2)}) collective-permute-start(f32[5,32,128]{2,1,0:T(8,128)S(1)} %copy-done.14), channel_id=1, source_target_pairs={{32,0},{64,32},{96,64},{0,96},{33,1},{65,33},{97,65},{1,97},{34,2}... | collective-permute-start | bytes 245768 | tf_op jit(solution)/shard_map/ppermute | solution.py:814

commit v6 on v5

--- a/solution.py
+++ b/solution.py
@@ -536,14 +536,9 @@
 
 
 def face_kernel(
-    slot_ref, rim_hbm, edge_hbm, _, out_hbm,
-    rim_ref, edge_ref, sum_ref, ghost_ref, rim_sem, edge_sem, sum_sem,
+    slot_ref, rim_hbm, edge_ref, _, out_hbm, rim_ref, sum_ref, ghost_ref, rim_sem, sum_sem
 ):
     count = edge_ref.shape[0]
-
-    def load(g):
-        part = pl.ds(g * BATCH, BATCH)
-        return pltpu.make_async_copy(edge_hbm.at[part], edge_ref.at[part], edge_sem.at[g])
 
     def save(p):
         place = out_hbm.at[slot_ref[p, 0], :, pl.ds(16, 16), :]
@@ -552,13 +547,10 @@
     def fetch(p):
         return pltpu.make_async_copy(rim_hbm.at[slot_ref[p, 0]], rim_ref.at[p], rim_sem.at[p])
 
-    for g in range(count // BATCH):
-        load(g).start()
-        for n in range(BATCH):
-            fetch(g * BATCH + n).start()
+    for p in range(count):
+        fetch(p).start()
 
     def chunk(g, carry):
-        load(g).wait()
         for n in range(BATCH):
             fetch(g * BATCH + n).wait()
         for n in range(BATCH):
@@ -594,21 +586,19 @@
         in_specs=[
             pl.BlockSpec(memory_space=SMEM),
             anywhere,
-            anywhere,
+            pl.BlockSpec(memory_space=VMEM),
             anywhere,
         ],
         out_specs=anywhere,
         input_output_aliases={3: 0},
         scratch_shapes=[
             pltpu.VMEM((count, 5, 16, 128), F32),
-            pltpu.VMEM(edges.shape, F32),
             pltpu.VMEM((count, 5, 16, 128), F32),
             pltpu.VMEM((BATCH, 6, 2, 32, 128), F32),
             pltpu.SemaphoreType.DMA((count,)),
-            pltpu.SemaphoreType.DMA((count // BATCH,)),
             pltpu.SemaphoreType.DMA((count,)),
         ],
-        compiler_params=pltpu.CompilerParams(vmem_limit_bytes=62 * MIB),
+        compiler_params=pltpu.CompilerParams(vmem_limit_bytes=57 * MIB),
         cost_estimate=pl.CostEstimate(
             flops=100 * count * 32 * 256, bytes_accessed=11 * MIB, transcendentals=0
         ),

time: 139 us -> 141 us (1.014)
  local copies, waits for them, and re-layouts: 7.92 us -> 11 us
    unnamed x38 -> x42, local copies, waits for them, and re-layouts: 7.61 us -> 10.7 us
  transfers between devices with their start and end apart: 6 -> 6, of which waited for: 3 -> 3; matrix products, arithmetic and copies ran while one was open for 1% -> 1% of each run, Pallas kernels for 50% -> 49%
where the time goes in v6:
time: 141 us
  Pallas kernels  81.5 us (58%)
  waiting for transfers between devices  24.1 us (17%)
  starting transfers between devices  21.9 us (16%)
  local copies, waits for them, and re-layouts  11 us (8%)
    pallas_call x1, Pallas kernels, open_patches(): pl.pallas_call(open_kernel, grid=(count // PER,), out_shape=[jax.ShapeDty...  24.1 us
    pallas_call x1, Pallas kernels, close_patches(): pl.pallas_call(close_kernel, grid=(count // PER,), out_shape=jax.ShapeDty...  21.8 us
    all_to_all x2, waiting for transfers between devices, exchange(): lax.all_to_all(buffer.reshape(groups, rows, 128), 'yz', split_axis=0, con...  21.5 us
    all_to_all x2, starting transfers between devices, exchange(): lax.all_to_all(buffer.reshape(groups, rows, 128), 'yz', split_axis=0, con...  12.7 us
    pallas_call x1, Pallas kernels, face_fluxes(): pl.pallas_call(face_kernel, out_shape=jax.ShapeDtypeStruct(buffer.shape,...  10.7 us
    unnamed x42, local copies, waits for them, and re-layouts  10.7 us
    pallas_call x1, Pallas kernels, coarse_step(): pl.pallas_call(coarse_kernel, out_shape=jax.ShapeDtypeStruct((5, cells, 1...  10.5 us
    pallas_call x1, Pallas kernels, merge(): pl.pallas_call(merge_kernel, out_shape=jax.ShapeDtypeStruct(base.shape, F...  6.45 us
  transfers between devices with their start and end apart: 6, of which 3 were waited for; matrix products, arithmetic and copies ran while one was open for 1% of the time, Pallas kernels for 49%

profile of v6, /device:TPU:0, one launch (start us, length us, event | category | flops | bytes accessed | tf_op | source)
XLA Modules:
  0.0 140.7 jit_solution(14568145106413785128)
XLA Ops:
  0.6 0.6 pad_add_fusion.1.place_ref
  1.3 6.1 %pack_rims.1 = (f32[64,5,16,128]{3,2,1,0:T(8,128)}, f32[5,32,128]{2,1,0:T(8,128)}, f32[5,32,128]{2,1,0:T(8,128)}, f32[5,32,128]{2,1,0:T(8,128)}, f32[5,32,128]{2...) custom-call(s32[2]{0:T(128)} %pad_add_fusion.1.place_ref, s32[32,128]{1,0:T(8,128)} %bitcast.54, s32[32,128]{1,0:T(8,128)} %bitcast.55, ...), custom_call_target="tpu_custom_call" | custom-call | bytes 6291456 | tf_op jit(solution)/shard_map/pack_rims/pallas_call | solution.py:175
  7.3 0.0 copy-start.19
  7.3 0.0 copy-start.18
  7.3 0.0 copy-start.13
  7.3 0.0 copy-start.14
  7.4 0.0 copy-start.15
  7.4 0.0 copy-start.12
  7.4 7.5 %all-to-all-start = ((f32[32,160,128]{2,1,0:T(8,128)}), f32[32,160,128]{2,1,0:T(8,128)S(1)}, u32[]{:S(2)}, u32[]{:S(2)}) async-start(f32[32,160,128]{2,1,0:T(8,128)} %bitcast.49), calls=%async_computation | async-start | bytes 5242880 | tf_op jit(solution)/shard_map/all_to_all | solution.py:745
  14.9 0.0 copy-done.19
  14.9 0.3 collective-permute-start.2
  15.3 0.0 copy-done.18
  15.3 4.8 %collective-permute-start.3 = (f32[5,32,128]{2,1,0:T(8,128)S(1)}, f32[5,32,128]{2,1,0:T(8,128)S(1)}, u32[]{:S(2)}, u32[]{:S(2)}) collective-permute-start(f32[5,32,128]{2,1,0:T(8,128)S(1)} %copy-done.18), channel_id=1, source_target_pairs={{1,0},{2,1},{3,2},{4,3},{5,4},{6,5},{7,6},{8,7},{9,8},{10,9},{11,1... | collective-permute-start | bytes 245768 | tf_op jit(solution)/shard_map/ppermute | solution.py:787
  20.1 0.0 copy-done.13
  20.1 0.1 copy.18
  20.2 0.0 copy-done.14
  20.2 0.0 copy-done.15
  20.2 0.6 copy.21
  20.8 0.0 copy-done.12
  20.8 0.1 reshape.63
  20.9 0.1 copy.17
  21.0 0.1 reshape.64
  21.1 0.6 pad_add_fusion.bins_ref
  21.7 1.9 %rate_lookup.1.rate_ref = f32[4,48,128]{2,1,0:T(8,128)} custom-call(s32[48,128]{1,0:T(8,128)} %pad_add_fusion.bins_ref, f32[2,16,128]{2,1,0:T(8,128)} %bitcast.52), custom_call_target="tpu_custom_call" | custom-call | flops 1048576 | bytes 1048576 | tf_op jit(solution)/shard_map/rate_lookup/pallas_call | solution.py:217
  23.6 24.1 %open_patches.1 = (f32[64,5,32,128]{3,2,1,0:T(8,128)}, f32[32,5,4,8,256]{4,3,2,1,0:T(8,128)}) custom-call(s32[32,128]{1,0:T(8,128)} %get-tuple-element.18.slot_ref, f32[32,64,256]{2,1,0:T(8,128)} %bitcast.37, f32[3,32,64,256]{3,2,1,0:T(8,128)} %bitcast.29, f32[3,32,64,256]{3,2,1,0:T(8,128)} %bitcast.30, f32[3,32,64,256]{3,2,1,0:T(8,128)} %bitcast.31, ...), custom_call_target="tpu_custom_call" | custom-call | flops 131072000 | bytes 18874368 | tf_op jit(solution)/shard_map/open_patches/pallas_call | solution.py:491
  47.8 3.3 %all-to-all-done = f32[32,160,128]{2,1,0:T(8,128)S(1)} async-done(((f32[32,160,128]{2,1,0:T(8,128)}), f32[32,160,128]{2,1,0:T(8,128)S(1)}, u32[]{:S(2)}, u32[]{:S(2)}) %all-to-all-start) | async-done | bytes 2621472 | tf_op jit(solution)/shard_map/all_to_all | solution.py:745
  51.1 1.5 %copy-done.1 = f32[32,160,128]{2,1,0:T(8,128)} copy-done((f32[32,160,128]{2,1,0:T(8,128)}, f32[32,160,128]{2,1,0:T(8,128)S(1)}, u32[]{:S(2)}) %copy-start.1) | copy-done | bytes 2621464
  52.6 10.7 %face_fluxes.1 = f32[64,5,32,128]{3,2,1,0:T(8,128)} custom-call(s32[32,128]{1,0:T(8,128)} %get-tuple-element.18.slot_ref, f32[64,5,16,128]{3,2,1,0:T(8,128)} %bitcast.35, f32[32,5,4,8,256]{4,3,2,1,0:T(8,128)} %get-tuple-element.20.edge_ref, f32[64,5,32,128]{3,2,1,0:T(8,128)} %get-tuple-element.25._), custom_call_target="tpu_custom_call", output_to_operand_aliasing={{}: (3, {})} | custom-call | flops 26214400 | bytes 11534336 | tf_op jit(solution)/shard_map/face_fluxes/pallas_call | solution.py:583
  63.3 0.0 collective-permute-done.2.ylo_ref
  63.3 0.0 collective-permute-done.3.yhi_ref
  63.3 0.0 copy-start.2
  63.3 0.0 copy-start.9
  63.4 0.0 copy-start.10
  63.4 5.2 %all-to-all-start.1 = ((f32[32,320,128]{2,1,0:T(8,128)}), f32[32,320,128]{2,1,0:T(8,128)}, u32[]{:S(2)}, u32[]{:S(2)}) async-start(f32[32,320,128]{2,1,0:T(8,128)} %bitcast.47), calls=%async_computation.1 | async-start | bytes 10485760 | tf_op jit(solution)/shard_map/all_to_all | solution.py:745
  68.6 0.0 copy-start
  68.6 2.8 %copy-done = f32[3,32,8,8,256]{4,3,2,1,0:T(8,128)S(1)} copy-done((f32[3,32,8,8,256]{4,3,2,1,0:T(8,128)S(1)}, f32[3,32,8,8,256]{4,3,2,1,0:T(8,128)}, u32[]{:S(2)}) %copy-start) | copy-done | bytes 6291480
  71.3 2.5 %copy-done.3 = f32[32,5,4,8,256]{4,3,2,1,0:T(8,128)S(1)} copy-done((f32[32,5,4,8,256]{4,3,2,1,0:T(8,128)S(1)}, f32[32,5,4,8,256]{4,3,2,1,0:T(8,128)}, u32[]{:S(2)}) %copy-start.3) | copy-done | bytes 5242904
  73.8 1.6 %copy-done.4 = f32[32,8,8,256]{3,2,1,0:T(8,128)S(1)} copy-done((f32[32,8,8,256]{3,2,1,0:T(8,128)S(1)}, f32[32,8,8,256]{3,2,1,0:T(8,128)}, u32[]{:S(2)}) %copy-start.4) | copy-done | bytes 2097176
  75.4 1.6 %copy-done.5 = f32[32,8,8,256]{3,2,1,0:T(8,128)S(1)} copy-done((f32[32,8,8,256]{3,2,1,0:T(8,128)S(1)}, f32[32,8,8,256]{3,2,1,0:T(8,128)}, u32[]{:S(2)}) %copy-start.5) | copy-done | bytes 2097176
  77.0 0.0 copy-start.8
  77.0 21.8 %close_patches.1 = f32[5,32,64,256]{3,2,1,0:T(8,128)} custom-call(s32[32,128]{1,0:T(8,128)S(1)} %copy-done.10, f32[32,64,256]{2,1,0:T(8,128)S(1)} %bitcast.38, f32[3,32,64,256]{3,2,1,0:T(8,128)S(1)} %bitcast.32, f32[3,32,64,256]{3,2,1,0:T(8,128)S(1)} %bitcast.33, f32[3,32,64,256]{3,2,1,0:T(8,128)S(1)} %bitcast.34, f32[32,64,256]{2,1,0:T(8,128)S(1)} %bitcast.40, ...), custom_call_target="tpu_custom_call" | custom-call | flops 131072000 | bytes 30408704 | tf_op jit(solution)/shard_map/close_patches/pallas_call | solution.py:642
  98.8 1.9 %collective-permute-start = (f32[5,32,128]{2,1,0:T(8,128)S(1)}, f32[5,32,128]{2,1,0:T(8,128)S(1)}, u32[]{:S(2)}, u32[]{:S(2)}) collective-permute-start(f32[5,32,128]{2,1,0:T(8,128)S(1)} %copy-done.17), channel_id=1, source_target_pairs={{0,32},{32,64},{64,96},{96,0},{1,33},{33,65},{65,97},{97,1},{2,34}... | collective-permute-start | bytes 245768 | tf_op jit(solution)/shard_map/ppermute | solution.py:803
  100.7 2.2 %collective-permute-start.1 = (f32[5,32,128]{2,1,0:T(8,128)S(1)}, f32[5,32,128]{2,1,0:T(8,128)S(1)}, u32[]{:S(2)}, u32[]{:S(2)}) collective-permute-start(f32[5,32,128]{2,1,0:T(8,128)S(1)} %copy-done.16), channel_id=1, source_target_pairs={{32,0},{64,32},{96,64},{0,96},{33,1},{65,33},{97,65},{1,97},{34,2}... | collective-permute-start | bytes 245768 | tf_op jit(solution)/shard_map/ppermute | solution.py:804
  102.9 2.6 %collective-permute-done.xlo_ref = f32[5,32,128]{2,1,0:T(8,128)S(1)} collective-permute-done((f32[5,32,128]{2,1,0:T(8,128)S(1)}, f32[5,32,128]{2,1,0:T(8,128)S(1)}, u32[]{:S(2)}, u32[]{:S(2)}) %collective-permute-start) | collective-permute-done | bytes 81952 | tf_op jit(solution)/shard_map/ppermute | solution.py:803
  105.5 0.0 collective-permute-done.1.xhi_ref
  105.6 10.5 %coarse_step.1.base_ref = f32[5,1024,128]{2,1,0:T(8,128)S(1)} custom-call(s32[8,128]{1,0:T(8,128)S(1)} %copy-done.11, f32[1024,128]{1,0:T(8,128)S(1)} %bitcast.44, f32[3,1024,128]{2,1,0:T(8,128)S(1)} %bitcast.42, f32[1024,128]{1,0:T(8,128)S(1)} %bitcast.46, f32[5,32,128]{2,1,0:T(8,128)S(1)} %collective-permute-done.xlo_ref, ...), custom_call_target="tpu_custom_call" | custom-call | flops 39321600 | bytes 31457280 | tf_op jit(solution)/shard_map/coarse_step/pallas_call | solution.py:338
  116.1 18.2 %all-to-all-done.1 = f32[32,320,128]{2,1,0:T(8,128)} async-done(((f32[32,320,128]{2,1,0:T(8,128)}), f32[32,320,128]{2,1,0:T(8,128)}, u32[]{:S(2)}, u32[]{:S(2)}) %all-to-all-start.1) | async-done | bytes 5242912 | tf_op jit(solution)/shard_map/all_to_all | solution.py:745
  134.3 6.4 %merge_patches.1 = f32[5,1024,128]{2,1,0:T(8,128)} custom-call(s32[8,128]{1,0:T(8,128)S(1)} %copy-done.11, f32[5,1024,128]{2,1,0:T(8,128)S(1)} %coarse_step.1.base_ref, f32[64,5,32,128]{3,2,1,0:T(8,128)} %bitcast.17.got_hbm), custom_call_target="tpu_custom_call" | custom-call | flops 1048576 | bytes 11534336 | tf_op jit(solution)/shard_map/merge_patches/pallas_call | solution.py:730
  (19 shorter events, 0.1 us)
Async XLA Ops:
  7.3 7.6 %copy-start.19 = (f32[5,32,128]{2,1,0:T(8,128)S(1)}, f32[5,32,128]{2,1,0:T(8,128)}, u32[]{:S(2)}) copy-start(f32[5,32,128]{2,1,0:T(8,128)} %get-tuple-element.26) | copy-start | bytes 245764
  7.3 8.0 %copy-start.18 = (f32[5,32,128]{2,1,0:T(8,128)S(1)}, f32[5,32,128]{2,1,0:T(8,128)}, u32[]{:S(2)}) copy-start(f32[5,32,128]{2,1,0:T(8,128)} %get-tuple-element.27) | copy-start | bytes 245764
  7.3 12.8 %copy-start.13 = (s32[32,32]{1,0:T(8,128)S(1)}, s32[32,32]{1,0:T(8,128)}, u32[]{:S(2)}) copy-start(s32[32,32]{1,0:T(8,128)} %param.15) | copy-start | bytes 12292
  7.3 12.8 %copy-start.14 = (f32[2000]{0:T(1024)S(1)}, f32[2000]{0:T(1024)}, u32[]{:S(2)}) copy-start(f32[2000]{0:T(1024)} %param.23) | copy-start | bytes 24004
  7.4 12.8 %copy-start.15 = (f32[2000]{0:T(1024)S(1)}, f32[2000]{0:T(1024)}, u32[]{:S(2)}) copy-start(f32[2000]{0:T(1024)} %param.22) | copy-start | bytes 24004
  7.4 13.4 %copy-start.12 = (s32[32,8,8]{0,2,1:T(8,128)S(1)}, s32[32,8,8]{0,2,1:T(8,128)}, u32[]{:S(2)}) copy-start(s32[32,8,8]{0,2,1:T(8,128)} %param.19) | copy-start | bytes 24580
  7.4 43.7 %all-to-all-start = ((f32[32,160,128]{2,1,0:T(8,128)}), f32[32,160,128]{2,1,0:T(8,128)S(1)}, u32[]{:S(2)}, u32[]{:S(2)}) async-start(f32[32,160,128]{2,1,0:T(8,128)} %bitcast.49), calls=%async_computation | async-start | bytes 5242880 | tf_op jit(solution)/shard_map/all_to_all | solution.py:745
  14.9 48.4 %collective-permute-start.2 = (f32[5,32,128]{2,1,0:T(8,128)S(1)}, f32[5,32,128]{2,1,0:T(8,128)S(1)}, u32[]{:S(2)}, u32[]{:S(2)}) collective-permute-start(f32[5,32,128]{2,1,0:T(8,128)S(1)} %copy-done.19), channel_id=1, source_target_pairs={{0,1},{1,2},{2,3},{3,4},{4,5},{5,6},{6,7},{7,8},{8,9},{9,10},{10,1... | collective-permute-start | bytes 245768 | tf_op jit(solution)/shard_map/ppermute | solution.py:786
  15.3 48.0 %collective-permute-start.3 = (f32[5,32,128]{2,1,0:T(8,128)S(1)}, f32[5,32,128]{2,1,0:T(8,128)S(1)}, u32[]{:S(2)}, u32[]{:S(2)}) collective-permute-start(f32[5,32,128]{2,1,0:T(8,128)S(1)} %copy-done.18), channel_id=1, source_target_pairs={{1,0},{2,1},{3,2},{4,3},{5,4},{6,5},{7,6},{8,7},{9,8},{10,9},{11,1... | collective-permute-start | bytes 245768 | tf_op jit(solution)/shard_map/ppermute | solution.py:787
  51.1 1.5 %copy-start.1 = (f32[32,160,128]{2,1,0:T(8,128)}, f32[32,160,128]{2,1,0:T(8,128)S(1)}, u32[]{:S(2)}) copy-start(f32[32,160,128]{2,1,0:T(8,128)S(1)} %all-to-all-done) | copy-start | bytes 7864324
  63.3 5.2 %copy-start.2 = (f32[32,160,128]{2,1,0:T(8,128)S(1)}, f32[32,160,128]{2,1,0:T(8,128)}, u32[]{:S(2)}) copy-start(f32[32,160,128]{2,1,0:T(8,128)} %copy-done.1) | copy-start | bytes 7864324
  63.3 5.2 %copy-start.9 = (f32[4,48,128]{2,1,0:T(8,128)S(1)}, f32[4,48,128]{2,1,0:T(8,128)}, u32[]{:S(2)}) copy-start(f32[4,48,128]{2,1,0:T(8,128)} %rate_lookup.1.rate_ref) | copy-start | bytes 294916
  63.4 5.2 %copy-start.10 = (s32[32,128]{1,0:T(8,128)S(1)}, s32[32,128]{1,0:T(8,128)}, u32[]{:S(2)}) copy-start(s32[32,128]{1,0:T(8,128)} %get-tuple-element.18.slot_ref) | copy-start | bytes 49156
  63.4 70.9 %all-to-all-start.1 = ((f32[32,320,128]{2,1,0:T(8,128)}), f32[32,320,128]{2,1,0:T(8,128)}, u32[]{:S(2)}, u32[]{:S(2)}) async-start(f32[32,320,128]{2,1,0:T(8,128)} %bitcast.47), calls=%async_computation.1 | async-start | bytes 10485760 | tf_op jit(solution)/shard_map/all_to_all | solution.py:745
  68.6 2.8 %copy-start = (f32[3,32,8,8,256]{4,3,2,1,0:T(8,128)S(1)}, f32[3,32,8,8,256]{4,3,2,1,0:T(8,128)}, u32[]{:S(2)}) copy-start(f32[3,32,8,8,256]{4,3,2,1,0:T(8,128)} %param.17) | copy-start | bytes 18874372
  71.3 2.5 %copy-start.3 = (f32[32,5,4,8,256]{4,3,2,1,0:T(8,128)S(1)}, f32[32,5,4,8,256]{4,3,2,1,0:T(8,128)}, u32[]{:S(2)}) copy-start(f32[32,5,4,8,256]{4,3,2,1,0:T(8,128)} %get-tuple-element.20.edge_ref) | copy-start | bytes 15728644
  73.8 1.6 %copy-start.4 = (f32[32,8,8,256]{3,2,1,0:T(8,128)S(1)}, f32[32,8,8,256]{3,2,1,0:T(8,128)}, u32[]{:S(2)}) copy-start(f32[32,8,8,256]{3,2,1,0:T(8,128)} %param.16) | copy-start | bytes 6291460
  75.4 1.6 %copy-start.5 = (f32[32,8,8,256]{3,2,1,0:T(8,128)S(1)}, f32[32,8,8,256]{3,2,1,0:T(8,128)}, u32[]{:S(2)}) copy-start(f32[32,8,8,256]{3,2,1,0:T(8,128)} %param.18) | copy-start | bytes 6291460
  77.0 21.8 %copy-start.17 = (f32[5,32,128]{2,1,0:T(8,128)S(1)}, f32[5,32,128]{2,1,0:T(8,128)}, u32[]{:S(2)}) copy-start(f32[5,32,128]{2,1,0:T(8,128)} %get-tuple-element.23) | copy-start | bytes 245764
  77.0 23.7 %copy-start.16 = (f32[5,32,128]{2,1,0:T(8,128)S(1)}, f32[5,32,128]{2,1,0:T(8,128)}, u32[]{:S(2)}) copy-start(f32[5,32,128]{2,1,0:T(8,128)} %get-tuple-element.24) | copy-start | bytes 245764
  77.0 28.5 %copy-start.6 = (f32[3,32,32,128]{3,2,1,0:T(8,128)S(1)}, f32[3,32,32,128]{3,2,1,0:T(8,128)}, u32[]{:S(2)}) copy-start(f32[3,32,32,128]{3,2,1,0:T(8,128)} %param.13) | copy-start | bytes 4718596
  77.0 28.5 %copy-start.7 = (f32[32,32,128]{2,1,0:T(8,128)S(1)}, f32[32,32,128]{2,1,0:T(8,128)}, u32[]{:S(2)}) copy-start(f32[32,32,128]{2,1,0:T(8,128)} %param.12) | copy-start | bytes 1572868
  77.0 28.5 %copy-start.8 = (f32[32,32,128]{2,1,0:T(8,128)S(1)}, f32[32,32,128]{2,1,0:T(8,128)}, u32[]{:S(2)}) copy-start(f32[32,32,128]{2,1,0:T(8,128)} %param.14) | copy-start | bytes 1572868
  77.0 28.5 %copy-start.11 = (s32[8,128]{1,0:T(8,128)S(1)}, s32[8,128]{1,0:T(8,128)}, u32[]{:S(2)}) copy-start(s32[8,128]{1,0:T(8,128)} %get-tuple-element.17.corner_ref) | copy-start | bytes 12292
  98.8 6.7 %collective-permute-start = (f32[5,32,128]{2,1,0:T(8,128)S(1)}, f32[5,32,128]{2,1,0:T(8,128)S(1)}, u32[]{:S(2)}, u32[]{:S(2)}) collective-permute-start(f32[5,32,128]{2,1,0:T(8,128)S(1)} %copy-done.17), channel_id=1, source_target_pairs={{0,32},{32,64},{64,96},{96,0},{1,33},{33,65},{65,97},{97,1},{2,34}... | collective-permute-start | bytes 245768 | tf_op jit(solution)/shard_map/ppermute | solution.py:803
  100.7 4.8 %collective-permute-start.1 = (f32[5,32,128]{2,1,0:T(8,128)S(1)}, f32[5,32,128]{2,1,0:T(8,128)S(1)}, u32[]{:S(2)}, u32[]{:S(2)}) collective-permute-start(f32[5,32,128]{2,1,0:T(8,128)S(1)} %copy-done.16), channel_id=1, source_target_pairs={{32,0},{64,32},{96,64},{0,96},{33,1},{65,33},{97,65},{1,97},{34,2}... | collective-permute-start | bytes 245768 | tf_op jit(solution)/shard_map/ppermute | solution.py:804
